TPU v7x, 256 devices: a whole 4x4x8 slice. The times are simulated.
256 devices in a mesh: band: 16 (over x_lo, z), slab: 16 (over y, x_hi, core).
Axes of the slice: x: 4 (x_hi: 2, x_lo: 2; x = x_hi * 2 + x_lo), y: 4, z: 8, core: 2. Of those that a mesh axis runs over, the one named last changes fastest.
Arguments:
- orbitals: float32 [1024, 128, 512], P('band', 'slab'), may hold values from -48 to 48
- potential: float32 [128, 512], P('slab'), may hold values from -2 to 2
Outputs:
- filtered: float32 [1024, 128, 512], P('band', 'slab')
- gram_matrix: float32 [1024, 1024], P('band', 'slab')
- projected: float32 [1024, 1024], P('band', 'slab')
All inputs are finite; a program needn't handle non-finite values.
Results may differ from a plain program's by a relative error of at most 0.00048.
Values may be sent and summed in bfloat16 or wider, within the bound.
No kernel may reach another device: no remote copies, remote signals or barrier semaphores. Data moves between devices by JAX's collectives and lax.ppermute only.
A program may use at most 64 MiB of HBM per device.

v0:
```python
import jax
import jax.numpy as jnp
from jax import lax
from jax.sharding import PartitionSpec as P

DEGREE = 4
NY = 16


COEFFS = (
    -5369.0 / 1800.0,
    12.0 / 7.0,
    -15.0 / 56.0,
    10.0 / 189.0,
    -1.0 / 112.0,
    2.0 / 1925.0,
    -1.0 / 16632.0,
)
SPACING = 0.6
LOWER = -2.0
CUTOFF = 8.0
UPPER = 32.0


def with_halo(block, sides, width):
    for axis, dim in sides:
        count = lax.axis_size(axis)
        forward = [(i, i + 1) for i in range(count - 1)]
        backward = [(target, source) for source, target in forward]
        low = lax.ppermute(
            lax.slice_in_dim(block, block.shape[dim] - width, None, axis=dim), axis, forward
        )
        high = lax.ppermute(lax.slice_in_dim(block, 0, width, axis=dim), axis, backward)
        block = jnp.concatenate([low, block, high], axis=dim)
    return block


def plane_terms(field):
    width = field.shape[-1]
    wide = jnp.pad(field, ((0, 0), (0, 0), (6 * NY, 6 * NY)))
    narrow = jnp.pad(field, ((0, 0), (0, 0), (6, 6)))
    column = jnp.arange(width) % NY
    total = jnp.zeros_like(field)
    for reach in range(1, 7):
        upper_mask = (column + reach < NY).astype(field.dtype)
        lower_mask = (column - reach >= 0).astype(field.dtype)
        along_x = (
            wide[:, :, (6 + reach) * NY : (6 + reach) * NY + width]
            + wide[:, :, (6 - reach) * NY : (6 - reach) * NY + width]
        )
        along_y = (
            upper_mask * narrow[:, :, 6 + reach : 6 + reach + width]
            + lower_mask * narrow[:, :, 6 - reach : 6 - reach + width]
        )
        total = total + COEFFS[reach] * (along_x + along_y)
    return total


def apply_field(padded, field, potential):
    depth = field.shape[1]
    total = 3.0 * COEFFS[0] * field + plane_terms(field)
    for reach in range(1, 7):
        total = total + COEFFS[reach] * (
            padded[:, 6 + reach : 6 + reach + depth] + padded[:, 6 - reach : 6 - reach + depth]
        )
    return -0.5 / SPACING**2 * total + potential[None] * field


def chebyshev(start, operate):
    half_width = (UPPER - CUTOFF) / 2.0
    center = (UPPER + CUTOFF) / 2.0
    sigma_first = half_width / (LOWER - center)
    sigma = sigma_first
    previous = start
    current = (operate(start) - center * start) * (sigma_first / half_width)
    for step in range(DEGREE - 1):
        sigma_next = 1.0 / (2.0 / sigma_first - sigma)
        following = (operate(current) - center * current) * (
            2.0 * sigma_next / half_width
        ) - sigma * sigma_next * previous
        previous = current
        current = following
        sigma = sigma_next
    return current


def operate_slab(field, potential):
    padded = with_halo(field, (("slab", 1),), 6)
    return apply_field(padded, field, potential)


def pair_blocks(own_low, own_applied, other_low, other_applied):
    gram_block = jnp.einsum("azp,bzp->ab", own_low, other_low, preferred_element_type=jnp.float32)
    first = jnp.einsum("azp,bzp->ab", own_applied, other_low, preferred_element_type=jnp.float32)
    second = jnp.einsum("azp,bzp->ab", own_low, other_applied, preferred_element_type=jnp.float32)
    return (gram_block, 0.5 * (first + second))


def on_device(orbitals, potential):

    def operate(field):
        return operate_slab(field, potential)

    filtered = chebyshev(orbitals, operate)
    applied = operate(filtered)
    filtered_low = filtered.astype(jnp.bfloat16)
    applied_low = applied.astype(jnp.bfloat16)
    gram_block, cross_block = pair_blocks(
        filtered_low,
        applied_low,
        lax.all_gather(filtered_low, "band", axis=0, tiled=True),
        lax.all_gather(applied_low, "band", axis=0, tiled=True),
    )
    sums = (
        lax.psum_scatter(gram_block, "slab", scatter_dimension=1, tiled=True),
        lax.psum_scatter(cross_block, "slab", scatter_dimension=1, tiled=True),
    )
    cells = orbitals.shape[1] * orbitals.shape[2] * lax.axis_size("slab")
    return (filtered, sums[0] / cells, sums[1] / cells)


def solution(mesh):
    return jax.shard_map(
        on_device,
        mesh=mesh,
        in_specs=(P("band", "slab", None), P("slab", None)),
        out_specs=(P("band", "slab", None), P("band", "slab"), P("band", "slab")),
        check_vma=False,
    )
```

profile of v0, /device:TPU:1, one launch (start us, length us, event | category | flops | bytes accessed | tf_op | source)
XLA Modules:
  0.0 520.3 jit_solution(10271647791222146557)
XLA Ops:
  7.2 1.8 copy.16
  9.2 6.2 %collective-permute-start.1 = (f32[64,6,512]{2,0,1:T(8,128)S(1)}, f32[64,6,512]{2,0,1:T(8,128)S(1)}, u32[]{:S(2)}, u32[]{:S(2)}) collective-permute-start(f32[64,6,512]{2,0,1:T(8,128)S(1)} %get-tuple-element.22), channel_id=1, source_target_pairs={{0,1},{1,2},{2,3},{3,4},{4,5},{5,6},{6,7},{7,8},{8,9},{9,10},{10,1... | collective-permute-start | bytes 2359304 | tf_op jit(solution)/shard_map/ppermute | solution.py:30
  15.4 1.9 collective-permute-start
  17.4 6.9 %collective-permute-done.1 = f32[64,6,512]{2,0,1:T(8,128)S(1)} collective-permute-done((f32[64,6,512]{2,0,1:T(8,128)S(1)}, f32[64,6,512]{2,0,1:T(8,128)S(1)}, u32[]{:S(2)}, u32[]{:S(2)}) %collective-permute-start.1) | collective-permute-done | bytes 786464 | tf_op jit(solution)/shard_map/ppermute | solution.py:30
  24.4 0.6 constant_dynamic-update-slice_fusion.1
  25.0 9.4 %collective-permute-done = f32[64,6,512]{2,0,1:T(8,128)S(1)} collective-permute-done((f32[64,6,512]{2,0,1:T(8,128)S(1)}, f32[64,6,512]{2,0,1:T(8,128)S(1)}, u32[]{:S(2)}, u32[]{:S(2)}) %collective-permute-start) | collective-permute-done | bytes 786464 | tf_op jit(solution)/shard_map/ppermute | solution.py:33
  34.5 8.2 %broadcast_multiply_fusion = (f32[64,8,512]{2,0,1:T(8,128)S(1)}, f32[64,8,512]{2,0,1:T(8,128)}) fusion(f32[64,8,512]{2,0,1:T(8,128)S(1)} %copy.16, f32[8,512]{1,0:T(8,128)S(1)} %copy-done.9, f32[64,14,512]{2,0,1:T(8,128)S(1)} %get-tuple-element.24, f32[64,14,512]{2,0,1:T(8,128)S(1)} %constant_dynamic-update-slice_fusion, f32[512]{0:T(512)S(1)} %get-tuple-element.36, ...), kind=kLoop, calls=%fused_computation.558 | loop fusion | flops 17563648 | bytes 15769600 | tf_op jit(solution)/shard_map/mul | solution.py:75
  42.7 0.2 fusion.355
  42.9 1.9 collective-permute-start.2
  44.8 5.1 collective-permute-start.3
  50.0 10.8 %collective-permute-done.2 = f32[64,6,512]{2,0,1:T(8,128)S(1)} collective-permute-done((f32[64,6,512]{2,0,1:T(8,128)S(1)}, f32[64,6,512]{2,0,1:T(8,128)S(1)}, u32[]{:S(2)}, u32[]{:S(2)}) %collective-permute-start.2) | collective-permute-done | bytes 786464 | tf_op jit(solution)/shard_map/ppermute | solution.py:33
  60.8 0.9 copy-done.7
  61.7 0.9 copy-done.8
  62.6 9.2 %multiply_subtract_fusion.2 = f32[64,8,512]{2,0,1:T(8,128)S(1)} fusion(f32[64,8,512]{2,0,1:T(8,128)} %get-tuple-element.12, f32[64,8,512]{2,0,1:T(8,128)S(1)} %get-tuple-element.11, f32[64,6,512]{2,0,1:T(8,128)} %copy-done.8, f32[64,6,512]{2,0,1:T(8,128)} %copy-done.7, f32[8,512]{1,0:T(8,128)S(1)} %broadcast_multiply_fusion.3, ...), kind=kLoop, calls=%fused_computation.556 | loop fusion | flops 21233664 | bytes 5808128 | tf_op jit(solution)/shard_map/sub | solution.py:78
  71.8 0.2 fusion.354
  72.0 2.1 collective-permute-start.4
  74.1 5.3 %collective-permute-start.5 = (f32[64,6,512]{2,0,1:T(8,128)S(1)}, f32[64,6,512]{2,0,1:T(8,128)}, u32[]{:S(2)}, u32[]{:S(2)}) collective-permute-start(f32[64,6,512]{2,0,1:T(8,128)S(1)} %get-tuple-element.18), channel_id=1, source_target_pairs={{0,1},{1,2},{2,3},{3,4},{4,5},{5,6},{6,7},{7,8},{8,9},{9,10},{10,1... | collective-permute-start | bytes 2359304 | tf_op jit(solution)/shard_map/ppermute | solution.py:30
  79.4 7.5 %collective-permute-done.4 = f32[64,6,512]{2,0,1:T(8,128)S(1)} collective-permute-done((f32[64,6,512]{2,0,1:T(8,128)S(1)}, f32[64,6,512]{2,0,1:T(8,128)S(1)}, u32[]{:S(2)}, u32[]{:S(2)}) %collective-permute-start.4) | collective-permute-done | bytes 786464 | tf_op jit(solution)/shard_map/ppermute | solution.py:33
  86.9 0.9 copy-done.6
  87.8 0.3 collective-permute-done.5
  88.1 8.9 %multiply_subtract_fusion.1 = f32[64,8,512]{2,0,1:T(8,128)S(1)} fusion(f32[64,8,512]{2,0,1:T(8,128)S(1)} %copy-done.3, f32[64,8,512]{2,0,1:T(8,128)S(1)} %multiply_subtract_fusion.2, f32[64,6,512]{2,0,1:T(8,128)} %collective-permute-done.5, f32[64,6,512]{2,0,1:T(8,128)} %copy-done.6, f32[8,512]{1,0:T(8,128)S(1)} %copy-done.9, f32[512]{0:T(512)S(1)} %get-tuple-element.36, ...), kind=kLoop, calls=%fused_computation.555 | loop fusion | flops 21233664 | bytes 4759552 | tf_op jit(solution)/shard_map/sub | solution.py:78
  97.0 0.2 fusion.353
  97.2 1.9 collective-permute-start.6
  99.2 6.0 %collective-permute-start.7 = (f32[64,6,512]{2,0,1:T(8,128)S(1)}, f32[64,6,512]{2,0,1:T(8,128)}, u32[]{:S(2)}, u32[]{:S(2)}) collective-permute-start(f32[64,6,512]{2,0,1:T(8,128)S(1)} %get-tuple-element.16), channel_id=1, source_target_pairs={{0,1},{1,2},{2,3},{3,4},{4,5},{5,6},{6,7},{7,8},{8,9},{9,10},{10,1... | collective-permute-start | bytes 2359304 | tf_op jit(solution)/shard_map/ppermute | solution.py:30
  105.2 7.7 %collective-permute-done.6 = f32[64,6,512]{2,0,1:T(8,128)S(1)} collective-permute-done((f32[64,6,512]{2,0,1:T(8,128)S(1)}, f32[64,6,512]{2,0,1:T(8,128)S(1)}, u32[]{:S(2)}, u32[]{:S(2)}) %collective-permute-start.6) | collective-permute-done | bytes 786464 | tf_op jit(solution)/shard_map/ppermute | solution.py:33
  112.9 0.9 copy-done.5
  113.8 0.3 collective-permute-done.7
  114.1 9.6 %fusion.351 = (bf16[64,8,512]{2,0,1:T(8,128)(2,1)}, f32[64,8,512]{2,0,1:T(8,128)S(1)}) fusion(f32[64,8,512]{2,0,1:T(8,128)S(1)} %multiply_subtract_fusion.2, f32[64,8,512]{2,0,1:T(8,128)S(1)} %multiply_subtract_fusion.1, f32[8,512]{1,0:T(8,128)S(1)} %copy-done.9, f32[64,6,512]{2,0,1:T(8,128)} %collective-permute-done.7, f32[64,6,512]{2,0,1:T(8,128)} %copy-done.5, ...), kind=kLoop, calls=%fused_computation.595 | loop fusion | flops 21495808 | bytes 5283840 | tf_op jit(solution)/shard_map/convert_element_type | solution.py:106
  123.8 0.2 fusion.352
  123.9 1.9 collective-permute-start.8
  125.9 6.1 %collective-permute-start.9 = (f32[64,6,512]{2,0,1:T(8,128)S(1)}, f32[64,6,512]{2,0,1:T(8,128)S(1)}, u32[]{:S(2)}, u32[]{:S(2)}) collective-permute-start(f32[64,6,512]{2,0,1:T(8,128)S(1)} %get-tuple-element.14), channel_id=1, source_target_pairs={{0,1},{1,2},{2,3},{3,4},{4,5},{5,6},{6,7},{7,8},{8,9},{9,10},{10,1... | collective-permute-start | bytes 2359304 | tf_op jit(solution)/shard_map/ppermute | solution.py:30
  132.0 7.6 %collective-permute-done.8 = f32[64,6,512]{2,0,1:T(8,128)S(1)} collective-permute-done((f32[64,6,512]{2,0,1:T(8,128)S(1)}, f32[64,6,512]{2,0,1:T(8,128)S(1)}, u32[]{:S(2)}, u32[]{:S(2)}) %collective-permute-start.8) | collective-permute-done | bytes 786464 | tf_op jit(solution)/shard_map/ppermute | solution.py:33
  139.6 1.3 collective-permute-done.9
  140.9 7.9 %add_convert_fusion = bf16[64,8,512]{2,0,1:T(8,128)(2,1)} fusion(f32[64,8,512]{2,0,1:T(8,128)S(1)} %get-tuple-element.10, f32[64,6,512]{2,0,1:T(8,128)S(1)} %collective-permute-done.9, f32[64,6,512]{2,0,1:T(8,128)S(1)} %collective-permute-done.8, f32[8,512]{1,0:T(8,128)S(1)} %copy-done.9, f32[512]{0:T(512)S(1)} %get-tuple-element.36, ...), kind=kLoop, calls=%fused_computation.553 | loop fusion | flops 20185088 | bytes 3186688 | tf_op jit(solution)/shard_map/convert_element_type | solution.py:107
  148.9 98.8 %all-gather.3.cloned.1.call-done = bf16[1024,8,512]{2,0,1:T(8,128)(2,1)} async-done(((bf16[64,8,512]{2,0,1:T(8,128)(2,1)}), bf16[1024,8,512]{2,0,1:T(8,128)(2,1)}) %all-gather.3.cloned.1.call-update) | async-done | bytes 8388624 | tf_op jit(solution)/shard_map/all_gather | solution.py:111
  247.7 6.5 %convolution_bitcast_fusion = f32[1024,64]{1,0:T(8,128)} fusion(bf16[64,8,512]{2,0,1:T(8,128)(2,1)S(1)} %copy-done.1, bf16[1024,8,512]{2,0,1:T(8,128)(2,1)} %all-gather.3.cloned.1.call-done), kind=kOutput, calls=%fused_computation.200 | convolution fusion | flops 536870912 | bytes 9175040 | tf_op jit(solution)/shard_map/azp,bzp->ab/dot_general | solution.py:93
  254.2 0.3 reduce-scatter.9.cloned.1.call-start
  254.5 108.3 %all-gather.5.cloned.1.call-done = bf16[1024,8,512]{2,0,1:T(8,128)(2,1)} async-done(((bf16[64,8,512]{2,0,1:T(8,128)(2,1)}), bf16[1024,8,512]{2,0,1:T(8,128)(2,1)}) %all-gather.5.cloned.1.call-update) | async-done | bytes 8388624 | tf_op jit(solution)/shard_map/all_gather | solution.py:112
  362.8 6.1 %convolution_bitcast_fusion.1 = f32[64,1024]{1,0:T(8,128)S(1)} fusion(bf16[64,8,512]{2,0,1:T(8,128)(2,1)S(1)} %copy-done.1, bf16[1024,8,512]{2,0,1:T(8,128)(2,1)} %all-gather.5.cloned.1.call-done), kind=kOutput, calls=%fused_computation.201 | convolution fusion | flops 536870912 | bytes 9175040 | tf_op jit(solution)/shard_map/azp,bzp->ab/dot_general | solution.py:95
  369.0 2.6 fusion.1
  371.6 1.0 copy.29
  372.7 1.6 copy.26
  374.2 61.5 %reduce-scatter.7.cloned.1.call-done = f32[64,64]{1,0:T(8,128)} async-done(((f32[1024,64]{1,0:T(8,128)}), f32[64,64]{1,0:T(8,128)}) %reduce-scatter.7.cloned.1.call-update) | async-done | bytes 16400
  435.8 0.8 copy.28
  436.6 0.6 broadcast_multiply_fusion.2
  437.2 75.1 %reduce-scatter.9.cloned.1.call-done = f32[64,64]{1,0:T(8,128)} async-done(((f32[1024,64]{1,0:T(8,128)}), f32[64,64]{1,0:T(8,128)}) %reduce-scatter.9.cloned.1.call-update) | async-done | bytes 16400
  512.3 0.8 copy.30
  513.2 0.6 broadcast_multiply_fusion.1
  (34 shorter events, 0.6 us)
Async XLA Ops:
  7.2 240.5 %all-gather.3.cloned.1.call-start = ((), (), s32[]{:S(2)}) async-start(), calls=%async_computation.2 | async-start | bytes 8912896 | tf_op jit(solution)/shard_map/all_gather | solution.py:111
  9.0 15.3 %copy-start.2 = (f32[64,8,512]{2,1,0:T(8,128)S(1)}, f32[64,8,512]{2,1,0:T(8,128)}, u32[]{:S(2)}) copy-start(f32[64,8,512]{2,1,0:T(8,128)} %param.2) | copy-start | bytes 3145732
  9.2 15.1 %collective-permute-start.1 = (f32[64,6,512]{2,0,1:T(8,128)S(1)}, f32[64,6,512]{2,0,1:T(8,128)S(1)}, u32[]{:S(2)}, u32[]{:S(2)}) collective-permute-start(f32[64,6,512]{2,0,1:T(8,128)S(1)} %get-tuple-element.22), channel_id=1, source_target_pairs={{0,1},{1,2},{2,3},{3,4},{4,5},{5,6},{6,7},{7,8},{8,9},{9,10},{10,1... | collective-permute-start | bytes 2359304 | tf_op jit(solution)/shard_map/ppermute | solution.py:30
  15.4 19.0 %collective-permute-start = (f32[64,6,512]{2,0,1:T(8,128)S(1)}, f32[64,6,512]{2,0,1:T(8,128)S(1)}, u32[]{:S(2)}, u32[]{:S(2)}) collective-permute-start(f32[64,6,512]{2,0,1:T(8,128)S(1)} %get-tuple-element.21), channel_id=1, source_target_pairs={{1,0},{2,1},{3,2},{4,3},{5,4},{6,5},{7,6},{8,7},{9,8},{10,9},{11,1... | collective-permute-start | bytes 2359304 | tf_op jit(solution)/shard_map/ppermute | solution.py:33
  24.4 10.1 %copy-start.9 = (f32[8,512]{1,0:T(8,128)S(1)}, f32[8,512]{1,0:T(8,128)}, u32[]{:S(2)}) copy-start(f32[8,512]{1,0:T(8,128)} %param.3) | copy-start | bytes 49156
  42.9 17.9 %collective-permute-start.2 = (f32[64,6,512]{2,0,1:T(8,128)S(1)}, f32[64,6,512]{2,0,1:T(8,128)S(1)}, u32[]{:S(2)}, u32[]{:S(2)}) collective-permute-start(f32[64,6,512]{2,0,1:T(8,128)S(1)} %get-tuple-element.19), channel_id=1, source_target_pairs={{1,0},{2,1},{3,2},{4,3},{5,4},{6,5},{7,6},{8,7},{9,8},{10,9},{11,1... | collective-permute-start | bytes 2359304 | tf_op jit(solution)/shard_map/ppermute | solution.py:33
  44.8 16.0 %collective-permute-start.3 = (f32[64,6,512]{2,0,1:T(8,128)S(1)}, f32[64,6,512]{2,0,1:T(8,128)S(1)}, u32[]{:S(2)}, u32[]{:S(2)}) collective-permute-start(f32[64,6,512]{2,0,1:T(8,128)S(1)} %get-tuple-element.20), channel_id=1, source_target_pairs={{0,1},{1,2},{2,3},{3,4},{4,5},{5,6},{6,7},{7,8},{8,9},{9,10},{10,1... | collective-permute-start | bytes 2359304 | tf_op jit(solution)/shard_map/ppermute | solution.py:30
  60.8 0.9 copy-start.7
  61.7 0.9 copy-start.8
  71.8 16.3 %copy-start.3 = (f32[64,8,512]{2,0,1:T(8,128)S(1)}, f32[64,8,512]{2,0,1:T(8,128)}, u32[]{:S(2)}) copy-start(f32[64,8,512]{2,0,1:T(8,128)} %get-tuple-element.12) | copy-start | bytes 3145732
  72.0 14.9 %collective-permute-start.4 = (f32[64,6,512]{2,0,1:T(8,128)S(1)}, f32[64,6,512]{2,0,1:T(8,128)S(1)}, u32[]{:S(2)}, u32[]{:S(2)}) collective-permute-start(f32[64,6,512]{2,0,1:T(8,128)S(1)} %get-tuple-element.17), channel_id=1, source_target_pairs={{1,0},{2,1},{3,2},{4,3},{5,4},{6,5},{7,6},{8,7},{9,8},{10,9},{11,1... | collective-permute-start | bytes 2359304 | tf_op jit(solution)/shard_map/ppermute | solution.py:33
  74.1 14.1 %collective-permute-start.5 = (f32[64,6,512]{2,0,1:T(8,128)S(1)}, f32[64,6,512]{2,0,1:T(8,128)}, u32[]{:S(2)}, u32[]{:S(2)}) collective-permute-start(f32[64,6,512]{2,0,1:T(8,128)S(1)} %get-tuple-element.18), channel_id=1, source_target_pairs={{0,1},{1,2},{2,3},{3,4},{4,5},{5,6},{6,7},{7,8},{8,9},{9,10},{10,1... | collective-permute-start | bytes 2359304 | tf_op jit(solution)/shard_map/ppermute | solution.py:30
  86.9 0.9 copy-start.6
  97.2 15.7 %collective-permute-start.6 = (f32[64,6,512]{2,0,1:T(8,128)S(1)}, f32[64,6,512]{2,0,1:T(8,128)S(1)}, u32[]{:S(2)}, u32[]{:S(2)}) collective-permute-start(f32[64,6,512]{2,0,1:T(8,128)S(1)} %get-tuple-element.15), channel_id=1, source_target_pairs={{1,0},{2,1},{3,2},{4,3},{5,4},{6,5},{7,6},{8,7},{9,8},{10,9},{11,1... | collective-permute-start | bytes 2359304 | tf_op jit(solution)/shard_map/ppermute | solution.py:33
  99.2 14.9 %collective-permute-start.7 = (f32[64,6,512]{2,0,1:T(8,128)S(1)}, f32[64,6,512]{2,0,1:T(8,128)}, u32[]{:S(2)}, u32[]{:S(2)}) collective-permute-start(f32[64,6,512]{2,0,1:T(8,128)S(1)} %get-tuple-element.16), channel_id=1, source_target_pairs={{0,1},{1,2},{2,3},{3,4},{4,5},{5,6},{6,7},{7,8},{8,9},{9,10},{10,1... | collective-permute-start | bytes 2359304 | tf_op jit(solution)/shard_map/ppermute | solution.py:30
  112.9 0.9 copy-start.5
  123.7 239.1 %all-gather.5.cloned.1.call-start = ((), (), s32[]{:S(2)}) async-start(), calls=%async_computation.3 | async-start | bytes 8912896 | tf_op jit(solution)/shard_map/all_gather | solution.py:112
  123.9 15.7 %collective-permute-start.8 = (f32[64,6,512]{2,0,1:T(8,128)S(1)}, f32[64,6,512]{2,0,1:T(8,128)S(1)}, u32[]{:S(2)}, u32[]{:S(2)}) collective-permute-start(f32[64,6,512]{2,0,1:T(8,128)S(1)} %get-tuple-element.13), channel_id=1, source_target_pairs={{1,0},{2,1},{3,2},{4,3},{5,4},{6,5},{7,6},{8,7},{9,8},{10,9},{11,1... | collective-permute-start | bytes 2359304 | tf_op jit(solution)/shard_map/ppermute | solution.py:33
  125.9 121.8 %copy-start.1 = (bf16[64,8,512]{2,0,1:T(8,128)(2,1)S(1)}, bf16[64,8,512]{2,0,1:T(8,128)(2,1)}, u32[]{:S(2)}) copy-start(bf16[64,8,512]{2,0,1:T(8,128)(2,1)} %get-tuple-element.9) | copy-start | bytes 1572868
  125.9 15.1 %collective-permute-start.9 = (f32[64,6,512]{2,0,1:T(8,128)S(1)}, f32[64,6,512]{2,0,1:T(8,128)S(1)}, u32[]{:S(2)}, u32[]{:S(2)}) collective-permute-start(f32[64,6,512]{2,0,1:T(8,128)S(1)} %get-tuple-element.14), channel_id=1, source_target_pairs={{0,1},{1,2},{2,3},{3,4},{4,5},{5,6},{6,7},{7,8},{8,9},{9,10},{10,1... | collective-permute-start | bytes 2359304 | tf_op jit(solution)/shard_map/ppermute | solution.py:30
  148.8 286.9 %reduce-scatter.7.cloned.1.call-start = ((), (), s32[]{:S(2)}) async-start(), calls=%async_computation.4 | async-start | bytes 557056
  254.2 114.8 %copy-start.4 = (bf16[64,8,512]{2,0,1:T(8,128)(2,1)S(1)}, bf16[64,8,512]{2,0,1:T(8,128)(2,1)}, u32[]{:S(2)}) copy-start(bf16[64,8,512]{2,0,1:T(8,128)(2,1)} %add_convert_fusion) | copy-start | bytes 1572868
  254.2 258.1 %reduce-scatter.9.cloned.1.call-start = ((), (), s32[]{:S(2)}) async-start(), calls=%async_computation.5 | async-start | bytes 557056
  362.8 6.2 %copy-start = (bf16[1024,8,512]{2,0,1:T(8,128)(2,1)S(1)}, bf16[1024,8,512]{2,0,1:T(8,128)(2,1)}, u32[]{:S(2)}) copy-start(bf16[1024,8,512]{2,0,1:T(8,128)(2,1)} %all-gather.3.cloned.1.call-done) | copy-start | bytes 25165828
Sparse Core Ops, SparseCore 0:
  123.8 123.8 all-gather.2
  250.1 112.7 all-gather.4
  366.8 68.9 reduce-scatter.6
  440.1 72.1 reduce-scatter.8
where the time goes:
time: 522 us; the launch traced here: 520 us
  waiting for transfers between devices  396 us (76%)
  other arithmetic  45.1 us (9%)
  starting transfers between devices  38.9 us (7%)
  matrix products  15.3 us (3%)
  between operations  14.1 us (3%)
  local copies, waits for them, and re-layouts  11.3 us (2%)
    unnamed x6, waiting for transfers between devices  137 us
    all_gather x1, waiting for transfers between devices, on_device(): lax.all_gather(applied_low, 'band', axis=0, tiled=True)  108 us
    all_gather x1, waiting for transfers between devices, on_device(): lax.all_gather(filtered_low, 'band', axis=0, tiled=True)  98.8 us
    ppermute x5, waiting for transfers between devices, with_halo(): lax.ppermute(lax.slice_in_dim(block, 0, width, axis=dim), axis, backward)  43.1 us
    ppermute x5, starting transfers between devices, with_halo(): lax.ppermute(lax.slice_in_dim(block, block.shape[dim] - width, None, axis...  28.8 us
    sub x2, other arithmetic, chebyshev(): (operate(current) - center * current) * (2.0 * sigma_next / half_width)  18.1 us
  transfers between devices with their start and end apart: 14, of which 13 were waited for; matrix products, arithmetic and copies ran while one was open for 5% of the time, Pallas kernels for 0%

commit v1 on v0

v1 whole, which is shorter than its diff:
```python
import jax
import jax.numpy as jnp
import numpy as np
from jax import lax
from jax.experimental import pallas as pl
from jax.experimental.pallas import tpu as pltpu
from jax.sharding import PartitionSpec as P

DEGREE = 4
NY = 16
NX = 32
NZ = 128
PLANE = NX * NY
NCELLS = NZ * PLANE
SLABS = 16
DEPTH = NZ // SLABS
OWN = 4
HALF = PLANE // 2
RING = 8
PEERS = 32

COEFFS = (
    -5369.0 / 1800.0,
    12.0 / 7.0,
    -15.0 / 56.0,
    10.0 / 189.0,
    -1.0 / 112.0,
    2.0 / 1925.0,
    -1.0 / 16632.0,
)
SPACING = 0.6
LOWER = -2.0
CUTOFF = 8.0
UPPER = 32.0
KINETIC = -0.5 / SPACING**2
DIAGONAL = 3.0 * COEFFS[0] * KINETIC
BF16 = jnp.bfloat16
F32 = jnp.float32


def line_matrix(size):
    matrix = np.zeros((size, size))
    for reach in range(1, 7):
        matrix += KINETIC * COEFFS[reach] * (np.eye(size, k=reach) + np.eye(size, k=-reach))
    return matrix


def two_terms(matrix):
    high = matrix.astype(jnp.bfloat16)
    low = (matrix - high.astype(np.float64)).astype(jnp.bfloat16)
    return high, low


def stencil_matrices():
    plane = np.kron(line_matrix(NX), np.eye(NY)) + np.kron(np.eye(NX), line_matrix(NY))
    plane_high, plane_low = two_terms(plane)
    z_high, z_low = two_terms(line_matrix(NZ))
    return plane_high, plane_low, np.concatenate([z_high, z_low, z_high], axis=1)


def schedule():
    half_width = (UPPER - CUTOFF) / 2.0
    center = (UPPER + CUTOFF) / 2.0
    sigma_first = half_width / (LOWER - center)
    sigma = sigma_first
    steps = [(sigma_first / half_width, center, 0.0)]
    for _ in range(DEGREE - 1):
        sigma_next = 1.0 / (2.0 / sigma_first - sigma)
        steps.append((2.0 * sigma_next / half_width, center, sigma * sigma_next))
        sigma = sigma_next
    steps.append((1.0, 0.0, 0.0))
    return steps


def filter_kernel(x_ref, mh_ref, ml_ref, z_ref, out_ref, low_ref, app_ref,
                  field_a, field_b, pot, split, total):
    for slab in range(SLABS):
        rows = slice(slab * DEPTH, (slab + 1) * DEPTH)
        for orb in range(OWN):
            field_a[orb, rows, :] = x_ref[slab, orb]
        pot[rows, :] = x_ref[slab, OWN] + DIAGONAL

    def put_low(ref, orb, value):
        for slab in range(SLABS):
            rows = slice(slab * DEPTH, (slab + 1) * DEPTH)
            for side in range(2):
                ref[side * SLABS + slab, orb] = value[rows, side * HALF : (side + 1) * HALF].astype(BF16)

    current, previous = field_a, field_b
    steps = schedule()
    for number, (scale, center, back) in enumerate(steps):
        last = number == len(steps) - 1
        for orb in range(OWN):
            value = current[orb]
            high = value.astype(BF16)
            low = (value - high.astype(F32)).astype(BF16)
            split[0, orb * NZ : (orb + 1) * NZ, :] = high
            split[1, orb * NZ : (orb + 1) * NZ, :] = low
        total[...] = (
            jnp.dot(split[0], mh_ref[...], preferred_element_type=F32)
            + jnp.dot(split[0], ml_ref[...], preferred_element_type=F32)
            + jnp.dot(split[1], mh_ref[...], preferred_element_type=F32)
        )
        for orb in range(OWN):
            rows = slice(orb * NZ, (orb + 1) * NZ)
            stack = jnp.concatenate([split[0, rows, :], split[0, rows, :], split[1, rows, :]], axis=0)
            applied = total[rows, :] + jnp.dot(z_ref[...], stack, preferred_element_type=F32)
            value = current[orb]
            applied = applied + (pot[...] - center) * value
            if last:
                put_low(app_ref, orb, applied)
                continue
            following = scale * applied
            if number:
                following = following - back * previous[orb]
            previous[orb] = following
            if number == len(steps) - 2:
                put_low(low_ref, orb, following)
                for slab in range(SLABS):
                    out_ref[slab, orb] = following[slab * DEPTH : (slab + 1) * DEPTH, :]
        current, previous = previous, current


def run_filter(block):
    plane_high, plane_low, z_stack = stencil_matrices()
    vmem = pl.BlockSpec(memory_space=pltpu.VMEM)
    return pl.pallas_call(
        filter_kernel,
        out_shape=(
            jax.ShapeDtypeStruct((SLABS, OWN, DEPTH, PLANE), F32),
            jax.ShapeDtypeStruct((PEERS, OWN, DEPTH, HALF), BF16),
            jax.ShapeDtypeStruct((PEERS, OWN, DEPTH, HALF), BF16),
        ),
        in_specs=[vmem] * 4,
        out_specs=(vmem, vmem, vmem),
        scratch_shapes=[
            pltpu.VMEM((OWN, NZ, PLANE), F32),
            pltpu.VMEM((OWN, NZ, PLANE), F32),
            pltpu.VMEM((NZ, PLANE), F32),
            pltpu.VMEM((2, OWN * NZ, PLANE), BF16),
            pltpu.VMEM((OWN * NZ, PLANE), F32),
        ],
        compiler_params=pltpu.CompilerParams(vmem_limit_bytes=40 * 1024 * 1024),
        cost_estimate=pl.CostEstimate(flops=6_000_000_000, bytes_accessed=6_000_000, transcendentals=0),
        name="chebyshev",
    )(block, jnp.asarray(plane_high), jnp.asarray(plane_low), jnp.asarray(z_stack))


def pair_kernel(w_ref, r_ref, out_ref):
    for ring in range(RING):
        part = jnp.zeros((2 * 64, 256), F32)
        for depth in range(DEPTH):
            part = part + lax.dot_general(
                r_ref[ring, depth], w_ref[depth], (((1,), (1,)), ((), ())), preferred_element_type=F32
            )
        for side in range(2):
            for own in range(2):
                out_ref[own * SLABS + side * RING + ring] = part[
                    side * 64 : (side + 1) * 64, own * 128 : (own + 1) * 128
                ]


def run_pairs(weights, gathered):
    vmem = pl.BlockSpec(memory_space=pltpu.VMEM)
    return pl.pallas_call(
        pair_kernel,
        out_shape=jax.ShapeDtypeStruct((PEERS, 64, 128), F32),
        in_specs=[vmem, vmem],
        out_specs=vmem,
        compiler_params=pltpu.CompilerParams(vmem_limit_bytes=40 * 1024 * 1024),
        cost_estimate=pl.CostEstimate(flops=1_073_741_824, bytes_accessed=6_000_000, transcendentals=0),
        name="pairs",
    )(weights, gathered)


def plane_groups():
    return [[(side * RING + ring) * SLABS + slab for side in range(2) for slab in range(SLABS)] for ring in range(RING)]


def ring_groups():
    return [[side * RING + ring for ring in range(RING)] for side in range(2)]


def over_plane(block):
    return lax.all_to_all(block, ("band", "slab"), 0, 0, axis_index_groups=plane_groups(), tiled=True)


def by_depth(block):
    return block.reshape(PEERS * OWN, DEPTH, HALF).transpose(1, 0, 2)


def on_device(orbitals, potential):
    block = orbitals.reshape(SLABS, OWN, DEPTH, PLANE)
    shared = jnp.broadcast_to(potential[None, None], (SLABS, 1, DEPTH, PLANE))
    block = lax.all_to_all(jnp.concatenate([block, shared], axis=1), "slab", 0, 0, tiled=True)
    filtered, filtered_low, applied_low = run_filter(block)
    filtered_low = by_depth(over_plane(filtered_low))
    gathered = lax.all_gather(filtered_low, "band", axis=0, axis_index_groups=ring_groups())
    applied_low = by_depth(over_plane(applied_low))
    filtered = lax.all_to_all(filtered, "slab", 0, 0, tiled=True)
    weights = jnp.concatenate(
        [filtered_low[:, :64], applied_low[:, :64], filtered_low[:, 64:], applied_low[:, 64:]], axis=1
    )
    sums = over_plane(run_pairs(weights, gathered))
    sums = jnp.sum(sums, axis=0) / NCELLS
    return (
        filtered.reshape(SLABS * OWN, DEPTH, PLANE),
        sums[:, :64].T,
        sums[:, 64:].T,
    )


def solution(mesh):
    return jax.shard_map(
        on_device,
        mesh=mesh,
        in_specs=(P("band", "slab", None), P("slab", None)),
        out_specs=(P("band", "slab", None), P("band", "slab"), P("band", "slab")),
        check_vma=False,
    )
```

time: 522 us -> 154 us (0.30)
  waiting for transfers between devices: 396 us -> 51.8 us
  blocking collectives: 0 us -> 58.6 us
  other arithmetic: 45.1 us -> 1.59 us
  starting transfers between devices: 38.9 us -> 11.4 us
  matrix products: 15.3 us -> 0 us
  Pallas kernels: 0 us -> 9.44 us
    all_gather x2 -> x1, waiting for transfers between devices: 207 us -> 34.7 us  [on_device(): lax.all_gather(filtered_low, 'band', axis=0, axis_index_groups=ring_group...]
    unnamed x6 -> x1, waiting for transfers between devices: 137 us -> 0.02 us
    all_to_all x0 -> x3, blocking collectives: none -> 58.6 us  [the longest x2 30.4 us: over_plane(): lax.all_to_all(block, ('band', 'slab'), 0, 0, axis_index_groups=plane_gro...]
    ppermute x10 -> x0, waiting for transfers between devices: 51.9 us -> none  [the longest x5 43.1 us: with_halo(): lax.ppermute(lax.slice_in_dim(block, 0, width, axis=dim), axis, backward)]
    ppermute x10 -> x0, starting transfers between devices: 38.5 us -> none  [the longest x5 28.8 us: with_halo(): lax.ppermute(lax.slice_in_dim(block, block.shape[dim] - width, None, axis...]
    sub x2 -> x0, other arithmetic: 18.1 us -> none  [chebyshev(): (operate(current) - center * current) * (2.0 * sigma_next / half_width)]
    convert_element_type x8 -> x0, other arithmetic: 17.5 us -> none  [the longest x1 9.6 us: on_device(): filtered_low = filtered.astype(jnp.bfloat16)]
    all_to_all x0 -> x2, waiting for transfers between devices: none -> 17.1 us  [the longest x1 17.1 us: over_plane(): lax.all_to_all(block, ('band', 'slab'), 0, 0, axis_index_groups=plane_gro...]
  transfers between devices with their start and end apart: 14 -> 3, of which waited for: 13 -> 2; matrix products, arithmetic and copies ran while one was open for 5% -> 0% of each run, Pallas kernels for 0% -> 2%
where the time goes in v1:
time: 154 us; the launch traced here: 153 us
  blocking collectives  58.6 us (38%)
  waiting for transfers between devices  51.8 us (34%)
  between operations  14.1 us (9%)
  starting transfers between devices  11.4 us (7%)
  Pallas kernels  9.44 us (6%)
  local copies, waits for them, and re-layouts  6.46 us (4%)
  other arithmetic  1.59 us (1%)
    all_gather x1, waiting for transfers between devices, on_device(): lax.all_gather(filtered_low, 'band', axis=0, axis_index_groups=ring_group...  34.7 us
    all_to_all x2, blocking collectives, over_plane(): lax.all_to_all(block, ('band', 'slab'), 0, 0, axis_index_groups=plane_gro...  30.4 us
    all_to_all x1, blocking collectives, on_device(): lax.all_to_all(jnp.concatenate([block, shared], axis=1), 'slab', 0, 0, ti...  28.2 us
    all_to_all x1, waiting for transfers between devices, over_plane(): lax.all_to_all(block, ('band', 'slab'), 0, 0, axis_index_groups=plane_gro...  17.1 us
    all_to_all x1, starting transfers between devices, over_plane(): lax.all_to_all(block, ('band', 'slab'), 0, 0, axis_index_groups=plane_gro...  7.53 us
    pallas_call x1, Pallas kernels, run_filter(): pl.pallas_call(filter_kernel, out_shape=(jax.ShapeDtypeStruct((SLABS, OWN...  5.72 us
    unnamed x13, local copies, waits for them, and re-layouts  4.58 us
    all_to_all x1, starting transfers between devices, on_device(): filtered = lax.all_to_all(filtered, 'slab', 0, 0, tiled=True)  3.81 us
  transfers between devices with their start and end apart: 3, of which 2 were waited for; matrix products, arithmetic and copies ran while one was open for 0% of the time, Pallas kernels for 2%

profile of v1, /device:TPU:1, one launch (start us, length us, event | category | flops | bytes accessed | tf_op | source)
XLA Modules:
  0.0 153.4 jit_solution(11717643498220489861)
XLA Ops:
  7.2 0.0 all-gather.3.cloned.1.call-start
  7.2 0.7 broadcast_in_dim.2
  8.0 0.0 copy-start.1
  8.0 0.0 copy-start.2
  8.0 0.0 copy-start.3
  8.0 1.4 pad_maximum_fusion
  9.4 28.2 %all_to_all.25.x_ref = f32[16,5,8,512]{3,2,1,0:T(8,128)S(1)} all-to-all(f32[16,5,8,512]{3,2,1,0:T(8,128)S(1)} %pad_maximum_fusion), channel_id=1, replica_groups=mesh['band'=16,'slab'=16] {'slab'}, dimensions={0} | all-to-all | bytes 2621440 | tf_op jit(solution)/shard_map/all_to_all | solution.py:195
  37.6 0.0 copy-done.1
  37.6 0.0 copy-done.2
  37.6 0.0 copy-done.3
  37.6 5.7 %chebyshev.1 = (f32[16,4,8,512]{3,2,1,0:T(8,128)}, bf16[32,4,8,256]{3,2,1,0:T(8,128)(2,1)S(1)}, bf16[32,4,8,256]{3,2,1,0:T(8,128)(2,1)S(1)}) custom-call(f32[16,5,8,512]{3,2,1,0:T(8,128)S(1)} %all_to_all.25.x_ref, bf16[512,512]{1,0:T(8,128)(2,1)S(1)} %copy-done.2, bf16[512,512]{1,0:T(8,128)(2,1)S(1)} %copy-done.1, bf16[128,384]{1,0:T(8,128)(2,1)S(1)} %copy-done.3), custom_call_target="tpu_custom_call" | custom-call | flops 6000000000 | bytes 6000000 | tf_op jit(solution)/shard_map/chebyshev/pallas_call | solution.py:127
  43.3 15.2 %all_to_all.26 = bf16[32,4,8,256]{3,2,1,0:T(8,128)(2,1)S(1)} all-to-all(bf16[32,4,8,256]{3,2,1,0:T(8,128)(2,1)S(1)} %get-tuple-element.7), channel_id=1, replica_groups={{0,1,2,3,4,5,6,7,8,9,10,11,12,13,14,15,128,129,130,131,132,133,134,135,..., dimensions={0} | all-to-all | bytes 1048576 | tf_op jit(solution)/shard_map/all_to_all | solution.py:185
  58.5 0.9 copy.19
  59.4 0.0 all-gather.3.cloned.1.call-update
  59.4 0.0 copy-start.4
  59.4 15.2 %all_to_all.27 = bf16[32,4,8,256]{3,2,1,0:T(8,128)(2,1)S(1)} all-to-all(bf16[32,4,8,256]{3,2,1,0:T(8,128)(2,1)S(1)} %get-tuple-element.8), channel_id=1, replica_groups={{0,1,2,3,4,5,6,7,8,9,10,11,12,13,14,15,128,129,130,131,132,133,134,135,..., dimensions={0} | all-to-all | bytes 1048576 | tf_op jit(solution)/shard_map/all_to_all | solution.py:185
  74.7 3.8 %all-to-all-start.1 = ((f32[16,4,8,512]{3,2,1,0:T(8,128)}), f32[16,4,8,512]{3,2,1,0:T(8,128)S(1)}, u32[]{:S(2)}, u32[]{:S(2)}) async-start(f32[16,4,8,512]{3,2,1,0:T(8,128)} %get-tuple-element.6), calls=%async_computation.1 | async-start | bytes 2097152 | tf_op jit(solution)/shard_map/all_to_all | solution.py:200
  78.5 0.1 copy.18
  78.6 0.0 copy-done.4
  78.7 0.1 pad_maximum_fusion.1.w_ref
  78.8 34.7 %all-gather.3.cloned.1.call-done = bf16[64,128,256]{2,1,0:T(8,128)(2,1)} async-done(((bf16[8,128,256]{2,1,0:T(8,128)(2,1)}), bf16[64,128,256]{2,1,0:T(8,128)(2,1)}) %all-gather.3.cloned.1.call-update) | async-done | bytes 4194320 | tf_op jit(solution)/shard_map/all_gather | solution.py:198
  113.5 0.0 copy-start
  113.5 2.2 %copy-done = bf16[64,128,256]{2,1,0:T(8,128)(2,1)S(1)} copy-done((bf16[64,128,256]{2,1,0:T(8,128)(2,1)S(1)}, bf16[64,128,256]{2,1,0:T(8,128)(2,1)}, u32[]{:S(2)}) %copy-start) | copy-done | bytes 4194328
  115.7 3.7 %pairs.1 = f32[32,64,128]{2,1,0:T(8,128)} custom-call(bf16[8,256,256]{2,1,0:T(8,128)(2,1)S(1)} %pad_maximum_fusion.1.w_ref, bf16[8,8,128,256]{3,2,1,0:T(8,128)(2,1)S(1)} %bitcast.15), custom_call_target="tpu_custom_call" | custom-call | flops 1073741824 | bytes 6000000 | tf_op jit(solution)/shard_map/pairs/pallas_call | solution.py:165
  119.4 0.0 all-to-all-done.1
  119.4 7.5 %all-to-all-start.4 = ((f32[32,64,128]{2,1,0:T(8,128)}), f32[32,64,128]{2,1,0:T(8,128)S(1)}, u32[]{:S(2)}, u32[]{:S(2)}) async-start(f32[32,64,128]{2,1,0:T(8,128)} %pairs.1), calls=%async_computation.4 | async-start | bytes 2097152 | tf_op jit(solution)/shard_map/all_to_all | solution.py:185
  126.9 17.1 %all-to-all-done.4 = f32[32,64,128]{2,1,0:T(8,128)S(1)} async-done(((f32[32,64,128]{2,1,0:T(8,128)}), f32[32,64,128]{2,1,0:T(8,128)S(1)}, u32[]{:S(2)}, u32[]{:S(2)}) %all-to-all-start.4) | async-done | bytes 1048608 | tf_op jit(solution)/shard_map/all_to_all | solution.py:185
  144.0 0.1 reduce_sum.9
  144.1 0.1 slice_bitcast_fusion
  144.1 0.7 copy.13
  144.9 0.7 copy.12
  145.6 1.0 copy.21
  (3 shorter events, 0.1 us)
Async XLA Ops:
  7.2 106.3 %all-gather.3.cloned.1.call-start = ((), (), s32[]{:S(2)}) async-start(), calls=%async_computation.5 | async-start | bytes 4718592 | tf_op jit(solution)/shard_map/all_gather | solution.py:198
  8.0 29.6 %copy-start.1 = (bf16[512,512]{1,0:T(8,128)(2,1)S(1)}, bf16[512,512]{1,0:T(8,128)(2,1)}, u32[]{:S(2)}) copy-start(bf16[512,512]{1,0:T(8,128)(2,1)} %constant.12.clone.ml_ref) | copy-start | bytes 1572868
  8.0 29.6 %copy-start.2 = (bf16[512,512]{1,0:T(8,128)(2,1)S(1)}, bf16[512,512]{1,0:T(8,128)(2,1)}, u32[]{:S(2)}) copy-start(bf16[512,512]{1,0:T(8,128)(2,1)} %constant.11.clone.mh_ref) | copy-start | bytes 1572868
  8.0 29.6 %copy-start.3 = (bf16[128,384]{1,0:T(8,128)(2,1)S(1)}, bf16[128,384]{1,0:T(8,128)(2,1)}, u32[]{:S(2)}) copy-start(bf16[128,384]{1,0:T(8,128)(2,1)} %constant.13.clone.z_ref) | copy-start | bytes 294916
  59.4 19.2 %copy-start.4 = (bf16[128,8,256]{2,0,1:T(8,128)(2,1)S(1)}, bf16[128,8,256]{2,0,1:T(8,128)(2,1)}, u32[]{:S(2)}) copy-start(bf16[128,8,256]{2,0,1:T(8,128)(2,1)} %copy.19) | copy-start | bytes 1572868
  74.7 44.7 %all-to-all-start.1 = ((f32[16,4,8,512]{3,2,1,0:T(8,128)}), f32[16,4,8,512]{3,2,1,0:T(8,128)S(1)}, u32[]{:S(2)}, u32[]{:S(2)}) async-start(f32[16,4,8,512]{3,2,1,0:T(8,128)} %get-tuple-element.6), calls=%async_computation.1 | async-start | bytes 2097152 | tf_op jit(solution)/shard_map/all_to_all | solution.py:200
  113.5 2.2 %copy-start = (bf16[64,128,256]{2,1,0:T(8,128)(2,1)S(1)}, bf16[64,128,256]{2,1,0:T(8,128)(2,1)}, u32[]{:S(2)}) copy-start(bf16[64,128,256]{2,1,0:T(8,128)(2,1)} %all-gather.3.cloned.1.call-done) | copy-start | bytes 12582916
  119.4 24.6 %all-to-all-start.4 = ((f32[32,64,128]{2,1,0:T(8,128)}), f32[32,64,128]{2,1,0:T(8,128)S(1)}, u32[]{:S(2)}, u32[]{:S(2)}) async-start(f32[32,64,128]{2,1,0:T(8,128)} %pairs.1), calls=%async_computation.4 | async-start | bytes 2097152 | tf_op jit(solution)/shard_map/all_to_all | solution.py:185
Sparse Core Ops, SparseCore 0:
  59.6 53.8 all-gather.2

commit v2 on v1

--- a/solution.py
+++ b/solution.py
@@ -146,43 +146,119 @@
     )(block, jnp.asarray(plane_high), jnp.asarray(plane_low), jnp.asarray(z_stack))
 
 
-def pair_kernel(w_ref, r_ref, out_ref):
-    for ring in range(RING):
-        part = jnp.zeros((2 * 64, 256), F32)
-        for depth in range(DEPTH):
-            part = part + lax.dot_general(
-                r_ref[ring, depth], w_ref[depth], (((1,), (1,)), ((), ())), preferred_element_type=F32
-            )
-        for side in range(2):
-            for own in range(2):
-                out_ref[own * SLABS + side * RING + ring] = part[
-                    side * 64 : (side + 1) * 64, own * 128 : (own + 1) * 128
-                ]
-
-
-def run_pairs(weights, gathered):
+def pair_kernel(w_ref, *refs):
+    blocks, keep_ref, send_ref = refs[:-2], refs[-2], refs[-1]
+    place = lax.rem(lax.axis_index("band"), RING)
+    core = lax.rem(lax.axis_index("slab"), 2)
+    last = RING // 2
+    pieces = {0: [(0, blocks[0])]}
+    for step in range(1, last):
+        at = 1 + 4 * (step - 1)
+        pieces[-step] = [(0, blocks[at]), (last, blocks[at + 1])]
+        pieces[step] = [(0, blocks[at + 2]), (last, blocks[at + 3])]
+    pieces[last] = [(0, blocks[-2]), (last, blocks[-1])]
+    for shift, parts in pieces.items():
+        total = jnp.zeros((128, 256), F32)
+        for start, ref in parts:
+            for depth in range(ref.shape[0]):
+                total = total + lax.dot_general(
+                    ref[depth], w_ref[start + depth], (((1,), (1,)), ((), ())), preferred_element_type=F32
+                )
+        ring = lax.rem(place + shift + RING, RING)
+        mine = lax.rem(ring, 2) == core
+        slot = lax.div(ring, 2)
+        for own in range(2):
+            for side in range(2):
+                block = total[side * 64 : (side + 1) * 64, own * 128 : (own + 1) * 128]
+                index = own * RING + side * last + slot
+
+                @pl.when(mine)
+                def _():
+                    keep_ref[index] = block
+
+                @pl.when(jnp.logical_not(mine))
+                def _():
+                    send_ref[index] = block
+
+
+def run_pairs(weights, blocks):
     vmem = pl.BlockSpec(memory_space=pltpu.VMEM)
+    shape = jax.ShapeDtypeStruct((2 * RING, 64, 128), F32)
     return pl.pallas_call(
         pair_kernel,
-        out_shape=jax.ShapeDtypeStruct((PEERS, 64, 128), F32),
-        in_specs=[vmem, vmem],
-        out_specs=vmem,
+        out_shape=(shape, shape),
+        in_specs=[vmem] * (1 + len(blocks)),
+        out_specs=(vmem, vmem),
         compiler_params=pltpu.CompilerParams(vmem_limit_bytes=40 * 1024 * 1024),
         cost_estimate=pl.CostEstimate(flops=1_073_741_824, bytes_accessed=6_000_000, transcendentals=0),
         name="pairs",
-    )(weights, gathered)
+    )(weights, *blocks)
+
+
+def finish_kernel(parts_ref, gram_ref, projected_ref):
+    total = jnp.sum(parts_ref[...], axis=0) * (1.0 / NCELLS)
+    turned = total.T
+    gram_ref[...] = turned[:64]
+    projected_ref[...] = turned[64:]
+
+
+def run_finish(parts):
+    vmem = pl.BlockSpec(memory_space=pltpu.VMEM)
+    shape = jax.ShapeDtypeStruct((64, 64), F32)
+    return pl.pallas_call(
+        finish_kernel,
+        out_shape=(shape, shape),
+        in_specs=[vmem],
+        out_specs=(vmem, vmem),
+        name="finish",
+    )(parts)
 
 
 def plane_groups():
     return [[(side * RING + ring) * SLABS + slab for side in range(2) for slab in range(SLABS)] for ring in range(RING)]
 
 
-def ring_groups():
-    return [[side * RING + ring for ring in range(RING)] for side in range(2)]
+def core_groups():
+    return [
+        [(side * RING + ring) * SLABS + 2 * chip + core for side in range(2) for chip in range(SLABS // 2)]
+        for ring in range(RING)
+        for core in range(2)
+    ]
+
+
+def ring_pairs(step):
+    return [
+        ((side * RING + ring) * SLABS + slab, (side * RING + (ring + step) % RING) * SLABS + slab)
+        for side in range(2)
+        for ring in range(RING)
+        for slab in range(SLABS)
+    ]
+
+
+def core_pairs():
+    return [(place, place ^ 1) for place in range(2 * RING * SLABS)]
+
+
+BOTH = ("band", "slab")
+
+
+def around_ring(block):
+    half = RING // 2
+    ahead = [block[:half], block[half:]]
+    behind = list(ahead)
+    blocks = [block]
+    for _ in range(half - 1):
+        for chunk in range(2):
+            ahead[chunk] = lax.ppermute(ahead[chunk], BOTH, ring_pairs(1))
+            behind[chunk] = lax.ppermute(behind[chunk], BOTH, ring_pairs(-1))
+        blocks += ahead + behind
+    blocks.append(lax.ppermute(ahead[0], BOTH, ring_pairs(1)))
+    blocks.append(lax.ppermute(behind[1], BOTH, ring_pairs(-1)))
+    return blocks
 
 
 def over_plane(block):
-    return lax.all_to_all(block, ("band", "slab"), 0, 0, axis_index_groups=plane_groups(), tiled=True)
+    return lax.all_to_all(block, BOTH, 0, 0, axis_index_groups=plane_groups(), tiled=True)
 
 
 def by_depth(block):
@@ -195,19 +271,17 @@
     block = lax.all_to_all(jnp.concatenate([block, shared], axis=1), "slab", 0, 0, tiled=True)
     filtered, filtered_low, applied_low = run_filter(block)
     filtered_low = by_depth(over_plane(filtered_low))
-    gathered = lax.all_gather(filtered_low, "band", axis=0, axis_index_groups=ring_groups())
+    blocks = around_ring(filtered_low)
     applied_low = by_depth(over_plane(applied_low))
     filtered = lax.all_to_all(filtered, "slab", 0, 0, tiled=True)
     weights = jnp.concatenate(
         [filtered_low[:, :64], applied_low[:, :64], filtered_low[:, 64:], applied_low[:, 64:]], axis=1
     )
-    sums = over_plane(run_pairs(weights, gathered))
-    sums = jnp.sum(sums, axis=0) / NCELLS
-    return (
-        filtered.reshape(SLABS * OWN, DEPTH, PLANE),
-        sums[:, :64].T,
-        sums[:, 64:].T,
-    )
+    keep, send = run_pairs(weights, blocks)
+    sums = keep + lax.ppermute(send, BOTH, core_pairs())
+    sums = lax.all_to_all(sums, BOTH, 0, 0, axis_index_groups=core_groups(), tiled=True)
+    gram, projected = run_finish(sums)
+    return filtered.reshape(SLABS * OWN, DEPTH, PLANE), gram, projected
 
 
 def solution(mesh):

time: 154 us -> 138 us (0.90)
  starting transfers between devices: 11.4 us -> 42.3 us
  waiting for transfers between devices: 51.8 us -> 28.4 us
  blocking collectives: 58.6 us -> 43.5 us
  between operations: 14.1 us -> 0.8 us
  Pallas kernels: 9.44 us -> 14.2 us
    all_gather x1 -> x0, waiting for transfers between devices: 34.7 us -> none  [on_device(): lax.all_gather(filtered_low, 'band', axis=0, axis_index_groups=ring_group...]
    ppermute x0 -> x15, starting transfers between devices: none -> 21.5 us  [the longest x6 19.2 us: around_ring(): behind[chunk] = lax.ppermute(behind[chunk], BOTH, ring_pairs(-1))]
    ppermute x0 -> x15, waiting for transfers between devices: none -> 18.9 us  [the longest x6 10.5 us: around_ring(): ahead[chunk] = lax.ppermute(ahead[chunk], BOTH, ring_pairs(1))]
    all_to_all x2 -> x1, blocking collectives: 30.4 us -> 15.2 us  [over_plane(): lax.all_to_all(block, BOTH, 0, 0, axis_index_groups=plane_groups(), tiled...]
    all_to_all x1 -> x2, waiting for transfers between devices: 17.1 us -> 9.52 us  [the longest x1 9.52 us: on_device(): lax.all_to_all(sums, BOTH, 0, 0, axis_index_groups=core_groups(), tiled=T...]
    all_to_all x1, starting transfers between devices: 3.81 us -> 9.26 us  [on_device(): filtered = lax.all_to_all(filtered, 'slab', 0, 0, tiled=True)]
    all_to_all x1 -> x2, starting transfers between devices: 7.53 us -> 11.5 us  [the longest x1 6.68 us: on_device(): lax.all_to_all(sums, BOTH, 0, 0, axis_index_groups=core_groups(), tiled=T...]
    pallas_call x1 -> x2, Pallas kernels: 3.72 us -> 7.51 us  [the longest x1 5.74 us: run_pairs(): pl.pallas_call(pair_kernel, out_shape=(shape, shape), in_specs=[vmem] * (...]
  transfers between devices with their start and end apart: 3 -> 18, of which waited for: 2 -> 7; matrix products, arithmetic and copies ran while one was open for 0% -> 2% of each run, Pallas kernels for 2% -> 4%
where the time goes in v2:
time: 138 us; the launch traced here: 137 us
  blocking collectives  43.5 us (32%)
  starting transfers between devices  42.3 us (31%)
  waiting for transfers between devices  28.4 us (21%)
  Pallas kernels  14.2 us (10%)
  local copies, waits for them, and re-layouts  5.16 us (4%)
  other arithmetic  2.32 us (2%)
    all_to_all x1, blocking collectives, on_device(): lax.all_to_all(jnp.concatenate([block, shared], axis=1), 'slab', 0, 0, ti...  28.3 us
    ppermute x6, starting transfers between devices, around_ring(): behind[chunk] = lax.ppermute(behind[chunk], BOTH, ring_pairs(-1))  19.2 us
    all_to_all x1, blocking collectives, over_plane(): lax.all_to_all(block, BOTH, 0, 0, axis_index_groups=plane_groups(), tiled...  15.2 us
    ppermute x6, waiting for transfers between devices, around_ring(): ahead[chunk] = lax.ppermute(ahead[chunk], BOTH, ring_pairs(1))  10.5 us
    all_to_all x1, waiting for transfers between devices, on_device(): lax.all_to_all(sums, BOTH, 0, 0, axis_index_groups=core_groups(), tiled=T...  9.52 us
    all_to_all x1, starting transfers between devices, on_device(): filtered = lax.all_to_all(filtered, 'slab', 0, 0, tiled=True)  9.26 us
    pallas_call x1, Pallas kernels, run_filter(): pl.pallas_call(filter_kernel, out_shape=(jax.ShapeDtypeStruct((SLABS, OWN...  6.73 us
    all_to_all x1, starting transfers between devices, on_device(): lax.all_to_all(sums, BOTH, 0, 0, axis_index_groups=core_groups(), tiled=T...  6.68 us
  transfers between devices with their start and end apart: 18, of which 7 were waited for; matrix products, arithmetic and copies ran while one was open for 2% of the time, Pallas kernels for 4%

profile of v2, /device:TPU:1, one launch (start us, length us, event | category | flops | bytes accessed | tf_op | source)
XLA Modules:
  0.0 136.7 jit_solution(6021919374398015645)
XLA Ops:
  0.6 0.7 broadcast_in_dim.2
  1.4 1.4 pad_maximum_fusion
  2.7 0.0 copy-start
  2.7 0.0 copy-start.1
  2.8 0.0 copy-start.2
  2.8 28.3 %all_to_all.25.x_ref = f32[16,5,8,512]{3,2,1,0:T(8,128)S(1)} all-to-all(f32[16,5,8,512]{3,2,1,0:T(8,128)S(1)} %pad_maximum_fusion), channel_id=1, replica_groups=mesh['band'=16,'slab'=16] {'slab'}, dimensions={0} | all-to-all | bytes 2621440 | tf_op jit(solution)/shard_map/all_to_all | solution.py:271
  31.1 6.7 %chebyshev.1 = (f32[16,4,8,512]{3,2,1,0:T(8,128)}, bf16[32,4,8,256]{3,2,1,0:T(8,128)(2,1)S(1)}, bf16[32,4,8,256]{3,2,1,0:T(8,128)(2,1)}) custom-call(f32[16,5,8,512]{3,2,1,0:T(8,128)S(1)} %all_to_all.25.x_ref, bf16[512,512]{1,0:T(8,128)(2,1)S(1)} %copy-done.1, bf16[512,512]{1,0:T(8,128)(2,1)S(1)} %copy-done, bf16[128,384]{1,0:T(8,128)(2,1)S(1)} %copy-done.2), custom_call_target="tpu_custom_call" | custom-call | flops 6000000000 | bytes 6000000 | tf_op jit(solution)/shard_map/chebyshev/pallas_call | solution.py:127
  37.8 15.2 %all_to_all.26 = bf16[32,4,8,256]{3,2,1,0:T(8,128)(2,1)S(1)} all-to-all(bf16[32,4,8,256]{3,2,1,0:T(8,128)(2,1)S(1)} %get-tuple-element.11), channel_id=1, replica_groups={{0,1,2,3,4,5,6,7,8,9,10,11,12,13,14,15,128,129,130,131,132,133,134,135,..., dimensions={0} | all-to-all | bytes 1048576 | tf_op jit(solution)/shard_map/all_to_all | solution.py:261
  53.0 0.1 copy.15
  53.1 5.7 %collective-permute-start.3 = (bf16[4,128,256]{2,1,0:T(8,128)(2,1)S(1)}, bf16[4,128,256]{2,1,0:T(8,128)(2,1)S(1)}, u32[]{:S(2)}, u32[]{:S(2)}) collective-permute-start(bf16[4,128,256]{2,1,0:T(8,128)(2,1)S(1)} %get-tuple-element.17), channel_id=1, source_target_pairs={{0,112},{1,113},{2,114},{3,115},{4,116},{5,117},{6,118},{7,119},{8... | collective-permute-start | bytes 786440 | tf_op jit(solution)/shard_map/ppermute | solution.py:253
  58.8 0.0 collective-permute-start
  58.8 4.8 %all-to-all-start.3 = ((bf16[32,4,8,256]{3,2,1,0:T(8,128)(2,1)}), bf16[32,4,8,256]{3,2,1,0:T(8,128)(2,1)}, u32[]{:S(2)}, u32[]{:S(2)}) async-start(bf16[32,4,8,256]{3,2,1,0:T(8,128)(2,1)} %get-tuple-element.12), calls=%async_computation.3 | async-start | bytes 1048576 | tf_op jit(solution)/shard_map/all_to_all | solution.py:261
  63.6 0.1 collective-permute-start.1
  63.7 3.0 %collective-permute-start.2 = (bf16[4,128,256]{2,1,0:T(8,128)(2,1)S(1)}, bf16[4,128,256]{2,1,0:T(8,128)(2,1)S(1)}, u32[]{:S(2)}, u32[]{:S(2)}) collective-permute-start(bf16[4,128,256]{2,1,0:T(8,128)(2,1)S(1)} %get-tuple-element.18), channel_id=1, source_target_pairs={{0,112},{1,113},{2,114},{3,115},{4,116},{5,117},{6,118},{7,119},{8... | collective-permute-start | bytes 786440 | tf_op jit(solution)/shard_map/ppermute | solution.py:253
  66.7 0.0 collective-permute-done.3.refs_4_
  66.7 1.4 %collective-permute-start.7 = (bf16[4,128,256]{2,1,0:T(8,128)(2,1)S(1)}, bf16[4,128,256]{2,1,0:T(8,128)(2,1)S(1)}, u32[]{:S(2)}, u32[]{:S(2)}) collective-permute-start(bf16[4,128,256]{2,1,0:T(8,128)(2,1)S(1)} %collective-permute-done.3.refs_4_), channel_id=1, source_target_pairs={{0,112},{1,113},{2,114},{3,115},{4,116},{5,117},{6,118},{7,119},{8... | collective-permute-start | bytes 786440 | tf_op jit(solution)/shard_map/ppermute | solution.py:253
  68.1 0.0 collective-permute-done.refs_1_
  68.1 0.1 collective-permute-start.4
  68.2 5.5 %collective-permute-done.1.refs_2_ = bf16[4,128,256]{2,1,0:T(8,128)(2,1)S(1)} collective-permute-done((bf16[4,128,256]{2,1,0:T(8,128)(2,1)S(1)}, bf16[4,128,256]{2,1,0:T(8,128)(2,1)S(1)}, u32[]{:S(2)}, u32[]{:S(2)}) %collective-permute-start.1) | collective-permute-done | bytes 262176 | tf_op jit(solution)/shard_map/ppermute | solution.py:252
  73.6 0.0 collective-permute-done.2.refs_3_
  73.6 2.7 %collective-permute-start.6 = (bf16[4,128,256]{2,1,0:T(8,128)(2,1)S(1)}, bf16[4,128,256]{2,1,0:T(8,128)(2,1)S(1)}, u32[]{:S(2)}, u32[]{:S(2)}) collective-permute-start(bf16[4,128,256]{2,1,0:T(8,128)(2,1)S(1)} %collective-permute-done.2.refs_3_), channel_id=1, source_target_pairs={{0,112},{1,113},{2,114},{3,115},{4,116},{5,117},{6,118},{7,119},{8... | collective-permute-start | bytes 786440 | tf_op jit(solution)/shard_map/ppermute | solution.py:253
  76.3 1.3 collective-permute-done.7.refs_8_
  77.6 3.4 %collective-permute-start.11 = (bf16[4,128,256]{2,1,0:T(8,128)(2,1)S(1)}, bf16[4,128,256]{2,1,0:T(8,128)(2,1)S(1)}, u32[]{:S(2)}, u32[]{:S(2)}) collective-permute-start(bf16[4,128,256]{2,1,0:T(8,128)(2,1)S(1)} %collective-permute-done.7.refs_8_), channel_id=1, source_target_pairs={{0,112},{1,113},{2,114},{3,115},{4,116},{5,117},{6,118},{7,119},{8... | collective-permute-start | bytes 786440 | tf_op jit(solution)/shard_map/ppermute | solution.py:253
  81.0 0.0 collective-permute-done.4.refs_5_
  81.0 0.0 collective-permute-start.8
  81.0 9.3 %all-to-all-start.1 = ((f32[16,4,8,512]{3,2,1,0:T(8,128)}), f32[16,4,8,512]{3,2,1,0:T(8,128)}, u32[]{:S(2)}, u32[]{:S(2)}) async-start(f32[16,4,8,512]{3,2,1,0:T(8,128)} %get-tuple-element.10), calls=%async_computation.1 | async-start | bytes 2097152 | tf_op jit(solution)/shard_map/all_to_all | solution.py:276
  90.3 1.1 copy.14
  91.5 0.1 collective-permute-start.9
  91.6 0.0 collective-permute-done.6.refs_7_
  91.6 3.0 %collective-permute-start.10 = (bf16[4,128,256]{2,1,0:T(8,128)(2,1)S(1)}, bf16[4,128,256]{2,1,0:T(8,128)(2,1)S(1)}, u32[]{:S(2)}, u32[]{:S(2)}) collective-permute-start(bf16[4,128,256]{2,1,0:T(8,128)(2,1)S(1)} %collective-permute-done.6.refs_7_), channel_id=1, source_target_pairs={{0,112},{1,113},{2,114},{3,115},{4,116},{5,117},{6,118},{7,119},{8... | collective-permute-start | bytes 786440 | tf_op jit(solution)/shard_map/ppermute | solution.py:253
  94.6 1.4 %collective-permute-start.13 = (bf16[4,128,256]{2,1,0:T(8,128)(2,1)S(1)}, bf16[4,128,256]{2,1,0:T(8,128)(2,1)S(1)}, u32[]{:S(2)}, u32[]{:S(2)}) collective-permute-start(bf16[4,128,256]{2,1,0:T(8,128)(2,1)S(1)} %collective-permute-done.11.refs_12_), channel_id=1, source_target_pairs={{0,112},{1,113},{2,114},{3,115},{4,116},{5,117},{6,118},{7,119},{8... | collective-permute-start | bytes 786440 | tf_op jit(solution)/shard_map/ppermute | solution.py:256
  96.0 0.0 collective-permute-done.8.refs_9_
  96.0 0.1 collective-permute-start.12
  96.1 0.1 pad_maximum_fusion.1.w_ref
  96.2 5.0 %collective-permute-done.9.refs_10_ = bf16[4,128,256]{2,1,0:T(8,128)(2,1)S(1)} collective-permute-done((bf16[4,128,256]{2,1,0:T(8,128)(2,1)S(1)}, bf16[4,128,256]{2,1,0:T(8,128)(2,1)S(1)}, u32[]{:S(2)}, u32[]{:S(2)}) %collective-permute-start.9) | collective-permute-done | bytes 262176 | tf_op jit(solution)/shard_map/ppermute | solution.py:252
  101.2 0.0 collective-permute-done.10.refs_11_
  101.2 4.6 %collective-permute-done.13.refs_14_ = bf16[4,128,256]{2,1,0:T(8,128)(2,1)S(1)} collective-permute-done((bf16[4,128,256]{2,1,0:T(8,128)(2,1)S(1)}, bf16[4,128,256]{2,1,0:T(8,128)(2,1)S(1)}, u32[]{:S(2)}, u32[]{:S(2)}) %collective-permute-start.13) | collective-permute-done | bytes 262176 | tf_op jit(solution)/shard_map/ppermute | solution.py:256
  105.7 1.1 collective-permute-done.12.refs_13_
  106.8 5.7 %pairs.1 = (f32[16,64,128]{2,1,0:T(8,128)S(1)}, f32[16,64,128]{2,1,0:T(8,128)S(1)}) custom-call(bf16[8,256,256]{2,1,0:T(8,128)(2,1)S(1)} %pad_maximum_fusion.1.w_ref, bf16[8,128,256]{2,1,0:T(8,128)(2,1)S(1)} %bitcast.12, bf16[4,128,256]{2,1,0:T(8,128)(2,1)S(1)} %collective-permute-done.refs_1_, bf16[4,128,256]{2,1,0:T(8,128)(2,1)S(1)} %collective-permute-done.1.refs_2_, ...), custom_call_target="tpu_custom_call" | custom-call | flops 1073741824 | bytes 6000000 | tf_op jit(solution)/shard_map/pairs/pallas_call | solution.py:187
  112.5 0.6 collective-permute-start.14
  113.2 1.5 %collective-permute-done.14 = f32[16,64,128]{2,1,0:T(8,128)S(1)} collective-permute-done((f32[16,64,128]{2,1,0:T(8,128)S(1)}, f32[16,64,128]{2,1,0:T(8,128)S(1)}, u32[]{:S(2)}, u32[]{:S(2)}) %collective-permute-start.14) | collective-permute-done | bytes 524320 | tf_op jit(solution)/shard_map/ppermute | solution.py:281
  114.7 0.9 add.3
  115.6 0.0 all-to-all-done.1
  115.6 6.7 %all-to-all-start.4 = ((f32[16,64,128]{2,1,0:T(8,128)}), f32[16,64,128]{2,1,0:T(8,128)S(1)}, u32[]{:S(2)}, u32[]{:S(2)}) async-start(f32[16,64,128]{2,1,0:T(8,128)} %add.3), calls=%async_computation.4 | async-start | bytes 1048576 | tf_op jit(solution)/shard_map/all_to_all | solution.py:282
  122.3 9.5 %all-to-all-done.4.parts_ref = f32[16,64,128]{2,1,0:T(8,128)S(1)} async-done(((f32[16,64,128]{2,1,0:T(8,128)}), f32[16,64,128]{2,1,0:T(8,128)S(1)}, u32[]{:S(2)}, u32[]{:S(2)}) %all-to-all-start.4) | async-done | bytes 524320 | tf_op jit(solution)/shard_map/all_to_all | solution.py:282
  131.8 0.8 copy-done.3
  132.6 1.8 %finish.1 = (f32[64,64]{1,0:T(8,128)}, f32[64,64]{1,0:T(8,128)}) custom-call(f32[16,64,128]{2,1,0:T(8,128)} %copy-done.3), custom_call_target="tpu_custom_call" | custom-call | tf_op jit(solution)/shard_map/finish/pallas_call | solution.py:208
  134.4 2.3 %copy.17 = f32[64,8,512]{2,1,0:T(8,128)} copy(f32[64,8,512]{2,1,0:T(8,128)} %bitcast.1) | data formatting | bytes 2097152
  (11 shorter events, 0.1 us)
Async XLA Ops:
  2.7 28.3 %copy-start = (bf16[512,512]{1,0:T(8,128)(2,1)S(1)}, bf16[512,512]{1,0:T(8,128)(2,1)}, u32[]{:S(2)}) copy-start(bf16[512,512]{1,0:T(8,128)(2,1)} %constant.7.clone.ml_ref) | copy-start | bytes 1572868
  2.7 28.3 %copy-start.1 = (bf16[512,512]{1,0:T(8,128)(2,1)S(1)}, bf16[512,512]{1,0:T(8,128)(2,1)}, u32[]{:S(2)}) copy-start(bf16[512,512]{1,0:T(8,128)(2,1)} %constant.6.clone.mh_ref) | copy-start | bytes 1572868
  2.8 28.3 %copy-start.2 = (bf16[128,384]{1,0:T(8,128)(2,1)S(1)}, bf16[128,384]{1,0:T(8,128)(2,1)}, u32[]{:S(2)}) copy-start(bf16[128,384]{1,0:T(8,128)(2,1)} %constant.8.clone.z_ref) | copy-start | bytes 294916
  53.1 13.6 %collective-permute-start.3 = (bf16[4,128,256]{2,1,0:T(8,128)(2,1)S(1)}, bf16[4,128,256]{2,1,0:T(8,128)(2,1)S(1)}, u32[]{:S(2)}, u32[]{:S(2)}) collective-permute-start(bf16[4,128,256]{2,1,0:T(8,128)(2,1)S(1)} %get-tuple-element.17), channel_id=1, source_target_pairs={{0,112},{1,113},{2,114},{3,115},{4,116},{5,117},{6,118},{7,119},{8... | collective-permute-start | bytes 786440 | tf_op jit(solution)/shard_map/ppermute | solution.py:253
  58.8 9.3 %collective-permute-start = (bf16[4,128,256]{2,1,0:T(8,128)(2,1)S(1)}, bf16[4,128,256]{2,1,0:T(8,128)(2,1)S(1)}, u32[]{:S(2)}, u32[]{:S(2)}) collective-permute-start(bf16[4,128,256]{2,1,0:T(8,128)(2,1)S(1)} %get-tuple-element.18), channel_id=1, source_target_pairs={{0,16},{1,17},{2,18},{3,19},{4,20},{5,21},{6,22},{7,23},{8,24},{9,... | collective-permute-start | bytes 786440 | tf_op jit(solution)/shard_map/ppermute | solution.py:252
  58.8 22.2 %all-to-all-start.3 = ((bf16[32,4,8,256]{3,2,1,0:T(8,128)(2,1)}), bf16[32,4,8,256]{3,2,1,0:T(8,128)(2,1)}, u32[]{:S(2)}, u32[]{:S(2)}) async-start(bf16[32,4,8,256]{3,2,1,0:T(8,128)(2,1)} %get-tuple-element.12), calls=%async_computation.3 | async-start | bytes 1048576 | tf_op jit(solution)/shard_map/all_to_all | solution.py:261
  63.6 10.1 %collective-permute-start.1 = (bf16[4,128,256]{2,1,0:T(8,128)(2,1)S(1)}, bf16[4,128,256]{2,1,0:T(8,128)(2,1)S(1)}, u32[]{:S(2)}, u32[]{:S(2)}) collective-permute-start(bf16[4,128,256]{2,1,0:T(8,128)(2,1)S(1)} %get-tuple-element.17), channel_id=1, source_target_pairs={{0,16},{1,17},{2,18},{3,19},{4,20},{5,21},{6,22},{7,23},{8,24},{9,... | collective-permute-start | bytes 786440 | tf_op jit(solution)/shard_map/ppermute | solution.py:252
  63.7 10.0 %collective-permute-start.2 = (bf16[4,128,256]{2,1,0:T(8,128)(2,1)S(1)}, bf16[4,128,256]{2,1,0:T(8,128)(2,1)S(1)}, u32[]{:S(2)}, u32[]{:S(2)}) collective-permute-start(bf16[4,128,256]{2,1,0:T(8,128)(2,1)S(1)} %get-tuple-element.18), channel_id=1, source_target_pairs={{0,112},{1,113},{2,114},{3,115},{4,116},{5,117},{6,118},{7,119},{8... | collective-permute-start | bytes 786440 | tf_op jit(solution)/shard_map/ppermute | solution.py:253
  66.7 10.9 %collective-permute-start.7 = (bf16[4,128,256]{2,1,0:T(8,128)(2,1)S(1)}, bf16[4,128,256]{2,1,0:T(8,128)(2,1)S(1)}, u32[]{:S(2)}, u32[]{:S(2)}) collective-permute-start(bf16[4,128,256]{2,1,0:T(8,128)(2,1)S(1)} %collective-permute-done.3.refs_4_), channel_id=1, source_target_pairs={{0,112},{1,113},{2,114},{3,115},{4,116},{5,117},{6,118},{7,119},{8... | collective-permute-start | bytes 786440 | tf_op jit(solution)/shard_map/ppermute | solution.py:253
  68.1 12.9 %collective-permute-start.4 = (bf16[4,128,256]{2,1,0:T(8,128)(2,1)S(1)}, bf16[4,128,256]{2,1,0:T(8,128)(2,1)S(1)}, u32[]{:S(2)}, u32[]{:S(2)}) collective-permute-start(bf16[4,128,256]{2,1,0:T(8,128)(2,1)S(1)} %collective-permute-done.refs_1_), channel_id=1, source_target_pairs={{0,16},{1,17},{2,18},{3,19},{4,20},{5,21},{6,22},{7,23},{8,24},{9,... | collective-permute-start | bytes 786440 | tf_op jit(solution)/shard_map/ppermute | solution.py:252
  73.6 17.8 %collective-permute-start.5 = (bf16[4,128,256]{2,1,0:T(8,128)(2,1)S(1)}, bf16[4,128,256]{2,1,0:T(8,128)(2,1)S(1)}, u32[]{:S(2)}, u32[]{:S(2)}) collective-permute-start(bf16[4,128,256]{2,1,0:T(8,128)(2,1)S(1)} %collective-permute-done.1.refs_2_), channel_id=1, source_target_pairs={{0,16},{1,17},{2,18},{3,19},{4,20},{5,21},{6,22},{7,23},{8,24},{9,... | collective-permute-start | bytes 786440 | tf_op jit(solution)/shard_map/ppermute | solution.py:252
  73.6 17.9 %collective-permute-start.6 = (bf16[4,128,256]{2,1,0:T(8,128)(2,1)S(1)}, bf16[4,128,256]{2,1,0:T(8,128)(2,1)S(1)}, u32[]{:S(2)}, u32[]{:S(2)}) collective-permute-start(bf16[4,128,256]{2,1,0:T(8,128)(2,1)S(1)} %collective-permute-done.2.refs_3_), channel_id=1, source_target_pairs={{0,112},{1,113},{2,114},{3,115},{4,116},{5,117},{6,118},{7,119},{8... | collective-permute-start | bytes 786440 | tf_op jit(solution)/shard_map/ppermute | solution.py:253
  77.6 17.0 %collective-permute-start.11 = (bf16[4,128,256]{2,1,0:T(8,128)(2,1)S(1)}, bf16[4,128,256]{2,1,0:T(8,128)(2,1)S(1)}, u32[]{:S(2)}, u32[]{:S(2)}) collective-permute-start(bf16[4,128,256]{2,1,0:T(8,128)(2,1)S(1)} %collective-permute-done.7.refs_8_), channel_id=1, source_target_pairs={{0,112},{1,113},{2,114},{3,115},{4,116},{5,117},{6,118},{7,119},{8... | collective-permute-start | bytes 786440 | tf_op jit(solution)/shard_map/ppermute | solution.py:253
  81.0 15.0 %collective-permute-start.8 = (bf16[4,128,256]{2,1,0:T(8,128)(2,1)S(1)}, bf16[4,128,256]{2,1,0:T(8,128)(2,1)S(1)}, u32[]{:S(2)}, u32[]{:S(2)}) collective-permute-start(bf16[4,128,256]{2,1,0:T(8,128)(2,1)S(1)} %collective-permute-done.4.refs_5_), channel_id=1, source_target_pairs={{0,16},{1,17},{2,18},{3,19},{4,20},{5,21},{6,22},{7,23},{8,24},{9,... | collective-permute-start | bytes 786440 | tf_op jit(solution)/shard_map/ppermute | solution.py:252
  81.0 34.6 %all-to-all-start.1 = ((f32[16,4,8,512]{3,2,1,0:T(8,128)}), f32[16,4,8,512]{3,2,1,0:T(8,128)}, u32[]{:S(2)}, u32[]{:S(2)}) async-start(f32[16,4,8,512]{3,2,1,0:T(8,128)} %get-tuple-element.10), calls=%async_computation.1 | async-start | bytes 2097152 | tf_op jit(solution)/shard_map/all_to_all | solution.py:276
  91.5 9.7 %collective-permute-start.9 = (bf16[4,128,256]{2,1,0:T(8,128)(2,1)S(1)}, bf16[4,128,256]{2,1,0:T(8,128)(2,1)S(1)}, u32[]{:S(2)}, u32[]{:S(2)}) collective-permute-start(bf16[4,128,256]{2,1,0:T(8,128)(2,1)S(1)} %collective-permute-done.5.refs_6_), channel_id=1, source_target_pairs={{0,16},{1,17},{2,18},{3,19},{4,20},{5,21},{6,22},{7,23},{8,24},{9,... | collective-permute-start | bytes 786440 | tf_op jit(solution)/shard_map/ppermute | solution.py:252
  91.6 9.6 %collective-permute-start.10 = (bf16[4,128,256]{2,1,0:T(8,128)(2,1)S(1)}, bf16[4,128,256]{2,1,0:T(8,128)(2,1)S(1)}, u32[]{:S(2)}, u32[]{:S(2)}) collective-permute-start(bf16[4,128,256]{2,1,0:T(8,128)(2,1)S(1)} %collective-permute-done.6.refs_7_), channel_id=1, source_target_pairs={{0,112},{1,113},{2,114},{3,115},{4,116},{5,117},{6,118},{7,119},{8... | collective-permute-start | bytes 786440 | tf_op jit(solution)/shard_map/ppermute | solution.py:253
  94.6 11.2 %collective-permute-start.13 = (bf16[4,128,256]{2,1,0:T(8,128)(2,1)S(1)}, bf16[4,128,256]{2,1,0:T(8,128)(2,1)S(1)}, u32[]{:S(2)}, u32[]{:S(2)}) collective-permute-start(bf16[4,128,256]{2,1,0:T(8,128)(2,1)S(1)} %collective-permute-done.11.refs_12_), channel_id=1, source_target_pairs={{0,112},{1,113},{2,114},{3,115},{4,116},{5,117},{6,118},{7,119},{8... | collective-permute-start | bytes 786440 | tf_op jit(solution)/shard_map/ppermute | solution.py:256
  96.0 10.8 %collective-permute-start.12 = (bf16[4,128,256]{2,1,0:T(8,128)(2,1)S(1)}, bf16[4,128,256]{2,1,0:T(8,128)(2,1)S(1)}, u32[]{:S(2)}, u32[]{:S(2)}) collective-permute-start(bf16[4,128,256]{2,1,0:T(8,128)(2,1)S(1)} %collective-permute-done.8.refs_9_), channel_id=1, source_target_pairs={{0,16},{1,17},{2,18},{3,19},{4,20},{5,21},{6,22},{7,23},{8,24},{9,... | collective-permute-start | bytes 786440 | tf_op jit(solution)/shard_map/ppermute | solution.py:255
  112.5 2.2 %collective-permute-start.14 = (f32[16,64,128]{2,1,0:T(8,128)S(1)}, f32[16,64,128]{2,1,0:T(8,128)S(1)}, u32[]{:S(2)}, u32[]{:S(2)}) collective-permute-start(f32[16,64,128]{2,1,0:T(8,128)S(1)} %get-tuple-element.14), channel_id=1, source_target_pairs={{0,1},{1,0},{2,3},{3,2},{4,5},{5,4},{6,7},{7,6},{8,9},{9,8},{10,11... | collective-permute-start | bytes 1572872 | tf_op jit(solution)/shard_map/ppermute | solution.py:281
  115.6 16.2 %all-to-all-start.4 = ((f32[16,64,128]{2,1,0:T(8,128)}), f32[16,64,128]{2,1,0:T(8,128)S(1)}, u32[]{:S(2)}, u32[]{:S(2)}) async-start(f32[16,64,128]{2,1,0:T(8,128)} %add.3), calls=%async_computation.4 | async-start | bytes 1048576 | tf_op jit(solution)/shard_map/all_to_all | solution.py:282
  131.8 0.8 copy-start.3

commit v3 on v1

v3 whole, which is shorter than its diff:
```python
import jax
import jax.numpy as jnp
import numpy as np
from jax import lax
from jax.experimental import pallas as pl
from jax.experimental.pallas import tpu as pltpu
from jax.sharding import PartitionSpec as P

DEGREE = 4
NY = 16
NX = 32
NZ = 128
PLANE = NX * NY
NCELLS = NZ * PLANE
SLABS = 16
DEPTH = NZ // SLABS
OWN = 4
HALF = PLANE // 2
RING = 8
PEERS = 32

COEFFS = (
    -5369.0 / 1800.0,
    12.0 / 7.0,
    -15.0 / 56.0,
    10.0 / 189.0,
    -1.0 / 112.0,
    2.0 / 1925.0,
    -1.0 / 16632.0,
)
SPACING = 0.6
LOWER = -2.0
CUTOFF = 8.0
UPPER = 32.0
KINETIC = -0.5 / SPACING**2
DIAGONAL = 3.0 * COEFFS[0] * KINETIC
BF16 = jnp.bfloat16
F32 = jnp.float32
BOTH = ("band", "slab")
KERNEL_BYTES = 16 * 1024 * 1024


def line_matrix(size):
    matrix = np.zeros((size, size))
    for reach in range(1, 7):
        matrix += KINETIC * COEFFS[reach] * (np.eye(size, k=reach) + np.eye(size, k=-reach))
    return matrix


def two_terms(matrix):
    high = matrix.astype(jnp.bfloat16)
    low = (matrix - high.astype(np.float64)).astype(jnp.bfloat16)
    return high, low


def stencil_matrices():
    plane = np.kron(line_matrix(NX), np.eye(NY)) + np.kron(np.eye(NX), line_matrix(NY))
    plane_high, plane_low = two_terms(plane)
    z_high, z_low = two_terms(line_matrix(NZ))
    return plane_high, plane_low, np.concatenate([z_high, z_low, z_high], axis=1)


def schedule():
    half_width = (UPPER - CUTOFF) / 2.0
    center = (UPPER + CUTOFF) / 2.0
    sigma_first = half_width / (LOWER - center)
    sigma = sigma_first
    steps = [(sigma_first / half_width, center, 0.0)]
    for _ in range(DEGREE - 1):
        sigma_next = 1.0 / (2.0 / sigma_first - sigma)
        steps.append((2.0 * sigma_next / half_width, center, sigma * sigma_next))
        sigma = sigma_next
    return steps


def slab_rows(slab):
    return slice(slab * DEPTH, (slab + 1) * DEPTH)


def put_low(ref, orb, value):
    for slab in range(SLABS):
        for side in range(2):
            ref[side * SLABS + slab, orb] = value[slab_rows(slab), side * HALF : (side + 1) * HALF].astype(BF16)


def filter_kernel(x_ref, mh_ref, ml_ref, z_ref, out_ref, low_ref, field_a, field_b, pot, split, total):
    for slab in range(SLABS):
        for orb in range(OWN):
            field_a[orb, slab_rows(slab), :] = x_ref[slab, orb]
        pot[slab_rows(slab), :] = x_ref[slab, OWN] + DIAGONAL

    current, previous = field_a, field_b
    steps = schedule()
    for number, (scale, center, back) in enumerate(steps):
        for orb in range(OWN):
            rows = slice(orb * NZ, (orb + 1) * NZ)
            value = current[orb]
            high = value.astype(BF16)
            split[0, rows, :] = high
            split[1, rows, :] = (value - high.astype(F32)).astype(BF16)
        total[...] = (
            jnp.dot(split[0], mh_ref[...], preferred_element_type=F32)
            + jnp.dot(split[0], ml_ref[...], preferred_element_type=F32)
            + jnp.dot(split[1], mh_ref[...], preferred_element_type=F32)
        )
        for orb in range(OWN):
            rows = slice(orb * NZ, (orb + 1) * NZ)
            stack = jnp.concatenate([split[0, rows, :], split[0, rows, :], split[1, rows, :]], axis=0)
            applied = total[rows, :] + jnp.dot(z_ref[...], stack, preferred_element_type=F32)
            following = scale * (applied + (pot[...] - center) * current[orb])
            if number:
                following = following - back * previous[orb]
            previous[orb] = following
            if number == len(steps) - 1:
                put_low(low_ref, orb, following)
                for slab in range(SLABS):
                    out_ref[slab, orb] = following[slab_rows(slab), :]
        current, previous = previous, current


def apply_kernel(x_ref, f_ref, mh_ref, ml_ref, z_ref, app_ref, rest_ref, pot, split, total, rest):
    for slab in range(SLABS):
        for orb in range(OWN):
            rows = slice(orb * NZ + slab * DEPTH, orb * NZ + (slab + 1) * DEPTH)
            total[rows, :] = f_ref[slab, orb]
        pot[slab_rows(slab), :] = x_ref[slab, OWN] + DIAGONAL
    for orb in range(OWN):
        rows = slice(orb * NZ, (orb + 1) * NZ)
        value = total[rows, :]
        high = value.astype(BF16)
        split[0, rows, :] = high
        split[1, rows, :] = (value - high.astype(F32)).astype(BF16)
    total[...] = jnp.dot(split[0], mh_ref[...], preferred_element_type=F32) + jnp.dot(
        split[0], ml_ref[...], preferred_element_type=F32
    )
    rest[...] = jnp.dot(split[1], mh_ref[...], preferred_element_type=F32)
    for orb in range(OWN):
        rows = slice(orb * NZ, (orb + 1) * NZ)
        high, low = split[0, rows, :], split[1, rows, :]
        stack = jnp.concatenate([high, high], axis=0)
        of_low = total[rows, :] + pot[...] * high.astype(F32)
        of_low = of_low + jnp.dot(z_ref[:, : 2 * NZ], stack, preferred_element_type=F32)
        of_rest = rest[rows, :] + pot[...] * low.astype(F32)
        of_rest = of_rest + jnp.dot(z_ref[:, 2 * NZ :], low, preferred_element_type=F32)
        applied_low = (of_low + of_rest).astype(BF16).astype(F32)
        middle = 0.5 * (applied_low + of_low)
        middle_high = middle.astype(BF16).astype(F32)
        put_low(app_ref, orb, middle_high)
        put_low(rest_ref, orb, middle - middle_high)


def run_filter(block):
    plane_high, plane_low, z_stack = (jnp.asarray(matrix) for matrix in stencil_matrices())
    vmem = pl.BlockSpec(memory_space=pltpu.VMEM)
    params = pltpu.CompilerParams(vmem_limit_bytes=KERNEL_BYTES)
    filtered, filtered_low = pl.pallas_call(
        filter_kernel,
        out_shape=(
            jax.ShapeDtypeStruct((SLABS, OWN, DEPTH, PLANE), F32),
            jax.ShapeDtypeStruct((PEERS, OWN, DEPTH, HALF), BF16),
        ),
        in_specs=[vmem] * 4,
        out_specs=(vmem, vmem),
        scratch_shapes=[
            pltpu.VMEM((OWN, NZ, PLANE), F32),
            pltpu.VMEM((OWN, NZ, PLANE), F32),
            pltpu.VMEM((NZ, PLANE), F32),
            pltpu.VMEM((2, OWN * NZ, PLANE), BF16),
            pltpu.VMEM((OWN * NZ, PLANE), F32),
        ],
        compiler_params=params,
        cost_estimate=pl.CostEstimate(flops=5_000_000_000, bytes_accessed=6_000_000, transcendentals=0),
        name="chebyshev",
    )(block, plane_high, plane_low, z_stack)
    applied, rest = pl.pallas_call(
        apply_kernel,
        out_shape=(jax.ShapeDtypeStruct((PEERS, OWN, DEPTH, HALF), BF16),) * 2,
        in_specs=[vmem] * 5,
        out_specs=(vmem, vmem),
        scratch_shapes=[
            pltpu.VMEM((NZ, PLANE), F32),
            pltpu.VMEM((2, OWN * NZ, PLANE), BF16),
            pltpu.VMEM((OWN * NZ, PLANE), F32),
            pltpu.VMEM((OWN * NZ, PLANE), F32),
        ],
        compiler_params=params,
        cost_estimate=pl.CostEstimate(flops=1_000_000_000, bytes_accessed=6_000_000, transcendentals=0),
        name="applied",
    )(block, filtered, plane_high, plane_low, z_stack)
    return filtered, filtered_low, applied, rest


def put_pairs(total, shift, keep_ref, send_ref):
    place = lax.rem(lax.axis_index("band"), RING)
    core = lax.rem(lax.axis_index("slab"), 2)
    ring = lax.rem(place + shift + RING, RING)
    mine = lax.rem(ring, 2) == core
    for own in range(2):
        rows = total[own * 192 : (own + 1) * 192]
        gram, cross = rows[:64], rows[64:128] + rows[128:]
        for side in range(2):
            lanes = slice(side * 64, (side + 1) * 64)
            block = jnp.concatenate([gram[:, lanes], cross[:, lanes]], axis=1)
            index = own * RING + side * (RING // 2) + lax.div(ring, 2)
            keep_ref[jnp.where(mine, index, 2 * RING)] = block
            send_ref[jnp.where(mine, 2 * RING, index)] = block


def pair_sum(w_ref, pick):
    total = None
    for depth in range(DEPTH):
        part = lax.dot_general(w_ref[depth], pick(depth), (((1,), (1,)), ((), ())), preferred_element_type=F32)
        total = part if total is None else total + part
    return total


def early_kernel(w_ref, own_ref, *refs):
    blocks, (keep_ref, send_ref) = refs[:-2], refs[-2:]
    put_pairs(pair_sum(w_ref, lambda depth: own_ref[depth]), 0, keep_ref, send_ref)
    for step in range(1, RING // 2):
        ahead, behind = blocks[2 * step - 2], blocks[2 * step - 1]
        total = pair_sum(w_ref, lambda depth: jnp.concatenate([ahead[depth], behind[depth]], axis=0))
        put_pairs(total[:, :128], -step, keep_ref, send_ref)
        put_pairs(total[:, 128:], step, keep_ref, send_ref)


def late_kernel(w_ref, ahead_ref, behind_ref, filtered_ref, keep_in, send_in, keep_ref, send_ref, out_ref, done):
    copy = pltpu.make_async_copy(filtered_ref, out_ref, done)
    copy.start()
    first = lax.rem(lax.axis_index("slab"), 2) == 0
    total = pair_sum(w_ref, lambda depth: jnp.where(first, ahead_ref[depth], behind_ref[depth]))
    put_pairs(total, RING // 2, keep_ref, send_ref)
    copy.wait()


def run_early(weights, blocks):
    vmem = pl.BlockSpec(memory_space=pltpu.VMEM)
    shape = jax.ShapeDtypeStruct((2 * RING + 1, 64, 128), F32)
    return pl.pallas_call(
        early_kernel,
        out_shape=(shape, shape),
        in_specs=[vmem] * (1 + len(blocks)),
        out_specs=(vmem, vmem),
        compiler_params=pltpu.CompilerParams(vmem_limit_bytes=KERNEL_BYTES),
        cost_estimate=pl.CostEstimate(flops=1_400_000_000, bytes_accessed=6_000_000, transcendentals=0),
        name="pairs_early",
    )(weights, *blocks)


def run_late(weights, ahead, behind, filtered, keep, send):
    vmem = pl.BlockSpec(memory_space=pltpu.VMEM)
    shape = jax.ShapeDtypeStruct(keep.shape, F32)
    return pl.pallas_call(
        late_kernel,
        out_shape=(shape, shape, jax.ShapeDtypeStruct(filtered.shape, F32)),
        in_specs=[vmem] * 6,
        out_specs=(vmem, vmem, pl.BlockSpec(memory_space=pl.ANY)),
        scratch_shapes=[pltpu.SemaphoreType.DMA],
        input_output_aliases={4: 0, 5: 1},
        compiler_params=pltpu.CompilerParams(vmem_limit_bytes=KERNEL_BYTES),
        cost_estimate=pl.CostEstimate(flops=200_000_000, bytes_accessed=4_000_000, transcendentals=0),
        name="pairs_late",
    )(weights, ahead, behind, filtered, keep, send)


def plane_groups():
    return [[(side * RING + ring) * SLABS + slab for side in range(2) for slab in range(SLABS)] for ring in range(RING)]


def core_groups():
    return [
        [(side * RING + ring) * SLABS + 2 * chip + core for side in range(2) for chip in range(SLABS // 2)]
        for ring in range(RING)
        for core in range(2)
    ]


def ring_pairs(step, cores=(0, 1)):
    return [
        ((side * RING + ring) * SLABS + slab, (side * RING + (ring + step) % RING) * SLABS + slab)
        for side in range(2)
        for ring in range(RING)
        for slab in range(SLABS)
        if slab % 2 in cores
    ]


def core_pairs():
    return [(place, place ^ 1) for place in range(2 * RING * SLABS)]


def over_plane(block):
    return lax.all_to_all(block, BOTH, 0, 0, axis_index_groups=plane_groups(), tiled=True)


def by_depth(block):
    return block.reshape(PEERS * OWN, DEPTH, HALF).transpose(1, 0, 2)


def after(value, *earlier):
    return lax.optimization_barrier((value, *earlier))[0]


def on_device(orbitals, potential):
    block = orbitals.reshape(SLABS, OWN, DEPTH, PLANE)
    shared = jnp.broadcast_to(potential[None, None], (SLABS, 1, DEPTH, PLANE))
    block = lax.all_to_all(jnp.concatenate([block, shared], axis=1), "slab", 0, 0, tiled=True)
    filtered, filtered_low, applied, rest = run_filter(block)
    own_low = by_depth(over_plane(filtered_low))
    ahead = lax.ppermute(own_low, BOTH, ring_pairs(1))
    behind = lax.ppermute(own_low, BOTH, ring_pairs(-1))
    blocks = [own_low, ahead, behind]
    applied_high = by_depth(over_plane(applied))
    applied_rest = by_depth(over_plane(after(rest, ahead, behind)))
    ahead = lax.ppermute(ahead, BOTH, ring_pairs(1))
    behind = lax.ppermute(behind, BOTH, ring_pairs(-1))
    blocks += [ahead, behind]
    filtered = lax.all_to_all(after(filtered, ahead, behind), "slab", 0, 0, tiled=True)
    ahead = lax.ppermute(ahead, BOTH, ring_pairs(1))
    behind = lax.ppermute(behind, BOTH, ring_pairs(-1))
    blocks += [ahead, behind]
    last_ahead = lax.ppermute(ahead, BOTH, ring_pairs(1, (0,)))
    last_behind = lax.ppermute(behind, BOTH, ring_pairs(-1, (1,)))
    weights = jnp.concatenate(
        [part[:, own * 64 : (own + 1) * 64] for own in range(2) for part in (own_low, applied_high, applied_rest)],
        axis=1,
    )
    keep, send = run_early(weights, blocks)
    keep, send, filtered = run_late(weights, last_ahead, last_behind, filtered, keep, send)
    sums = (keep + lax.ppermute(send, BOTH, core_pairs()))[: 2 * RING]
    sums = lax.all_to_all(sums, BOTH, 0, 0, axis_index_groups=core_groups(), tiled=True)
    sums = jnp.sum(sums, axis=0) / NCELLS
    return filtered.reshape(SLABS * OWN, DEPTH, PLANE), sums[:, :64], sums[:, 64:]


def solution(mesh):
    return jax.shard_map(
        on_device,
        mesh=mesh,
        in_specs=(P("band", "slab", None), P("slab", None)),
        out_specs=(P("band", "slab", None), P("band", "slab"), P("band", "slab")),
        check_vma=False,
    )
```

time: 154 us -> 134 us (0.87)
  waiting for transfers between devices: 51.8 us -> 23.9 us
  starting transfers between devices: 11.4 us -> 28.9 us
  between operations: 14.1 us -> 0.83 us
  Pallas kernels: 9.44 us -> 13.6 us
  blocking collectives: 58.6 us -> 55.9 us
  local copies, waits for them, and re-layouts: 6.46 us -> 8.41 us
    all_gather x1 -> x0, waiting for transfers between devices: 34.7 us -> none  [on_device(): lax.all_gather(filtered_low, 'band', axis=0, axis_index_groups=ring_group...]
    ppermute x0 -> x9, starting transfers between devices: none -> 17.1 us  [the longest x2 5.35 us: on_device(): behind = lax.ppermute(behind, BOTH, ring_pairs(-1))]
    ppermute x0 -> x9, waiting for transfers between devices: none -> 10.9 us  [the longest x1 5.34 us: on_device(): ahead = lax.ppermute(own_low, BOTH, ring_pairs(1))]
    pallas_call x1 -> x3, Pallas kernels: 3.72 us -> 8.95 us  [the longest x1 3.77 us: run_early(): pl.pallas_call(early_kernel, out_shape=(shape, shape), in_specs=[vmem] *...]
    all_to_all x2 -> x3, waiting for transfers between devices: 17.1 us -> 13.1 us  [the longest x2 8.34 us: over_plane(): lax.all_to_all(block, BOTH, 0, 0, axis_index_groups=plane_groups(), tiled...]
    all_to_all x2, blocking collectives: 30.4 us -> 27.6 us  [the longest x1 15.2 us: over_plane(): lax.all_to_all(block, BOTH, 0, 0, axis_index_groups=plane_groups(), tiled...]
    unnamed x13 -> x25, local copies, waits for them, and re-layouts: 4.58 us -> 5.86 us
    all_to_all x2 -> x3, starting transfers between devices: 11.3 us -> 11.7 us  [the longest x2 7.98 us: over_plane(): lax.all_to_all(block, BOTH, 0, 0, axis_index_groups=plane_groups(), tiled...]
  transfers between devices with their start and end apart: 3 -> 12, of which waited for: 2 -> 6; matrix products, arithmetic and copies ran while one was open for 0% -> 2% of each run, Pallas kernels for 2% -> 5%
where the time goes in v3:
time: 134 us; the launch traced here: 133 us
  blocking collectives  55.9 us (42%)
  starting transfers between devices  28.9 us (22%)
  waiting for transfers between devices  23.9 us (18%)
  Pallas kernels  13.6 us (10%)
  local copies, waits for them, and re-layouts  8.41 us (6%)
  other arithmetic  1.48 us (1%)
    all_to_all x1, blocking collectives, on_device(): lax.all_to_all(jnp.concatenate([block, shared], axis=1), 'slab', 0, 0, ti...  28.3 us
    all_to_all x1, blocking collectives, over_plane(): lax.all_to_all(block, BOTH, 0, 0, axis_index_groups=plane_groups(), tiled...  15.2 us
    all_to_all x1, blocking collectives, on_device(): lax.all_to_all(sums, BOTH, 0, 0, axis_index_groups=core_groups(), tiled=T...  12.4 us
    all_to_all x2, waiting for transfers between devices, over_plane(): lax.all_to_all(block, BOTH, 0, 0, axis_index_groups=plane_groups(), tiled...  8.34 us
    all_to_all x2, starting transfers between devices, over_plane(): lax.all_to_all(block, BOTH, 0, 0, axis_index_groups=plane_groups(), tiled...  7.98 us
    unnamed x25, local copies, waits for them, and re-layouts  5.86 us
    ppermute x2, starting transfers between devices, on_device(): behind = lax.ppermute(behind, BOTH, ring_pairs(-1))  5.35 us
    ppermute x1, waiting for transfers between devices, on_device(): ahead = lax.ppermute(own_low, BOTH, ring_pairs(1))  5.34 us
  transfers between devices with their start and end apart: 12, of which 6 were waited for; matrix products, arithmetic and copies ran while one was open for 2% of the time, Pallas kernels for 5%

profile of v3, /device:TPU:1, one launch (start us, length us, event | category | flops | bytes accessed | tf_op | source)
XLA Modules:
  0.0 133.0 jit_solution(14208730491525812296)
XLA Ops:
  0.6 0.7 broadcast_in_dim.2
  1.4 1.4 %pad_maximum_fusion = f32[16,5,8,512]{3,2,1,0:T(8,128)S(1)} fusion(f32[16,1,8,512]{3,2,1,0:T(8,128)S(1)} %broadcast_in_dim.2, f32[16,4,8,512]{3,2,1,0:T(8,128)} %bitcast.26), kind=kLoop, calls=%fused_computation | loop fusion | flops 327680 | bytes 2621440 | tf_op jit(solution)/shard_map/concatenate | solution.py:307
  2.7 0.0 copy-start.5
  2.8 0.0 copy-start.6
  2.8 0.0 copy-start.7
  2.8 28.3 %all_to_all.30.x_ref = f32[16,5,8,512]{3,2,1,0:T(8,128)S(1)} all-to-all(f32[16,5,8,512]{3,2,1,0:T(8,128)S(1)} %pad_maximum_fusion), channel_id=1, replica_groups=mesh['band'=16,'slab'=16] {'slab'}, dimensions={0} | all-to-all | bytes 2621440 | tf_op jit(solution)/shard_map/all_to_all | solution.py:307
  31.1 4.6 %chebyshev.1 = (f32[16,4,8,512]{3,2,1,0:T(8,128)S(1)}, bf16[32,4,8,256]{3,2,1,0:T(8,128)(2,1)S(1)}) custom-call(f32[16,5,8,512]{3,2,1,0:T(8,128)S(1)} %all_to_all.30.x_ref, bf16[512,512]{1,0:T(8,128)(2,1)S(1)} %copy-done.5, bf16[512,512]{1,0:T(8,128)(2,1)S(1)} %copy-done.6, bf16[128,384]{1,0:T(8,128)(2,1)S(1)} %copy-done.7), custom_call_target="tpu_custom_call" | custom-call | flops 5000000000 | bytes 6000000 | tf_op jit(solution)/shard_map/chebyshev/pallas_call | solution.py:156
  35.7 0.0 copy-start.2
  35.7 15.2 %all_to_all.31 = bf16[32,4,8,256]{3,2,1,0:T(8,128)(2,1)S(1)} all-to-all(bf16[32,4,8,256]{3,2,1,0:T(8,128)(2,1)S(1)} %get-tuple-element.14), channel_id=1, replica_groups={{0,1,2,3,4,5,6,7,8,9,10,11,12,13,14,15,128,129,130,131,132,133,134,135,..., dimensions={0} | all-to-all | bytes 1048576 | tf_op jit(solution)/shard_map/all_to_all | solution.py:293
  50.9 0.1 copy.21
  51.0 1.7 %collective-permute-start = (bf16[8,128,256]{2,1,0:T(8,128)(2,1)S(1)}, bf16[8,128,256]{2,1,0:T(8,128)(2,1)}, u32[]{:S(2)}, u32[]{:S(2)}) collective-permute-start(bf16[8,128,256]{2,1,0:T(8,128)(2,1)S(1)} %bitcast.14), channel_id=1, source_target_pairs={{0,16},{1,17},{2,18},{3,19},{4,20},{5,21},{6,22},{7,23},{8,24},{9,... | collective-permute-start | bytes 1572872 | tf_op jit(solution)/shard_map/ppermute | solution.py:310
  52.7 4.0 %collective-permute-start.1 = (bf16[8,128,256]{2,1,0:T(8,128)(2,1)S(1)}, bf16[8,128,256]{2,1,0:T(8,128)(2,1)}, u32[]{:S(2)}, u32[]{:S(2)}) collective-permute-start(bf16[8,128,256]{2,1,0:T(8,128)(2,1)S(1)} %bitcast.15), channel_id=1, source_target_pairs={{0,112},{1,113},{2,114},{3,115},{4,116},{5,117},{6,118},{7,119},{8... | collective-permute-start | bytes 1572872 | tf_op jit(solution)/shard_map/ppermute | solution.py:311
  56.7 2.6 %applied.1 = (bf16[32,4,8,256]{3,2,1,0:T(8,128)(2,1)}, bf16[32,4,8,256]{3,2,1,0:T(8,128)(2,1)}) custom-call(f32[16,5,8,512]{3,2,1,0:T(8,128)S(1)} %all_to_all.30.x_ref, f32[16,4,8,512]{3,2,1,0:T(8,128)S(1)} %get-tuple-element.19.f_ref, bf16[512,512]{1,0:T(8,128)(2,1)S(1)} %copy-done.5, bf16[512,512]{1,0:T(8,128)(2,1)S(1)} %copy-done.6, ...), custom_call_target="tpu_custom_call" | custom-call | flops 1000000000 | bytes 6000000 | tf_op jit(solution)/shard_map/applied/pallas_call | solution.py:175
  59.3 4.1 %all-to-all-start.2 = ((bf16[32,4,8,256]{3,2,1,0:T(8,128)(2,1)}), bf16[32,4,8,256]{3,2,1,0:T(8,128)(2,1)S(1)}, u32[]{:S(2)}, u32[]{:S(2)}) async-start(bf16[32,4,8,256]{3,2,1,0:T(8,128)(2,1)} %get-tuple-element.16), calls=%async_computation.2 | async-start | bytes 1048576 | tf_op jit(solution)/shard_map/all_to_all | solution.py:293
  63.5 5.3 %collective-permute-done.refs_0_ = bf16[8,128,256]{2,1,0:T(8,128)(2,1)} collective-permute-done((bf16[8,128,256]{2,1,0:T(8,128)(2,1)S(1)}, bf16[8,128,256]{2,1,0:T(8,128)(2,1)}, u32[]{:S(2)}, u32[]{:S(2)}) %collective-permute-start) | collective-permute-done | bytes 524320 | tf_op jit(solution)/shard_map/ppermute | solution.py:310
  68.8 0.0 collective-permute-start.2
  68.8 0.0 collective-permute-done.1.refs_1_
  68.8 2.7 %collective-permute-start.5 = (bf16[8,128,256]{2,1,0:T(8,128)(2,1)}, bf16[8,128,256]{2,1,0:T(8,128)(2,1)}, u32[]{:S(2)}, u32[]{:S(2)}) collective-permute-start(bf16[8,128,256]{2,1,0:T(8,128)(2,1)} %collective-permute-done.1.refs_1_), channel_id=1, source_target_pairs={{0,112},{1,113},{2,114},{3,115},{4,116},{5,117},{6,118},{7,119},{8... | collective-permute-start | bytes 1572872 | tf_op jit(solution)/shard_map/ppermute | solution.py:316
  71.5 3.5 %all-to-all-done.2 = bf16[32,4,8,256]{3,2,1,0:T(8,128)(2,1)S(1)} async-done(((bf16[32,4,8,256]{3,2,1,0:T(8,128)(2,1)}), bf16[32,4,8,256]{3,2,1,0:T(8,128)(2,1)S(1)}, u32[]{:S(2)}, u32[]{:S(2)}) %all-to-all-start.2) | async-done | bytes 524320 | tf_op jit(solution)/shard_map/all_to_all | solution.py:293
  75.0 3.8 %all-to-all-start.3 = ((bf16[32,4,8,256]{3,2,1,0:T(8,128)(2,1)}), bf16[32,4,8,256]{3,2,1,0:T(8,128)(2,1)S(1)}, u32[]{:S(2)}, u32[]{:S(2)}) async-start(bf16[32,4,8,256]{3,2,1,0:T(8,128)(2,1)} %get-tuple-element.18), calls=%async_computation.3 | async-start | bytes 1048576 | tf_op jit(solution)/shard_map/all_to_all | solution.py:293
  78.9 0.1 copy.20
  79.0 3.9 %collective-permute-done.2.refs_2_ = bf16[8,128,256]{2,1,0:T(8,128)(2,1)} collective-permute-done((bf16[8,128,256]{2,1,0:T(8,128)(2,1)}, bf16[8,128,256]{2,1,0:T(8,128)(2,1)}, u32[]{:S(2)}, u32[]{:S(2)}) %collective-permute-start.2) | collective-permute-done | bytes 524320 | tf_op jit(solution)/shard_map/ppermute | solution.py:315
  83.0 0.0 collective-permute-start.3
  83.0 0.0 collective-permute-done.5.refs_3_
  83.0 2.7 %collective-permute-start.6 = (bf16[8,128,256]{2,1,0:T(8,128)(2,1)}, bf16[8,128,256]{2,1,0:T(8,128)(2,1)}, u32[]{:S(2)}, u32[]{:S(2)}) collective-permute-start(bf16[8,128,256]{2,1,0:T(8,128)(2,1)} %collective-permute-done.5.refs_3_), channel_id=1, source_target_pairs={{0,112},{1,113},{2,114},{3,115},{4,116},{5,117},{6,118},{7,119},{8... | collective-permute-start | bytes 1572872 | tf_op jit(solution)/shard_map/ppermute | solution.py:320
  85.7 4.8 %all-to-all-done.3 = bf16[32,4,8,256]{3,2,1,0:T(8,128)(2,1)S(1)} async-done(((bf16[32,4,8,256]{3,2,1,0:T(8,128)(2,1)}), bf16[32,4,8,256]{3,2,1,0:T(8,128)(2,1)S(1)}, u32[]{:S(2)}, u32[]{:S(2)}) %all-to-all-start.3) | async-done | bytes 524320 | tf_op jit(solution)/shard_map/all_to_all | solution.py:293
  90.5 0.9 copy.19
  91.4 3.8 %all-to-all-start.4 = ((f32[16,4,8,512]{3,2,1,0:T(8,128)}), f32[16,4,8,512]{3,2,1,0:T(8,128)S(1)}, u32[]{:S(2)}, u32[]{:S(2)}) async-start(f32[16,4,8,512]{3,2,1,0:T(8,128)} %copy-done.2), calls=%async_computation.4 | async-start | bytes 2097152 | tf_op jit(solution)/shard_map/all_to_all | solution.py:318
  95.1 1.0 slice_dynamic-update-slice_fusion.3
  96.2 0.0 collective-permute-done.3.refs_4_
  96.2 1.5 %collective-permute-start.4 = (bf16[8,128,256]{2,1,0:T(8,128)(2,1)}, bf16[8,128,256]{2,1,0:T(8,128)(2,1)}, u32[]{:S(2)}, u32[]{:S(2)}) collective-permute-start(bf16[8,128,256]{2,1,0:T(8,128)(2,1)} %collective-permute-done.3.refs_4_), channel_id=1, source_target_pairs={{0,16},{2,18},{4,20},{6,22},{8,24},{10,26},{12,28},{14,30},{16,32}... | collective-permute-start | bytes 1572872 | tf_op jit(solution)/shard_map/ppermute | solution.py:322
  97.7 0.0 collective-permute-done.6.refs_5_
  97.7 3.6 %collective-permute-start.7 = (bf16[8,128,256]{2,1,0:T(8,128)(2,1)}, bf16[8,128,256]{2,1,0:T(8,128)(2,1)}, u32[]{:S(2)}, u32[]{:S(2)}) collective-permute-start(bf16[8,128,256]{2,1,0:T(8,128)(2,1)} %collective-permute-done.6.refs_5_), channel_id=1, source_target_pairs={{1,113},{3,115},{5,117},{7,119},{9,121},{11,123},{13,125},{15,127}... | collective-permute-start | bytes 1572872 | tf_op jit(solution)/shard_map/ppermute | solution.py:323
  101.2 1.0 slice_dynamic-update-slice_fusion.1
  102.3 3.8 %pairs_early.1 = (f32[17,64,128]{2,1,0:T(8,128)S(1)}, f32[17,64,128]{2,1,0:T(8,128)S(1)}) custom-call(bf16[8,384,256]{2,1,0:T(8,128)(2,1)S(1)} %slice_dynamic-update-slice_fusion.w_ref, bf16[8,128,256]{2,1,0:T(8,128)(2,1)S(1)} %bitcast.18, bf16[8,128,256]{2,1,0:T(8,128)(2,1)} %collective-permute-done.refs_0_, ...), custom_call_target="tpu_custom_call" | custom-call | flops 1400000000 | bytes 6000000 | tf_op jit(solution)/shard_map/pairs_early/pallas_call | solution.py:239
  106.0 0.8 copy-done
  106.9 0.8 copy-done.3
  107.7 4.7 %all-to-all-done.4.filtered_ref = f32[16,4,8,512]{3,2,1,0:T(8,128)S(1)} async-done(((f32[16,4,8,512]{3,2,1,0:T(8,128)}), f32[16,4,8,512]{3,2,1,0:T(8,128)S(1)}, u32[]{:S(2)}, u32[]{:S(2)}) %all-to-all-start.4) | async-done | bytes 1048608 | tf_op jit(solution)/shard_map/all_to_all | solution.py:318
  112.4 0.0 collective-permute-done.4.ahead_ref
  112.4 0.0 collective-permute-done.7.behind_ref
  112.4 1.1 copy-done.1
  113.5 1.1 copy-done.4
  114.5 2.6 %pairs_late.1 = (f32[17,64,128]{2,1,0:T(8,128)S(1)}, f32[17,64,128]{2,1,0:T(8,128)S(1)}, f32[16,4,8,512]{3,2,1,0:T(8,128)}) custom-call(bf16[8,384,256]{2,1,0:T(8,128)(2,1)S(1)} %slice_dynamic-update-slice_fusion.w_ref, bf16[8,128,256]{2,1,0:T(8,128)(2,1)} %collective-permute-done.4.ahead_ref, ...), custom_call_target="tpu_custom_call", output_to_operand_aliasing={{0}: (4, {}), {1}: (5, {})} | custom-call | flops 200000000 | bytes 4000000 | tf_op jit(solution)/shard_map/pairs_late/pallas_call | solution.py:253
  117.1 1.0 collective-permute-start.8
  118.1 1.6 %collective-permute-done.8 = f32[17,64,128]{2,1,0:T(8,128)S(1)} collective-permute-done((f32[17,64,128]{2,1,0:T(8,128)S(1)}, f32[17,64,128]{2,1,0:T(8,128)S(1)}, u32[]{:S(2)}, u32[]{:S(2)}) %collective-permute-start.8) | collective-permute-done | bytes 557088 | tf_op jit(solution)/shard_map/ppermute | solution.py:330
  119.7 0.1 slice_add_fusion
  119.8 12.4 %all_to_all.32 = f32[16,64,128]{2,1,0:T(8,128)S(1)} all-to-all(f32[16,64,128]{2,1,0:T(8,128)S(1)} %slice_add_fusion), channel_id=1, replica_groups={{0,2,4,6,8,10,12,14,128,130,132,134,136,138,140,142},{1,3,5,7,9,11,13,1..., dimensions={0} | all-to-all | bytes 1048576 | tf_op jit(solution)/shard_map/all_to_all | solution.py:331
  132.3 0.7 fusion
  (18 shorter events, 0.1 us)
Async XLA Ops:
  2.7 28.3 %copy-start.5 = (bf16[512,512]{1,0:T(8,128)(2,1)S(1)}, bf16[512,512]{1,0:T(8,128)(2,1)}, u32[]{:S(2)}) copy-start(bf16[512,512]{1,0:T(8,128)(2,1)} %constant.11.clone.mh_ref) | copy-start | bytes 1572868
  2.8 28.3 %copy-start.6 = (bf16[512,512]{1,0:T(8,128)(2,1)S(1)}, bf16[512,512]{1,0:T(8,128)(2,1)}, u32[]{:S(2)}) copy-start(bf16[512,512]{1,0:T(8,128)(2,1)} %constant.12.clone.ml_ref) | copy-start | bytes 1572868
  2.8 28.3 %copy-start.7 = (bf16[128,384]{1,0:T(8,128)(2,1)S(1)}, bf16[128,384]{1,0:T(8,128)(2,1)}, u32[]{:S(2)}) copy-start(bf16[128,384]{1,0:T(8,128)(2,1)} %constant.13.clone.z_ref) | copy-start | bytes 294916
  35.7 23.7 %copy-start.2 = (f32[16,4,8,512]{3,2,1,0:T(8,128)}, f32[16,4,8,512]{3,2,1,0:T(8,128)S(1)}, u32[]{:S(2)}) copy-start(f32[16,4,8,512]{3,2,1,0:T(8,128)S(1)} %get-tuple-element.19.f_ref) | copy-start | bytes 3145732
  51.0 17.8 %collective-permute-start = (bf16[8,128,256]{2,1,0:T(8,128)(2,1)S(1)}, bf16[8,128,256]{2,1,0:T(8,128)(2,1)}, u32[]{:S(2)}, u32[]{:S(2)}) collective-permute-start(bf16[8,128,256]{2,1,0:T(8,128)(2,1)S(1)} %bitcast.14), channel_id=1, source_target_pairs={{0,16},{1,17},{2,18},{3,19},{4,20},{5,21},{6,22},{7,23},{8,24},{9,... | collective-permute-start | bytes 1572872 | tf_op jit(solution)/shard_map/ppermute | solution.py:310
  52.7 16.1 %collective-permute-start.1 = (bf16[8,128,256]{2,1,0:T(8,128)(2,1)S(1)}, bf16[8,128,256]{2,1,0:T(8,128)(2,1)}, u32[]{:S(2)}, u32[]{:S(2)}) collective-permute-start(bf16[8,128,256]{2,1,0:T(8,128)(2,1)S(1)} %bitcast.15), channel_id=1, source_target_pairs={{0,112},{1,113},{2,114},{3,115},{4,116},{5,117},{6,118},{7,119},{8... | collective-permute-start | bytes 1572872 | tf_op jit(solution)/shard_map/ppermute | solution.py:311
  59.3 15.7 %all-to-all-start.2 = ((bf16[32,4,8,256]{3,2,1,0:T(8,128)(2,1)}), bf16[32,4,8,256]{3,2,1,0:T(8,128)(2,1)S(1)}, u32[]{:S(2)}, u32[]{:S(2)}) async-start(bf16[32,4,8,256]{3,2,1,0:T(8,128)(2,1)} %get-tuple-element.16), calls=%async_computation.2 | async-start | bytes 1048576 | tf_op jit(solution)/shard_map/all_to_all | solution.py:293
  68.8 14.2 %collective-permute-start.2 = (bf16[8,128,256]{2,1,0:T(8,128)(2,1)}, bf16[8,128,256]{2,1,0:T(8,128)(2,1)}, u32[]{:S(2)}, u32[]{:S(2)}) collective-permute-start(bf16[8,128,256]{2,1,0:T(8,128)(2,1)} %collective-permute-done.refs_0_), channel_id=1, source_target_pairs={{0,16},{1,17},{2,18},{3,19},{4,20},{5,21},{6,22},{7,23},{8,24},{9,... | collective-permute-start | bytes 1572872 | tf_op jit(solution)/shard_map/ppermute | solution.py:315
  68.8 14.2 %collective-permute-start.5 = (bf16[8,128,256]{2,1,0:T(8,128)(2,1)}, bf16[8,128,256]{2,1,0:T(8,128)(2,1)}, u32[]{:S(2)}, u32[]{:S(2)}) collective-permute-start(bf16[8,128,256]{2,1,0:T(8,128)(2,1)} %collective-permute-done.1.refs_1_), channel_id=1, source_target_pairs={{0,112},{1,113},{2,114},{3,115},{4,116},{5,117},{6,118},{7,119},{8... | collective-permute-start | bytes 1572872 | tf_op jit(solution)/shard_map/ppermute | solution.py:316
  75.0 15.4 %all-to-all-start.3 = ((bf16[32,4,8,256]{3,2,1,0:T(8,128)(2,1)}), bf16[32,4,8,256]{3,2,1,0:T(8,128)(2,1)S(1)}, u32[]{:S(2)}, u32[]{:S(2)}) async-start(bf16[32,4,8,256]{3,2,1,0:T(8,128)(2,1)} %get-tuple-element.18), calls=%async_computation.3 | async-start | bytes 1048576 | tf_op jit(solution)/shard_map/all_to_all | solution.py:293
  79.0 6.6 %copy-start.8 = (bf16[128,8,256]{2,0,1:T(8,128)(2,1)}, bf16[128,8,256]{2,0,1:T(8,128)(2,1)S(1)}, u32[]{:S(2)}) copy-start(bf16[128,8,256]{2,0,1:T(8,128)(2,1)S(1)} %copy.20) | copy-start | bytes 1572868
  83.0 13.2 %collective-permute-start.3 = (bf16[8,128,256]{2,1,0:T(8,128)(2,1)}, bf16[8,128,256]{2,1,0:T(8,128)(2,1)}, u32[]{:S(2)}, u32[]{:S(2)}) collective-permute-start(bf16[8,128,256]{2,1,0:T(8,128)(2,1)} %collective-permute-done.2.refs_2_), channel_id=1, source_target_pairs={{0,16},{1,17},{2,18},{3,19},{4,20},{5,21},{6,22},{7,23},{8,24},{9,... | collective-permute-start | bytes 1572872 | tf_op jit(solution)/shard_map/ppermute | solution.py:319
  83.0 14.7 %collective-permute-start.6 = (bf16[8,128,256]{2,1,0:T(8,128)(2,1)}, bf16[8,128,256]{2,1,0:T(8,128)(2,1)}, u32[]{:S(2)}, u32[]{:S(2)}) collective-permute-start(bf16[8,128,256]{2,1,0:T(8,128)(2,1)} %collective-permute-done.5.refs_3_), channel_id=1, source_target_pairs={{0,112},{1,113},{2,114},{3,115},{4,116},{5,117},{6,118},{7,119},{8... | collective-permute-start | bytes 1572872 | tf_op jit(solution)/shard_map/ppermute | solution.py:320
  91.4 21.0 %all-to-all-start.4 = ((f32[16,4,8,512]{3,2,1,0:T(8,128)}), f32[16,4,8,512]{3,2,1,0:T(8,128)S(1)}, u32[]{:S(2)}, u32[]{:S(2)}) async-start(f32[16,4,8,512]{3,2,1,0:T(8,128)} %copy-done.2), calls=%async_computation.4 | async-start | bytes 2097152 | tf_op jit(solution)/shard_map/all_to_all | solution.py:318
  95.1 7.1 %copy-start.9 = (bf16[128,8,256]{2,0,1:T(8,128)(2,1)S(1)}, bf16[128,8,256]{2,0,1:T(8,128)(2,1)}, u32[]{:S(2)}) copy-start(bf16[128,8,256]{2,0,1:T(8,128)(2,1)} %copy.19) | copy-start | bytes 1572868
  96.2 16.2 %collective-permute-start.4 = (bf16[8,128,256]{2,1,0:T(8,128)(2,1)}, bf16[8,128,256]{2,1,0:T(8,128)(2,1)}, u32[]{:S(2)}, u32[]{:S(2)}) collective-permute-start(bf16[8,128,256]{2,1,0:T(8,128)(2,1)} %collective-permute-done.3.refs_4_), channel_id=1, source_target_pairs={{0,16},{2,18},{4,20},{6,22},{8,24},{10,26},{12,28},{14,30},{16,32}... | collective-permute-start | bytes 1572872 | tf_op jit(solution)/shard_map/ppermute | solution.py:322
  97.7 14.7 %collective-permute-start.7 = (bf16[8,128,256]{2,1,0:T(8,128)(2,1)}, bf16[8,128,256]{2,1,0:T(8,128)(2,1)}, u32[]{:S(2)}, u32[]{:S(2)}) collective-permute-start(bf16[8,128,256]{2,1,0:T(8,128)(2,1)} %collective-permute-done.6.refs_5_), channel_id=1, source_target_pairs={{1,113},{3,115},{5,117},{7,119},{9,121},{11,123},{13,125},{15,127}... | collective-permute-start | bytes 1572872 | tf_op jit(solution)/shard_map/ppermute | solution.py:323
  106.0 0.8 copy-start
  106.9 0.8 copy-start.3
  112.4 1.1 copy-start.1
  113.5 1.1 copy-start.4
  117.1 2.6 %collective-permute-start.8 = (f32[17,64,128]{2,1,0:T(8,128)S(1)}, f32[17,64,128]{2,1,0:T(8,128)S(1)}, u32[]{:S(2)}, u32[]{:S(2)}) collective-permute-start(f32[17,64,128]{2,1,0:T(8,128)S(1)} %get-tuple-element.24), channel_id=1, source_target_pairs={{0,1},{1,0},{2,3},{3,2},{4,5},{5,4},{6,7},{7,6},{8,9},{9,8},{10,11... | collective-permute-start | bytes 1671176 | tf_op jit(solution)/shard_map/ppermute | solution.py:330

commit v4 on v3

--- a/solution.py
+++ b/solution.py
@@ -147,6 +147,7 @@
         middle_high = middle.astype(BF16).astype(F32)
         put_low(app_ref, orb, middle_high)
         put_low(rest_ref, orb, middle - middle_high)
+        put_low(rest_ref, OWN + orb, low.astype(F32))
 
 
 def run_filter(block):
@@ -174,7 +175,10 @@
     )(block, plane_high, plane_low, z_stack)
     applied, rest = pl.pallas_call(
         apply_kernel,
-        out_shape=(jax.ShapeDtypeStruct((PEERS, OWN, DEPTH, HALF), BF16),) * 2,
+        out_shape=(
+            jax.ShapeDtypeStruct((PEERS, OWN, DEPTH, HALF), BF16),
+            jax.ShapeDtypeStruct((PEERS, 2 * OWN, DEPTH, HALF), BF16),
+        ),
         in_specs=[vmem] * 5,
         out_specs=(vmem, vmem),
         scratch_shapes=[
@@ -187,7 +191,7 @@
         cost_estimate=pl.CostEstimate(flops=1_000_000_000, bytes_accessed=6_000_000, transcendentals=0),
         name="applied",
     )(block, filtered, plane_high, plane_low, z_stack)
-    return filtered, filtered_low, applied, rest
+    return filtered_low, applied, rest
 
 
 def put_pairs(total, shift, keep_ref, send_ref):
@@ -214,8 +218,12 @@
     return total
 
 
-def early_kernel(w_ref, own_ref, *refs):
-    blocks, (keep_ref, send_ref) = refs[:-2], refs[-2:]
+def early_kernel(own_ref, high_ref, rest_ref, *refs):
+    blocks, (w_ref, keep_ref, send_ref) = refs[:-3], refs[-3:]
+    for side in range(2):
+        for place, ref in enumerate((own_ref, high_ref, rest_ref)):
+            start = side * 192 + place * 64
+            w_ref[:, start : start + 64, :] = ref[:, side * 64 : (side + 1) * 64, :]
     put_pairs(pair_sum(w_ref, lambda depth: own_ref[depth]), 0, keep_ref, send_ref)
     for step in range(1, RING // 2):
         ahead, behind = blocks[2 * step - 2], blocks[2 * step - 1]
@@ -224,43 +232,84 @@
         put_pairs(total[:, 128:], step, keep_ref, send_ref)
 
 
-def late_kernel(w_ref, ahead_ref, behind_ref, filtered_ref, keep_in, send_in, keep_ref, send_ref, out_ref, done):
-    copy = pltpu.make_async_copy(filtered_ref, out_ref, done)
-    copy.start()
-    first = lax.rem(lax.axis_index("slab"), 2) == 0
-    total = pair_sum(w_ref, lambda depth: jnp.where(first, ahead_ref[depth], behind_ref[depth]))
-    put_pairs(total, RING // 2, keep_ref, send_ref)
-    copy.wait()
-
-
-def run_early(weights, blocks):
+def late_kernel(w_ref, last_ref, keep_in, send_in, keep_ref, send_ref):
+    put_pairs(pair_sum(w_ref, lambda depth: last_ref[depth]), RING // 2, keep_ref, send_ref)
+
+
+def run_early(own_low, high, rest, blocks):
     vmem = pl.BlockSpec(memory_space=pltpu.VMEM)
     shape = jax.ShapeDtypeStruct((2 * RING + 1, 64, 128), F32)
     return pl.pallas_call(
         early_kernel,
-        out_shape=(shape, shape),
-        in_specs=[vmem] * (1 + len(blocks)),
-        out_specs=(vmem, vmem),
+        out_shape=(jax.ShapeDtypeStruct((DEPTH, 6 * 64, HALF), BF16), shape, shape),
+        in_specs=[vmem] * (3 + len(blocks)),
+        out_specs=(vmem, vmem, vmem),
         compiler_params=pltpu.CompilerParams(vmem_limit_bytes=KERNEL_BYTES),
         cost_estimate=pl.CostEstimate(flops=1_400_000_000, bytes_accessed=6_000_000, transcendentals=0),
         name="pairs_early",
-    )(weights, *blocks)
-
-
-def run_late(weights, ahead, behind, filtered, keep, send):
+    )(own_low, high, rest, *blocks)
+
+
+def run_late(weights, last, keep, send):
     vmem = pl.BlockSpec(memory_space=pltpu.VMEM)
     shape = jax.ShapeDtypeStruct(keep.shape, F32)
     return pl.pallas_call(
         late_kernel,
-        out_shape=(shape, shape, jax.ShapeDtypeStruct(filtered.shape, F32)),
-        in_specs=[vmem] * 6,
-        out_specs=(vmem, vmem, pl.BlockSpec(memory_space=pl.ANY)),
-        scratch_shapes=[pltpu.SemaphoreType.DMA],
-        input_output_aliases={4: 0, 5: 1},
+        out_shape=(shape, shape),
+        in_specs=[vmem] * 4,
+        out_specs=(vmem, vmem),
+        input_output_aliases={2: 0, 3: 1},
         compiler_params=pltpu.CompilerParams(vmem_limit_bytes=KERNEL_BYTES),
-        cost_estimate=pl.CostEstimate(flops=200_000_000, bytes_accessed=4_000_000, transcendentals=0),
+        cost_estimate=pl.CostEstimate(flops=200_000_000, bytes_accessed=2_000_000, transcendentals=0),
         name="pairs_late",
-    )(weights, ahead, behind, filtered, keep, send)
+    )(weights, last, keep, send)
+
+
+def join_kernel(high_ref, rest_ref, near_ref, far_ref):
+    side = lax.div(lax.axis_index("band"), RING)
+    for ref, which in ((near_ref, side), (far_ref, 1 - side)):
+        sources = pl.ds(which * SLABS, SLABS)
+        ref[...] = high_ref[sources].astype(F32) + rest_ref[sources, OWN:].astype(F32)
+
+
+def run_join(high, rest):
+    vmem = pl.BlockSpec(memory_space=pltpu.VMEM)
+    shape = jax.ShapeDtypeStruct((SLABS, OWN, DEPTH, HALF), F32)
+    return pl.pallas_call(
+        join_kernel,
+        out_shape=(shape, shape),
+        in_specs=[vmem, vmem],
+        out_specs=(vmem, vmem),
+        compiler_params=pltpu.CompilerParams(vmem_limit_bytes=KERNEL_BYTES),
+        cost_estimate=pl.CostEstimate(flops=1_000_000, bytes_accessed=2_000_000, transcendentals=0),
+        name="join",
+    )(high, rest)
+
+
+def place_kernel(near_ref, far_ref, out_ref, done):
+    side = lax.div(lax.axis_index("band"), RING)
+    copies = []
+    for number, (ref, which) in enumerate(((near_ref, side), (far_ref, 1 - side))):
+        lanes = pl.ds(pl.multiple_of(which * HALF, HALF), HALF)
+        copies.append(pltpu.make_async_copy(ref, out_ref.at[:, :, :, lanes], done.at[number]))
+    for copy in copies:
+        copy.start()
+    for copy in copies:
+        copy.wait()
+
+
+def run_place(near, far):
+    vmem = pl.BlockSpec(memory_space=pltpu.VMEM)
+    return pl.pallas_call(
+        place_kernel,
+        out_shape=jax.ShapeDtypeStruct((SLABS, OWN, DEPTH, PLANE), F32),
+        in_specs=[vmem, vmem],
+        out_specs=pl.BlockSpec(memory_space=pl.ANY),
+        scratch_shapes=[pltpu.SemaphoreType.DMA((2,))],
+        compiler_params=pltpu.CompilerParams(vmem_limit_bytes=KERNEL_BYTES),
+        cost_estimate=pl.CostEstimate(flops=0, bytes_accessed=2_000_000, transcendentals=0),
+        name="place",
+    )(near, far)
 
 
 def plane_groups():
@@ -275,14 +324,18 @@
     ]
 
 
-def ring_pairs(step, cores=(0, 1)):
-    return [
-        ((side * RING + ring) * SLABS + slab, (side * RING + (ring + step) % RING) * SLABS + slab)
-        for side in range(2)
-        for ring in range(RING)
-        for slab in range(SLABS)
-        if slab % 2 in cores
-    ]
+def ring_pairs(even, odd):
+    pairs = []
+    for side in range(2):
+        for ring in range(RING):
+            for slab in range(SLABS):
+                step = odd if slab % 2 else even
+                pairs.append(((side * RING + ring) * SLABS + slab, (side * RING + (ring + step) % RING) * SLABS + slab))
+    return pairs
+
+
+def side_pairs():
+    return [(place, place ^ (RING * SLABS)) for place in range(2 * RING * SLABS)]
 
 
 def core_pairs():
@@ -305,28 +358,31 @@
     block = orbitals.reshape(SLABS, OWN, DEPTH, PLANE)
     shared = jnp.broadcast_to(potential[None, None], (SLABS, 1, DEPTH, PLANE))
     block = lax.all_to_all(jnp.concatenate([block, shared], axis=1), "slab", 0, 0, tiled=True)
-    filtered, filtered_low, applied, rest = run_filter(block)
-    own_low = by_depth(over_plane(filtered_low))
-    ahead = lax.ppermute(own_low, BOTH, ring_pairs(1))
-    behind = lax.ppermute(own_low, BOTH, ring_pairs(-1))
-    blocks = [own_low, ahead, behind]
-    applied_high = by_depth(over_plane(applied))
-    applied_rest = by_depth(over_plane(after(rest, ahead, behind)))
-    ahead = lax.ppermute(ahead, BOTH, ring_pairs(1))
-    behind = lax.ppermute(behind, BOTH, ring_pairs(-1))
+    filtered_low, applied, rest = run_filter(block)
+    filtered_low = over_plane(filtered_low)
+    own_low = by_depth(filtered_low)
+    ahead = lax.ppermute(own_low, BOTH, ring_pairs(1, 1))
+    behind = lax.ppermute(own_low, BOTH, ring_pairs(-1, -1))
+    blocks = [ahead, behind]
+    high = over_plane(applied)
+    ahead, behind, applied = lax.optimization_barrier((ahead, behind, applied))
+    ahead = lax.ppermute(ahead, BOTH, ring_pairs(1, 1))
+    behind = lax.ppermute(behind, BOTH, ring_pairs(-1, -1))
     blocks += [ahead, behind]
-    filtered = lax.all_to_all(after(filtered, ahead, behind), "slab", 0, 0, tiled=True)
-    ahead = lax.ppermute(ahead, BOTH, ring_pairs(1))
-    behind = lax.ppermute(behind, BOTH, ring_pairs(-1))
+    ahead, behind, high = lax.optimization_barrier((ahead, behind, high))
+    rest = over_plane(rest)
+    ahead = lax.ppermute(ahead, BOTH, ring_pairs(1, 1))
+    behind = lax.ppermute(behind, BOTH, ring_pairs(-1, -1))
     blocks += [ahead, behind]
-    last_ahead = lax.ppermute(ahead, BOTH, ring_pairs(1, (0,)))
-    last_behind = lax.ppermute(behind, BOTH, ring_pairs(-1, (1,)))
-    weights = jnp.concatenate(
-        [part[:, own * 64 : (own + 1) * 64] for own in range(2) for part in (own_low, applied_high, applied_rest)],
-        axis=1,
-    )
-    keep, send = run_early(weights, blocks)
-    keep, send, filtered = run_late(weights, last_ahead, last_behind, filtered, keep, send)
+    ahead, behind, rest = lax.optimization_barrier((ahead, behind, rest))
+    last = jnp.where(lax.axis_index("slab") % 2 == 0, ahead, behind)
+    last = lax.ppermute(last, BOTH, ring_pairs(1, -1))
+    weights, keep, send = run_early(own_low, by_depth(high), by_depth(rest[:, :OWN]), blocks)
+    near, far = run_join(filtered_low, rest)
+    far = lax.ppermute(far, BOTH, side_pairs())
+    filtered = run_place(near, far)
+    last, filtered = lax.optimization_barrier((last, filtered))
+    keep, send = run_late(weights, last, keep, send)
     sums = (keep + lax.ppermute(send, BOTH, core_pairs()))[: 2 * RING]
     sums = lax.all_to_all(sums, BOTH, 0, 0, axis_index_groups=core_groups(), tiled=True)
     sums = jnp.sum(sums, axis=0) / NCELLS

time: 134 us -> 129 us (0.963)
  local copies, waits for them, and re-layouts: 8.41 us -> 3.62 us
  waiting for transfers between devices: 23.9 us -> 28 us
  starting transfers between devices: 28.9 us -> 26.2 us
  Pallas kernels: 13.6 us -> 12.2 us
    ppermute x8, waiting for transfers between devices: 9.29 us -> 14.5 us  [the longest x2 4.2 us: on_device(): ahead = lax.ppermute(ahead, BOTH, ring_pairs(1, 1))]
    all_to_all x1 -> x0, waiting for transfers between devices: 4.72 us -> none  [on_device(): lax.all_to_all(after(filtered, ahead, behind), 'slab', 0, 0, tiled=True)]
    unnamed x25 -> x18, local copies, waits for them, and re-layouts: 5.86 us -> 1.85 us
    all_to_all x1 -> x0, starting transfers between devices: 3.75 us -> none  [on_device(): lax.all_to_all(after(filtered, ahead, behind), 'slab', 0, 0, tiled=True)]
    all_to_all x2, waiting for transfers between devices: 8.34 us -> 11.9 us  [over_plane(): lax.all_to_all(block, BOTH, 0, 0, axis_index_groups=plane_groups(), tiled...]
    ppermute x1, starting transfers between devices: 1 us -> 3.84 us  [on_device(): sums = (keep + lax.ppermute(send, BOTH, core_pairs()))[:2 * RING]]
    ppermute x8, starting transfers between devices: 16.1 us -> 14.3 us  [the longest x1 5.65 us: on_device(): behind = lax.ppermute(own_low, BOTH, ring_pairs(-1, -1))]
    pallas_call x2 -> x4, Pallas kernels: 6.35 us -> 4.87 us  [the longest x1 3.14 us: run_early(): pl.pallas_call(early_kernel, out_shape=(jax.ShapeDtypeStruct((DEPTH, 6 *...]
  transfers between devices with their start and end apart: 12 -> 11, of which waited for: 6 -> 7; matrix products, arithmetic and copies ran while one was open for 2% -> 0% of each run, Pallas kernels for 5% -> 5%
where the time goes in v4:
time: 129 us; the launch traced here: 128 us
  blocking collectives  55.7 us (43%)
  waiting for transfers between devices  28 us (22%)
  starting transfers between devices  26.2 us (20%)
  Pallas kernels  12.2 us (9%)
  local copies, waits for them, and re-layouts  3.62 us (3%)
  other arithmetic  1.53 us (1%)
    all_to_all x1, blocking collectives, on_device(): lax.all_to_all(jnp.concatenate([block, shared], axis=1), 'slab', 0, 0, ti...  28.3 us
    all_to_all x1, blocking collectives, over_plane(): lax.all_to_all(block, BOTH, 0, 0, axis_index_groups=plane_groups(), tiled...  15.2 us
    all_to_all x1, blocking collectives, on_device(): lax.all_to_all(sums, BOTH, 0, 0, axis_index_groups=core_groups(), tiled=T...  12.2 us
    all_to_all x2, waiting for transfers between devices, over_plane(): lax.all_to_all(block, BOTH, 0, 0, axis_index_groups=plane_groups(), tiled...  11.9 us
    all_to_all x2, starting transfers between devices, over_plane(): lax.all_to_all(block, BOTH, 0, 0, axis_index_groups=plane_groups(), tiled...  8.08 us
    ppermute x1, starting transfers between devices, on_device(): behind = lax.ppermute(own_low, BOTH, ring_pairs(-1, -1))  5.65 us
    ppermute x2, starting transfers between devices, on_device(): behind = lax.ppermute(behind, BOTH, ring_pairs(-1, -1))  5.34 us
    pallas_call x1, Pallas kernels, run_filter(): pl.pallas_call(filter_kernel, out_shape=(jax.ShapeDtypeStruct((SLABS, OWN...  4.61 us
  transfers between devices with their start and end apart: 11, of which 7 were waited for; matrix products, arithmetic and copies ran while one was open for 0% of the time, Pallas kernels for 5%

profile of v4, /device:TPU:1, one launch (start us, length us, event | category | flops | bytes accessed | tf_op | source)
XLA Modules:
  0.0 128.1 jit_solution(14792152382919101611)
XLA Ops:
  0.6 0.7 broadcast_in_dim.2
  1.4 1.4 %pad_maximum_fusion = f32[16,5,8,512]{3,2,1,0:T(8,128)S(1)} fusion(f32[16,1,8,512]{3,2,1,0:T(8,128)S(1)} %broadcast_in_dim.2, f32[16,4,8,512]{3,2,1,0:T(8,128)} %bitcast.22), kind=kLoop, calls=%fused_computation | loop fusion | flops 327680 | bytes 2621440 | tf_op jit(solution)/shard_map/concatenate | solution.py:360
  2.7 0.0 copy-start.4
  2.7 0.0 copy-start.5
  2.8 0.0 copy-start.6
  2.8 28.3 %all_to_all.25.x_ref = f32[16,5,8,512]{3,2,1,0:T(8,128)S(1)} all-to-all(f32[16,5,8,512]{3,2,1,0:T(8,128)S(1)} %pad_maximum_fusion), channel_id=1, replica_groups=mesh['band'=16,'slab'=16] {'slab'}, dimensions={0} | all-to-all | bytes 2621440 | tf_op jit(solution)/shard_map/all_to_all | solution.py:360
  31.1 0.0 copy-done.4
  31.1 0.0 copy-done.6
  31.1 4.6 %chebyshev.1 = (f32[16,4,8,512]{3,2,1,0:T(8,128)S(1)}, bf16[32,4,8,256]{3,2,1,0:T(8,128)(2,1)S(1)}) custom-call(f32[16,5,8,512]{3,2,1,0:T(8,128)S(1)} %all_to_all.25.x_ref, bf16[512,512]{1,0:T(8,128)(2,1)S(1)} %copy-done.5, bf16[512,512]{1,0:T(8,128)(2,1)S(1)} %copy-done.4, bf16[128,384]{1,0:T(8,128)(2,1)S(1)} %copy-done.6), custom_call_target="tpu_custom_call" | custom-call | flops 5000000000 | bytes 6000000 | tf_op jit(solution)/shard_map/chebyshev/pallas_call | solution.py:157
  35.7 15.2 %all_to_all.26.high_ref = bf16[32,4,8,256]{3,2,1,0:T(8,128)(2,1)S(1)} all-to-all(bf16[32,4,8,256]{3,2,1,0:T(8,128)(2,1)S(1)} %get-tuple-element.24), channel_id=1, replica_groups={{0,1,2,3,4,5,6,7,8,9,10,11,12,13,14,15,128,129,130,131,132,133,134,135,..., dimensions={0} | all-to-all | bytes 1048576 | tf_op jit(solution)/shard_map/all_to_all | solution.py:346
  50.9 0.1 copy.21
  51.0 5.7 %collective-permute-start.1 = (bf16[8,128,256]{2,1,0:T(8,128)(2,1)S(1)}, bf16[8,128,256]{2,1,0:T(8,128)(2,1)S(1)}, u32[]{:S(2)}, u32[]{:S(2)}) collective-permute-start(bf16[8,128,256]{2,1,0:T(8,128)(2,1)S(1)} %bitcast.15), channel_id=1, source_target_pairs={{0,112},{1,113},{2,114},{3,115},{4,116},{5,117},{6,118},{7,119},{8... | collective-permute-start | bytes 1572872 | tf_op jit(solution)/shard_map/ppermute | solution.py:365
  56.6 0.0 collective-permute-start
  56.6 2.7 %applied.1 = (bf16[32,4,8,256]{3,2,1,0:T(8,128)(2,1)}, bf16[32,8,8,256]{3,2,1,0:T(8,128)(2,1)}) custom-call(f32[16,5,8,512]{3,2,1,0:T(8,128)S(1)} %all_to_all.25.x_ref, f32[16,4,8,512]{3,2,1,0:T(8,128)S(1)} %get-tuple-element.25.f_ref, bf16[512,512]{1,0:T(8,128)(2,1)S(1)} %copy-done.5, bf16[512,512]{1,0:T(8,128)(2,1)S(1)} %copy-done.4, ...), custom_call_target="tpu_custom_call" | custom-call | flops 1000000000 | bytes 6000000 | tf_op jit(solution)/shard_map/applied/pallas_call | solution.py:176
  59.4 4.1 %all-to-all-start.2 = ((bf16[32,4,8,256]{3,2,1,0:T(8,128)(2,1)}), bf16[32,4,8,256]{3,2,1,0:T(8,128)(2,1)S(1)}, u32[]{:S(2)}, u32[]{:S(2)}) async-start(bf16[32,4,8,256]{3,2,1,0:T(8,128)(2,1)} %get-tuple-element.26), calls=%async_computation.2 | async-start | bytes 1048576 | tf_op jit(solution)/shard_map/all_to_all | solution.py:346
  63.5 4.1 %collective-permute-done.1.refs_1_ = bf16[8,128,256]{2,1,0:T(8,128)(2,1)S(1)} collective-permute-done((bf16[8,128,256]{2,1,0:T(8,128)(2,1)S(1)}, bf16[8,128,256]{2,1,0:T(8,128)(2,1)S(1)}, u32[]{:S(2)}, u32[]{:S(2)}) %collective-permute-start.1) | collective-permute-done | bytes 524320 | tf_op jit(solution)/shard_map/ppermute | solution.py:365
  67.6 3.1 %collective-permute-done.refs_0_ = bf16[8,128,256]{2,1,0:T(8,128)(2,1)S(1)} collective-permute-done((bf16[8,128,256]{2,1,0:T(8,128)(2,1)S(1)}, bf16[8,128,256]{2,1,0:T(8,128)(2,1)S(1)}, u32[]{:S(2)}, u32[]{:S(2)}) %collective-permute-start) | collective-permute-done | bytes 524320 | tf_op jit(solution)/shard_map/ppermute | solution.py:364
  70.7 0.0 collective-permute-start.2
  70.7 2.7 %collective-permute-start.3 = (bf16[8,128,256]{2,1,0:T(8,128)(2,1)S(1)}, bf16[8,128,256]{2,1,0:T(8,128)(2,1)}, u32[]{:S(2)}, u32[]{:S(2)}) collective-permute-start(bf16[8,128,256]{2,1,0:T(8,128)(2,1)S(1)} %collective-permute-done.1.refs_1_), channel_id=1, source_target_pairs={{0,112},{1,113},{2,114},{3,115},{4,116},{5,117},{6,118},{7,119},{8... | collective-permute-start | bytes 1572872 | tf_op jit(solution)/shard_map/ppermute | solution.py:370
  73.4 1.7 %all-to-all-done.2 = bf16[32,4,8,256]{3,2,1,0:T(8,128)(2,1)S(1)} async-done(((bf16[32,4,8,256]{3,2,1,0:T(8,128)(2,1)}), bf16[32,4,8,256]{3,2,1,0:T(8,128)(2,1)S(1)}, u32[]{:S(2)}, u32[]{:S(2)}) %all-to-all-start.2) | async-done | bytes 524320 | tf_op jit(solution)/shard_map/all_to_all | solution.py:346
  75.1 0.8 copy-done.7
  75.9 3.9 %all-to-all-start.3 = ((bf16[32,8,8,256]{3,2,1,0:T(8,128)(2,1)}), bf16[32,8,8,256]{3,2,1,0:T(8,128)(2,1)S(1)}, u32[]{:S(2)}, u32[]{:S(2)}) async-start(bf16[32,8,8,256]{3,2,1,0:T(8,128)(2,1)} %get-tuple-element.31), calls=%async_computation.3 | async-start | bytes 2097152 | tf_op jit(solution)/shard_map/all_to_all | solution.py:346
  79.8 4.2 %collective-permute-done.2.refs_2_ = bf16[8,128,256]{2,1,0:T(8,128)(2,1)} collective-permute-done((bf16[8,128,256]{2,1,0:T(8,128)(2,1)S(1)}, bf16[8,128,256]{2,1,0:T(8,128)(2,1)}, u32[]{:S(2)}, u32[]{:S(2)}) %collective-permute-start.2) | collective-permute-done | bytes 524320 | tf_op jit(solution)/shard_map/ppermute | solution.py:369
  84.0 0.0 copy-done
  84.0 0.0 collective-permute-done.3.refs_3_
  84.0 0.1 collective-permute-start.4
  84.1 2.7 %collective-permute-start.5 = (bf16[8,128,256]{2,1,0:T(8,128)(2,1)}, bf16[8,128,256]{2,1,0:T(8,128)(2,1)S(1)}, u32[]{:S(2)}, u32[]{:S(2)}) collective-permute-start(bf16[8,128,256]{2,1,0:T(8,128)(2,1)} %collective-permute-done.3.refs_3_), channel_id=1, source_target_pairs={{0,112},{1,113},{2,114},{3,115},{4,116},{5,117},{6,118},{7,119},{8... | collective-permute-start | bytes 1572872 | tf_op jit(solution)/shard_map/ppermute | solution.py:375
  86.8 10.2 %all-to-all-done.3.rest_ref = bf16[32,8,8,256]{3,2,1,0:T(8,128)(2,1)S(1)} async-done(((bf16[32,8,8,256]{3,2,1,0:T(8,128)(2,1)}), bf16[32,8,8,256]{3,2,1,0:T(8,128)(2,1)S(1)}, u32[]{:S(2)}, u32[]{:S(2)}) %all-to-all-start.3) | async-done | bytes 1048608 | tf_op jit(solution)/shard_map/all_to_all | solution.py:346
  97.0 0.0 collective-permute-done.4.refs_4_
  97.0 0.0 collective-permute-done.5.refs_5_
  97.0 0.1 join.1
  97.1 0.3 collective-permute-start.7
  97.4 0.1 broadcast_select_fusion
  97.5 3.0 %collective-permute-start.6 = (bf16[8,128,256]{2,1,0:T(8,128)(2,1)S(1)}, bf16[8,128,256]{2,1,0:T(8,128)(2,1)S(1)}, u32[]{:S(2)}, u32[]{:S(2)}) collective-permute-start(bf16[8,128,256]{2,1,0:T(8,128)(2,1)S(1)} %broadcast_select_fusion), channel_id=1, source_target_pairs={{0,16},{1,113},{2,18},{3,115},{4,20},{5,117},{6,22},{7,119},{8,24}... | collective-permute-start | bytes 1572872 | tf_op jit(solution)/shard_map/ppermute | solution.py:379
  100.5 0.1 copy.20
  100.6 0.1 copy.19
  100.7 0.9 copy-done.1
  101.6 0.2 copy-done.3
  101.8 3.1 %pairs_early.1 = (bf16[8,384,256]{2,1,0:T(8,128)(2,1)S(1)}, f32[17,64,128]{2,1,0:T(8,128)S(1)}, f32[17,64,128]{2,1,0:T(8,128)S(1)}) custom-call(bf16[8,128,256]{2,1,0:T(8,128)(2,1)S(1)} %bitcast.17, bf16[8,128,256]{2,1,0:T(8,128)(2,1)S(1)} %bitcast.18, bf16[8,128,256]{2,1,0:T(8,128)(2,1)S(1)} %bitcast.19, bf16[8,128,256]{2,1,0:T(8,128)(2,1)S(1)} %copy-done.3, ...), custom_call_target="tpu_custom_call" | custom-call | flops 1400000000 | bytes 6000000 | tf_op jit(solution)/shard_map/pairs_early/pallas_call | solution.py:242
  104.9 3.1 %collective-permute-done.7.far_ref = f32[16,4,8,256]{3,2,1,0:T(8,128)S(1)} collective-permute-done((f32[16,4,8,256]{3,2,1,0:T(8,128)S(1)}, f32[16,4,8,256]{3,2,1,0:T(8,128)S(1)}, u32[]{:S(2)}, u32[]{:S(2)}) %collective-permute-start.7) | collective-permute-done | bytes 524320 | tf_op jit(solution)/shard_map/ppermute | solution.py:382
  108.0 1.0 place.1
  109.0 0.0 collective-permute-done.6.last_ref
  109.0 0.6 pairs_late.1
  109.6 3.8 %collective-permute-start.8 = (f32[17,64,128]{2,1,0:T(8,128)S(1)}, f32[17,64,128]{2,1,0:T(8,128)S(1)}, u32[]{:S(2)}, u32[]{:S(2)}) collective-permute-start(f32[17,64,128]{2,1,0:T(8,128)S(1)} %get-tuple-element.44), channel_id=1, source_target_pairs={{0,1},{1,0},{2,3},{3,2},{4,5},{5,4},{6,7},{7,6},{8,9},{9,8},{10,11... | collective-permute-start | bytes 1671176 | tf_op jit(solution)/shard_map/ppermute | solution.py:386
  113.5 1.6 %collective-permute-done.8 = f32[17,64,128]{2,1,0:T(8,128)S(1)} collective-permute-done((f32[17,64,128]{2,1,0:T(8,128)S(1)}, f32[17,64,128]{2,1,0:T(8,128)S(1)}, u32[]{:S(2)}, u32[]{:S(2)}) %collective-permute-start.8) | collective-permute-done | bytes 557088 | tf_op jit(solution)/shard_map/ppermute | solution.py:386
  115.1 0.1 slice_add_fusion
  115.1 12.2 %all_to_all.27 = f32[16,64,128]{2,1,0:T(8,128)S(1)} all-to-all(f32[16,64,128]{2,1,0:T(8,128)S(1)} %slice_add_fusion), channel_id=1, replica_groups={{0,2,4,6,8,10,12,14,128,130,132,134,136,138,140,142},{1,3,5,7,9,11,13,1..., dimensions={0} | all-to-all | bytes 1048576 | tf_op jit(solution)/shard_map/all_to_all | solution.py:387
  127.4 0.7 fusion
  (12 shorter events, 0.1 us)
Async XLA Ops:
  2.7 28.3 %copy-start.4 = (bf16[512,512]{1,0:T(8,128)(2,1)S(1)}, bf16[512,512]{1,0:T(8,128)(2,1)}, u32[]{:S(2)}) copy-start(bf16[512,512]{1,0:T(8,128)(2,1)} %constant.30.clone.ml_ref) | copy-start | bytes 1572868
  2.7 28.3 %copy-start.5 = (bf16[512,512]{1,0:T(8,128)(2,1)S(1)}, bf16[512,512]{1,0:T(8,128)(2,1)}, u32[]{:S(2)}) copy-start(bf16[512,512]{1,0:T(8,128)(2,1)} %constant.29.clone.mh_ref) | copy-start | bytes 1572868
  2.8 28.3 %copy-start.6 = (bf16[128,384]{1,0:T(8,128)(2,1)S(1)}, bf16[128,384]{1,0:T(8,128)(2,1)}, u32[]{:S(2)}) copy-start(bf16[128,384]{1,0:T(8,128)(2,1)} %constant.31.clone.z_ref) | copy-start | bytes 294916
  51.0 16.7 %collective-permute-start.1 = (bf16[8,128,256]{2,1,0:T(8,128)(2,1)S(1)}, bf16[8,128,256]{2,1,0:T(8,128)(2,1)S(1)}, u32[]{:S(2)}, u32[]{:S(2)}) collective-permute-start(bf16[8,128,256]{2,1,0:T(8,128)(2,1)S(1)} %bitcast.15), channel_id=1, source_target_pairs={{0,112},{1,113},{2,114},{3,115},{4,116},{5,117},{6,118},{7,119},{8... | collective-permute-start | bytes 1572872 | tf_op jit(solution)/shard_map/ppermute | solution.py:365
  56.6 14.1 %collective-permute-start = (bf16[8,128,256]{2,1,0:T(8,128)(2,1)S(1)}, bf16[8,128,256]{2,1,0:T(8,128)(2,1)S(1)}, u32[]{:S(2)}, u32[]{:S(2)}) collective-permute-start(bf16[8,128,256]{2,1,0:T(8,128)(2,1)S(1)} %bitcast.16), channel_id=1, source_target_pairs={{0,16},{1,17},{2,18},{3,19},{4,20},{5,21},{6,22},{7,23},{8,24},{9,... | collective-permute-start | bytes 1572872 | tf_op jit(solution)/shard_map/ppermute | solution.py:364
  59.4 15.7 %all-to-all-start.2 = ((bf16[32,4,8,256]{3,2,1,0:T(8,128)(2,1)}), bf16[32,4,8,256]{3,2,1,0:T(8,128)(2,1)S(1)}, u32[]{:S(2)}, u32[]{:S(2)}) async-start(bf16[32,4,8,256]{3,2,1,0:T(8,128)(2,1)} %get-tuple-element.26), calls=%async_computation.2 | async-start | bytes 1048576 | tf_op jit(solution)/shard_map/all_to_all | solution.py:346
  67.6 16.4 %copy-start = (bf16[8,128,256]{2,1,0:T(8,128)(2,1)}, bf16[8,128,256]{2,1,0:T(8,128)(2,1)S(1)}, u32[]{:S(2)}) copy-start(bf16[8,128,256]{2,1,0:T(8,128)(2,1)S(1)} %collective-permute-done.1.refs_1_) | copy-start | bytes 1572868
  70.7 13.3 %copy-start.2 = (bf16[8,128,256]{2,1,0:T(8,128)(2,1)}, bf16[8,128,256]{2,1,0:T(8,128)(2,1)S(1)}, u32[]{:S(2)}) copy-start(bf16[8,128,256]{2,1,0:T(8,128)(2,1)S(1)} %collective-permute-done.refs_0_) | copy-start | bytes 1572868
  70.7 13.3 %collective-permute-start.2 = (bf16[8,128,256]{2,1,0:T(8,128)(2,1)S(1)}, bf16[8,128,256]{2,1,0:T(8,128)(2,1)}, u32[]{:S(2)}, u32[]{:S(2)}) collective-permute-start(bf16[8,128,256]{2,1,0:T(8,128)(2,1)S(1)} %collective-permute-done.refs_0_), channel_id=1, source_target_pairs={{0,16},{1,17},{2,18},{3,19},{4,20},{5,21},{6,22},{7,23},{8,24},{9,... | collective-permute-start | bytes 1572872 | tf_op jit(solution)/shard_map/ppermute | solution.py:369
  70.7 13.3 %collective-permute-start.3 = (bf16[8,128,256]{2,1,0:T(8,128)(2,1)S(1)}, bf16[8,128,256]{2,1,0:T(8,128)(2,1)}, u32[]{:S(2)}, u32[]{:S(2)}) collective-permute-start(bf16[8,128,256]{2,1,0:T(8,128)(2,1)S(1)} %collective-permute-done.1.refs_1_), channel_id=1, source_target_pairs={{0,112},{1,113},{2,114},{3,115},{4,116},{5,117},{6,118},{7,119},{8... | collective-permute-start | bytes 1572872 | tf_op jit(solution)/shard_map/ppermute | solution.py:370
  75.1 0.8 copy-start.7
  75.9 21.1 %all-to-all-start.3 = ((bf16[32,8,8,256]{3,2,1,0:T(8,128)(2,1)}), bf16[32,8,8,256]{3,2,1,0:T(8,128)(2,1)S(1)}, u32[]{:S(2)}, u32[]{:S(2)}) async-start(bf16[32,8,8,256]{3,2,1,0:T(8,128)(2,1)} %get-tuple-element.31), calls=%async_computation.3 | async-start | bytes 2097152 | tf_op jit(solution)/shard_map/all_to_all | solution.py:346
  84.0 13.0 %collective-permute-start.4 = (bf16[8,128,256]{2,1,0:T(8,128)(2,1)}, bf16[8,128,256]{2,1,0:T(8,128)(2,1)S(1)}, u32[]{:S(2)}, u32[]{:S(2)}) collective-permute-start(bf16[8,128,256]{2,1,0:T(8,128)(2,1)} %collective-permute-done.2.refs_2_), channel_id=1, source_target_pairs={{0,16},{1,17},{2,18},{3,19},{4,20},{5,21},{6,22},{7,23},{8,24},{9,... | collective-permute-start | bytes 1572872 | tf_op jit(solution)/shard_map/ppermute | solution.py:374
  84.1 12.9 %collective-permute-start.5 = (bf16[8,128,256]{2,1,0:T(8,128)(2,1)}, bf16[8,128,256]{2,1,0:T(8,128)(2,1)S(1)}, u32[]{:S(2)}, u32[]{:S(2)}) collective-permute-start(bf16[8,128,256]{2,1,0:T(8,128)(2,1)} %collective-permute-done.3.refs_3_), channel_id=1, source_target_pairs={{0,112},{1,113},{2,114},{3,115},{4,116},{5,117},{6,118},{7,119},{8... | collective-permute-start | bytes 1572872 | tf_op jit(solution)/shard_map/ppermute | solution.py:375
  97.0 3.5 %copy-start.8 = (bf16[32,4,8,256]{3,2,1,0:T(8,128)(2,1)S(1)}, bf16[32,4,8,256]{3,2,1,0:T(8,128)(2,1)}, u32[]{:S(2)}) copy-start(bf16[32,4,8,256]{3,2,1,0:T(8,128)(2,1)} %copy-done.7) | copy-start | bytes 1572868
  97.1 10.8 %collective-permute-start.7 = (f32[16,4,8,256]{3,2,1,0:T(8,128)S(1)}, f32[16,4,8,256]{3,2,1,0:T(8,128)S(1)}, u32[]{:S(2)}, u32[]{:S(2)}) collective-permute-start(f32[16,4,8,256]{3,2,1,0:T(8,128)S(1)} %get-tuple-element.36), channel_id=1, source_target_pairs={{0,128},{1,129},{2,130},{3,131},{4,132},{5,133},{6,134},{7,135},{8... | collective-permute-start | bytes 1572872 | tf_op jit(solution)/shard_map/ppermute | solution.py:382
  97.5 11.5 %collective-permute-start.6 = (bf16[8,128,256]{2,1,0:T(8,128)(2,1)S(1)}, bf16[8,128,256]{2,1,0:T(8,128)(2,1)S(1)}, u32[]{:S(2)}, u32[]{:S(2)}) collective-permute-start(bf16[8,128,256]{2,1,0:T(8,128)(2,1)S(1)} %broadcast_select_fusion), channel_id=1, source_target_pairs={{0,16},{1,113},{2,18},{3,115},{4,20},{5,117},{6,22},{7,119},{8,24}... | collective-permute-start | bytes 1572872 | tf_op jit(solution)/shard_map/ppermute | solution.py:379
  100.6 1.0 copy-start.1
  100.6 1.2 copy-start.3
  109.6 5.4 %collective-permute-start.8 = (f32[17,64,128]{2,1,0:T(8,128)S(1)}, f32[17,64,128]{2,1,0:T(8,128)S(1)}, u32[]{:S(2)}, u32[]{:S(2)}) collective-permute-start(f32[17,64,128]{2,1,0:T(8,128)S(1)} %get-tuple-element.44), channel_id=1, source_target_pairs={{0,1},{1,0},{2,3},{3,2},{4,5},{5,4},{6,7},{7,6},{8,9},{9,8},{10,11... | collective-permute-start | bytes 1671176 | tf_op jit(solution)/shard_map/ppermute | solution.py:386

commit v5 on v4

--- a/solution.py
+++ b/solution.py
@@ -83,7 +83,7 @@
             ref[side * SLABS + slab, orb] = value[slab_rows(slab), side * HALF : (side + 1) * HALF].astype(BF16)
 
 
-def filter_kernel(x_ref, mh_ref, ml_ref, z_ref, out_ref, low_ref, field_a, field_b, pot, split, total):
+def filter_kernel(x_ref, mh_ref, ml_ref, z_ref, out_ref, low_ref, rest_ref, field_a, field_b, pot, split, total):
     for slab in range(SLABS):
         for orb in range(OWN):
             field_a[orb, slab_rows(slab), :] = x_ref[slab, orb]
@@ -112,13 +112,15 @@
                 following = following - back * previous[orb]
             previous[orb] = following
             if number == len(steps) - 1:
-                put_low(low_ref, orb, following)
+                high = following.astype(BF16).astype(F32)
+                put_low(low_ref, orb, high)
+                put_low(rest_ref, orb, following - high)
                 for slab in range(SLABS):
                     out_ref[slab, orb] = following[slab_rows(slab), :]
         current, previous = previous, current
 
 
-def apply_kernel(x_ref, f_ref, mh_ref, ml_ref, z_ref, app_ref, rest_ref, pot, split, total, rest):
+def apply_kernel(x_ref, f_ref, mh_ref, ml_ref, z_ref, app_ref, pot, split, total, rest):
     for slab in range(SLABS):
         for orb in range(OWN):
             rows = slice(orb * NZ + slab * DEPTH, orb * NZ + (slab + 1) * DEPTH)
@@ -146,22 +148,22 @@
         middle = 0.5 * (applied_low + of_low)
         middle_high = middle.astype(BF16).astype(F32)
         put_low(app_ref, orb, middle_high)
-        put_low(rest_ref, orb, middle - middle_high)
-        put_low(rest_ref, OWN + orb, low.astype(F32))
+        put_low(app_ref, OWN + orb, middle - middle_high)
 
 
 def run_filter(block):
     plane_high, plane_low, z_stack = (jnp.asarray(matrix) for matrix in stencil_matrices())
     vmem = pl.BlockSpec(memory_space=pltpu.VMEM)
     params = pltpu.CompilerParams(vmem_limit_bytes=KERNEL_BYTES)
-    filtered, filtered_low = pl.pallas_call(
+    filtered, filtered_low, filtered_rest = pl.pallas_call(
         filter_kernel,
         out_shape=(
             jax.ShapeDtypeStruct((SLABS, OWN, DEPTH, PLANE), F32),
             jax.ShapeDtypeStruct((PEERS, OWN, DEPTH, HALF), BF16),
+            jax.ShapeDtypeStruct((PEERS, OWN, DEPTH, HALF), BF16),
         ),
         in_specs=[vmem] * 4,
-        out_specs=(vmem, vmem),
+        out_specs=(vmem, vmem, vmem),
         scratch_shapes=[
             pltpu.VMEM((OWN, NZ, PLANE), F32),
             pltpu.VMEM((OWN, NZ, PLANE), F32),
@@ -173,14 +175,11 @@
         cost_estimate=pl.CostEstimate(flops=5_000_000_000, bytes_accessed=6_000_000, transcendentals=0),
         name="chebyshev",
     )(block, plane_high, plane_low, z_stack)
-    applied, rest = pl.pallas_call(
+    applied = pl.pallas_call(
         apply_kernel,
-        out_shape=(
-            jax.ShapeDtypeStruct((PEERS, OWN, DEPTH, HALF), BF16),
-            jax.ShapeDtypeStruct((PEERS, 2 * OWN, DEPTH, HALF), BF16),
-        ),
+        out_shape=jax.ShapeDtypeStruct((PEERS, 2 * OWN, DEPTH, HALF), BF16),
         in_specs=[vmem] * 5,
-        out_specs=(vmem, vmem),
+        out_specs=vmem,
         scratch_shapes=[
             pltpu.VMEM((NZ, PLANE), F32),
             pltpu.VMEM((2, OWN * NZ, PLANE), BF16),
@@ -191,7 +190,7 @@
         cost_estimate=pl.CostEstimate(flops=1_000_000_000, bytes_accessed=6_000_000, transcendentals=0),
         name="applied",
     )(block, filtered, plane_high, plane_low, z_stack)
-    return filtered_low, applied, rest
+    return filtered_low, filtered_rest, applied
 
 
 def put_pairs(total, shift, keep_ref, send_ref):
@@ -269,7 +268,7 @@
     side = lax.div(lax.axis_index("band"), RING)
     for ref, which in ((near_ref, side), (far_ref, 1 - side)):
         sources = pl.ds(which * SLABS, SLABS)
-        ref[...] = high_ref[sources].astype(F32) + rest_ref[sources, OWN:].astype(F32)
+        ref[...] = high_ref[sources].astype(F32) + rest_ref[sources].astype(F32)
 
 
 def run_join(high, rest):
@@ -358,29 +357,32 @@
     block = orbitals.reshape(SLABS, OWN, DEPTH, PLANE)
     shared = jnp.broadcast_to(potential[None, None], (SLABS, 1, DEPTH, PLANE))
     block = lax.all_to_all(jnp.concatenate([block, shared], axis=1), "slab", 0, 0, tiled=True)
-    filtered_low, applied, rest = run_filter(block)
+    filtered_low, filtered_rest, applied = run_filter(block)
     filtered_low = over_plane(filtered_low)
     own_low = by_depth(filtered_low)
     ahead = lax.ppermute(own_low, BOTH, ring_pairs(1, 1))
     behind = lax.ppermute(own_low, BOTH, ring_pairs(-1, -1))
     blocks = [ahead, behind]
-    high = over_plane(applied)
-    ahead, behind, applied = lax.optimization_barrier((ahead, behind, applied))
+    filtered_rest = over_plane(filtered_rest)
+    ahead, applied = lax.optimization_barrier((ahead, applied))
+    behind, applied = lax.optimization_barrier((behind, applied))
     ahead = lax.ppermute(ahead, BOTH, ring_pairs(1, 1))
     behind = lax.ppermute(behind, BOTH, ring_pairs(-1, -1))
     blocks += [ahead, behind]
-    ahead, behind, high = lax.optimization_barrier((ahead, behind, high))
-    rest = over_plane(rest)
+    ahead, filtered_rest = lax.optimization_barrier((ahead, filtered_rest))
+    behind, filtered_rest = lax.optimization_barrier((behind, filtered_rest))
+    applied = over_plane(applied)
     ahead = lax.ppermute(ahead, BOTH, ring_pairs(1, 1))
     behind = lax.ppermute(behind, BOTH, ring_pairs(-1, -1))
     blocks += [ahead, behind]
-    ahead, behind, rest = lax.optimization_barrier((ahead, behind, rest))
+    ahead, applied = lax.optimization_barrier((ahead, applied))
+    behind, applied = lax.optimization_barrier((behind, applied))
     last = jnp.where(lax.axis_index("slab") % 2 == 0, ahead, behind)
     last = lax.ppermute(last, BOTH, ring_pairs(1, -1))
-    weights, keep, send = run_early(own_low, by_depth(high), by_depth(rest[:, :OWN]), blocks)
-    near, far = run_join(filtered_low, rest)
+    weights, keep, send = run_early(own_low, by_depth(applied[:, :OWN]), by_depth(applied[:, OWN:]), blocks)
+    near, far = run_join(filtered_low, filtered_rest)
     far = lax.ppermute(far, BOTH, side_pairs())
-    filtered = run_place(near, far)
+    filtered = run_place(near, after(far, keep))
     last, filtered = lax.optimization_barrier((last, filtered))
     keep, send = run_late(weights, last, keep, send)
     sums = (keep + lax.ppermute(send, BOTH, core_pairs()))[: 2 * RING]

time: 129 us -> 127 us (0.984)
  waiting for transfers between devices: 28 us -> 21.3 us
  local copies, waits for them, and re-layouts: 3.62 us -> 5.94 us
    ppermute x1, waiting for transfers between devices: 4.14 us -> 0.01 us  [on_device(): behind = lax.ppermute(own_low, BOTH, ring_pairs(-1, -1))]
    all_to_all x2, waiting for transfers between devices: 11.9 us -> 8.53 us  [over_plane(): lax.all_to_all(block, BOTH, 0, 0, axis_index_groups=plane_groups(), tiled...]
    ppermute x2, waiting for transfers between devices: 4.2 us -> 7.47 us  [on_device(): ahead = lax.ppermute(ahead, BOTH, ring_pairs(1, 1))]
    ppermute x1, waiting for transfers between devices: 3.07 us -> 0.01 us  [on_device(): far = lax.ppermute(far, BOTH, side_pairs())]
    ppermute x1, starting transfers between devices: 5.65 us -> 3.94 us  [on_device(): behind = lax.ppermute(own_low, BOTH, ring_pairs(-1, -1))]
    ppermute x1, starting transfers between devices: 0.01 us -> 1.64 us  [on_device(): ahead = lax.ppermute(own_low, BOTH, ring_pairs(1, 1))]
  transfers between devices with their start and end apart: 11 -> 11, of which waited for: 7 -> 7; matrix products, arithmetic and copies ran while one was open for 0% -> 1% of each run, Pallas kernels for 5% -> 6%
where the time goes in v5:
time: 127 us; the launch traced here: 126 us
  blocking collectives  56.3 us (44%)
  starting transfers between devices  27 us (21%)
  waiting for transfers between devices  21.3 us (17%)
  Pallas kernels  13.2 us (10%)
  local copies, waits for them, and re-layouts  5.94 us (5%)
  other arithmetic  1.53 us (1%)
    all_to_all x1, blocking collectives, on_device(): lax.all_to_all(jnp.concatenate([block, shared], axis=1), 'slab', 0, 0, ti...  28.3 us
    all_to_all x1, blocking collectives, over_plane(): lax.all_to_all(block, BOTH, 0, 0, axis_index_groups=plane_groups(), tiled...  15.2 us
    all_to_all x1, blocking collectives, on_device(): lax.all_to_all(sums, BOTH, 0, 0, axis_index_groups=core_groups(), tiled=T...  12.8 us
    all_to_all x2, starting transfers between devices, over_plane(): lax.all_to_all(block, BOTH, 0, 0, axis_index_groups=plane_groups(), tiled...  9.1 us
    all_to_all x2, waiting for transfers between devices, over_plane(): lax.all_to_all(block, BOTH, 0, 0, axis_index_groups=plane_groups(), tiled...  8.53 us
    ppermute x2, waiting for transfers between devices, on_device(): ahead = lax.ppermute(ahead, BOTH, ring_pairs(1, 1))  7.47 us
    ppermute x2, starting transfers between devices, on_device(): behind = lax.ppermute(behind, BOTH, ring_pairs(-1, -1))  5.35 us
    pallas_call x1, Pallas kernels, run_filter(): pl.pallas_call(filter_kernel, out_shape=(jax.ShapeDtypeStruct((SLABS, OWN...  4.68 us
  transfers between devices with their start and end apart: 11, of which 7 were waited for; matrix products, arithmetic and copies ran while one was open for 1% of the time, Pallas kernels for 6%

profile of v5, /device:TPU:1, one launch (start us, length us, event | category | flops | bytes accessed | tf_op | source)
XLA Modules:
  0.0 126.0 jit_solution(4720112712062085005)
XLA Ops:
  0.6 0.7 broadcast_in_dim.2
  1.4 1.4 %pad_maximum_fusion = f32[16,5,8,512]{3,2,1,0:T(8,128)S(1)} fusion(f32[16,1,8,512]{3,2,1,0:T(8,128)S(1)} %broadcast_in_dim.2, f32[16,4,8,512]{3,2,1,0:T(8,128)} %bitcast.15), kind=kLoop, calls=%fused_computation | loop fusion | flops 327680 | bytes 2621440 | tf_op jit(solution)/shard_map/concatenate | solution.py:359
  2.7 0.0 copy-start
  2.7 0.0 copy-start.2
  2.8 0.0 copy-start.5
  2.8 28.3 %all_to_all.25.x_ref = f32[16,5,8,512]{3,2,1,0:T(8,128)S(1)} all-to-all(f32[16,5,8,512]{3,2,1,0:T(8,128)S(1)} %pad_maximum_fusion), channel_id=1, replica_groups=mesh['band'=16,'slab'=16] {'slab'}, dimensions={0} | all-to-all | bytes 2621440 | tf_op jit(solution)/shard_map/all_to_all | solution.py:359
  31.1 0.0 copy-done
  31.1 0.0 copy-done.2
  31.1 4.7 %chebyshev.1 = (f32[16,4,8,512]{3,2,1,0:T(8,128)S(1)}, bf16[32,4,8,256]{3,2,1,0:T(8,128)(2,1)S(1)}, bf16[32,4,8,256]{3,2,1,0:T(8,128)(2,1)S(1)}) custom-call(f32[16,5,8,512]{3,2,1,0:T(8,128)S(1)} %all_to_all.25.x_ref, bf16[512,512]{1,0:T(8,128)(2,1)S(1)} %copy-done, bf16[512,512]{1,0:T(8,128)(2,1)S(1)} %copy-done.2, bf16[128,384]{1,0:T(8,128)(2,1)S(1)} %copy-done.5), custom_call_target="tpu_custom_call" | custom-call | flops 5000000000 | bytes 6000000 | tf_op jit(solution)/shard_map/chebyshev/pallas_call | solution.py:158
  35.8 15.2 %all_to_all.26.high_ref = bf16[32,4,8,256]{3,2,1,0:T(8,128)(2,1)S(1)} all-to-all(bf16[32,4,8,256]{3,2,1,0:T(8,128)(2,1)S(1)} %get-tuple-element.28), channel_id=1, replica_groups={{0,1,2,3,4,5,6,7,8,9,10,11,12,13,14,15,128,129,130,131,132,133,134,135,..., dimensions={0} | all-to-all | bytes 1048576 | tf_op jit(solution)/shard_map/all_to_all | solution.py:345
  51.0 0.9 copy.19
  51.9 1.6 %collective-permute-start = (bf16[8,128,256]{2,1,0:T(8,128)(2,1)}, bf16[8,128,256]{2,1,0:T(8,128)(2,1)}, u32[]{:S(2)}, u32[]{:S(2)}) collective-permute-start(bf16[8,128,256]{2,1,0:T(8,128)(2,1)} %bitcast.11.own_ref), channel_id=1, source_target_pairs={{0,16},{1,17},{2,18},{3,19},{4,20},{5,21},{6,22},{7,23},{8,24},{9,... | collective-permute-start | bytes 1572872 | tf_op jit(solution)/shard_map/ppermute | solution.py:363
  53.5 3.9 %collective-permute-start.3 = (bf16[8,128,256]{2,1,0:T(8,128)(2,1)}, bf16[8,128,256]{2,1,0:T(8,128)(2,1)}, u32[]{:S(2)}, u32[]{:S(2)}) collective-permute-start(bf16[8,128,256]{2,1,0:T(8,128)(2,1)} %bitcast.11.own_ref), channel_id=1, source_target_pairs={{0,112},{1,113},{2,114},{3,115},{4,116},{5,117},{6,118},{7,119},{8... | collective-permute-start | bytes 1572872 | tf_op jit(solution)/shard_map/ppermute | solution.py:364
  57.4 0.0 copy-done.4
  57.4 4.1 %all-to-all-start.2 = ((bf16[32,4,8,256]{3,2,1,0:T(8,128)(2,1)}), bf16[32,4,8,256]{3,2,1,0:T(8,128)(2,1)S(1)}, u32[]{:S(2)}, u32[]{:S(2)}) async-start(bf16[32,4,8,256]{3,2,1,0:T(8,128)(2,1)} %copy-done.4), calls=%async_computation.2 | async-start | bytes 1048576 | tf_op jit(solution)/shard_map/all_to_all | solution.py:345
  61.6 0.0 copy-start.1
  61.6 1.0 copy-done.1
  62.6 1.0 copy-done.3
  63.7 2.6 %applied.1 = bf16[32,8,8,256]{3,2,1,0:T(8,128)(2,1)} custom-call(f32[16,5,8,512]{3,2,1,0:T(8,128)S(1)} %all_to_all.25.x_ref, f32[16,4,8,512]{3,2,1,0:T(8,128)S(1)} %get-tuple-element.29.f_ref, bf16[512,512]{1,0:T(8,128)(2,1)S(1)} %copy-done.1, bf16[512,512]{1,0:T(8,128)(2,1)S(1)} %copy-done.3, bf16[128,384]{1,0:T(8,128)(2,1)S(1)} %copy-done.5), custom_call_target="tpu_custom_call" | custom-call | flops 1000000000 | bytes 6000000 | tf_op jit(solution)/shard_map/applied/pallas_call | solution.py:178
  66.2 3.6 %collective-permute-done.refs_0_ = bf16[8,128,256]{2,1,0:T(8,128)(2,1)} collective-permute-done((bf16[8,128,256]{2,1,0:T(8,128)(2,1)}, bf16[8,128,256]{2,1,0:T(8,128)(2,1)}, u32[]{:S(2)}, u32[]{:S(2)}) %collective-permute-start) | collective-permute-done | bytes 524320 | tf_op jit(solution)/shard_map/ppermute | solution.py:363
  69.8 0.0 collective-permute-start.1
  69.8 0.0 collective-permute-done.3.refs_1_
  69.8 2.7 %collective-permute-start.4 = (bf16[8,128,256]{2,1,0:T(8,128)(2,1)}, bf16[8,128,256]{2,1,0:T(8,128)(2,1)}, u32[]{:S(2)}, u32[]{:S(2)}) collective-permute-start(bf16[8,128,256]{2,1,0:T(8,128)(2,1)} %collective-permute-done.3.refs_1_), channel_id=1, source_target_pairs={{0,112},{1,113},{2,114},{3,115},{4,116},{5,117},{6,118},{7,119},{8... | collective-permute-start | bytes 1572872 | tf_op jit(solution)/shard_map/ppermute | solution.py:370
  72.5 0.7 all-to-all-done.2.rest_ref
  73.1 5.0 %all-to-all-start.3 = ((bf16[32,8,8,256]{3,2,1,0:T(8,128)(2,1)}), bf16[32,8,8,256]{3,2,1,0:T(8,128)(2,1)}, u32[]{:S(2)}, u32[]{:S(2)}) async-start(bf16[32,8,8,256]{3,2,1,0:T(8,128)(2,1)} %applied.1), calls=%async_computation.3 | async-start | bytes 2097152 | tf_op jit(solution)/shard_map/all_to_all | solution.py:345
  78.1 5.8 %collective-permute-done.1.refs_2_ = bf16[8,128,256]{2,1,0:T(8,128)(2,1)S(1)} collective-permute-done((bf16[8,128,256]{2,1,0:T(8,128)(2,1)}, bf16[8,128,256]{2,1,0:T(8,128)(2,1)S(1)}, u32[]{:S(2)}, u32[]{:S(2)}) %collective-permute-start.1) | collective-permute-done | bytes 524320 | tf_op jit(solution)/shard_map/ppermute | solution.py:369
  84.0 0.0 collective-permute-start.2
  84.0 0.0 collective-permute-done.4.refs_3_
  84.0 2.7 %collective-permute-start.5 = (bf16[8,128,256]{2,1,0:T(8,128)(2,1)}, bf16[8,128,256]{2,1,0:T(8,128)(2,1)S(1)}, u32[]{:S(2)}, u32[]{:S(2)}) collective-permute-start(bf16[8,128,256]{2,1,0:T(8,128)(2,1)} %collective-permute-done.4.refs_3_), channel_id=1, source_target_pairs={{0,112},{1,113},{2,114},{3,115},{4,116},{5,117},{6,118},{7,119},{8... | collective-permute-start | bytes 1572872 | tf_op jit(solution)/shard_map/ppermute | solution.py:376
  86.6 0.8 join.1
  87.5 0.0 collective-permute-start.7
  87.5 7.9 %all-to-all-done.3 = bf16[32,8,8,256]{3,2,1,0:T(8,128)(2,1)} async-done(((bf16[32,8,8,256]{3,2,1,0:T(8,128)(2,1)}), bf16[32,8,8,256]{3,2,1,0:T(8,128)(2,1)}, u32[]{:S(2)}, u32[]{:S(2)}) %all-to-all-start.3) | async-done | bytes 1048608 | tf_op jit(solution)/shard_map/all_to_all | solution.py:345
  95.4 1.6 %collective-permute-done.2.refs_4_ = bf16[8,128,256]{2,1,0:T(8,128)(2,1)S(1)} collective-permute-done((bf16[8,128,256]{2,1,0:T(8,128)(2,1)S(1)}, bf16[8,128,256]{2,1,0:T(8,128)(2,1)S(1)}, u32[]{:S(2)}, u32[]{:S(2)}) %collective-permute-start.2) | collective-permute-done | bytes 524320 | tf_op jit(solution)/shard_map/ppermute | solution.py:375
  97.0 0.0 collective-permute-done.5.refs_5_
  97.0 0.1 broadcast_select_fusion
  97.0 2.7 %collective-permute-start.6 = (bf16[8,128,256]{2,1,0:T(8,128)(2,1)S(1)}, bf16[8,128,256]{2,1,0:T(8,128)(2,1)S(1)}, u32[]{:S(2)}, u32[]{:S(2)}) collective-permute-start(bf16[8,128,256]{2,1,0:T(8,128)(2,1)S(1)} %broadcast_select_fusion), channel_id=1, source_target_pairs={{0,16},{1,113},{2,18},{3,115},{4,20},{5,117},{6,22},{7,119},{8,24}... | collective-permute-start | bytes 1572872 | tf_op jit(solution)/shard_map/ppermute | solution.py:381
  99.7 1.3 %fusion = (bf16[32,4,8,256]{3,2,1,0:T(8,128)(2,1)S(1)}, bf16[32,4,8,256]{3,2,1,0:T(8,128)(2,1)S(1)}) fusion(bf16[32,8,8,256]{3,2,1,0:T(8,128)(2,1)} %all-to-all-done.3), kind=kLoop, calls=%fused_computation.7 | loop fusion | bytes 2097152 | tf_op jit(solution)/shard_map/slice | solution.py:382
  101.0 0.2 copy_bitcast_fusion
  101.2 3.5 %pairs_early.1 = (bf16[8,384,256]{2,1,0:T(8,128)(2,1)S(1)}, f32[17,64,128]{2,1,0:T(8,128)S(1)}, f32[17,64,128]{2,1,0:T(8,128)S(1)}) custom-call(bf16[8,128,256]{2,1,0:T(8,128)(2,1)} %bitcast.11.own_ref, bf16[8,128,256]{2,1,0:T(8,128)(2,1)S(1)} %get-tuple-element.58.high_ref, bf16[8,128,256]{2,1,0:T(8,128)(2,1)S(1)} %get-tuple-element.57.rest_ref, ...), custom_call_target="tpu_custom_call" | custom-call | flops 1400000000 | bytes 6000000 | tf_op jit(solution)/shard_map/pairs_early/pallas_call | solution.py:241
  104.7 0.0 collective-permute-done.7.far_ref
  104.7 1.0 place.1
  105.7 0.1 collective-permute-done.6.last_ref
  105.9 0.6 pairs_late.1
  106.5 4.3 %collective-permute-start.8 = (f32[17,64,128]{2,1,0:T(8,128)S(1)}, f32[17,64,128]{2,1,0:T(8,128)S(1)}, u32[]{:S(2)}, u32[]{:S(2)}) collective-permute-start(f32[17,64,128]{2,1,0:T(8,128)S(1)} %get-tuple-element.52), channel_id=1, source_target_pairs={{0,1},{1,0},{2,3},{3,2},{4,5},{5,4},{6,7},{7,6},{8,9},{9,8},{10,11... | collective-permute-start | bytes 1671176 | tf_op jit(solution)/shard_map/ppermute | solution.py:388
  110.8 1.6 %collective-permute-done.8 = f32[17,64,128]{2,1,0:T(8,128)S(1)} collective-permute-done((f32[17,64,128]{2,1,0:T(8,128)S(1)}, f32[17,64,128]{2,1,0:T(8,128)S(1)}, u32[]{:S(2)}, u32[]{:S(2)}) %collective-permute-start.8) | collective-permute-done | bytes 557088 | tf_op jit(solution)/shard_map/ppermute | solution.py:388
  112.4 0.1 slice_add_fusion
  112.4 12.8 %all_to_all.27 = f32[16,64,128]{2,1,0:T(8,128)S(1)} all-to-all(f32[16,64,128]{2,1,0:T(8,128)S(1)} %slice_add_fusion), channel_id=1, replica_groups={{0,2,4,6,8,10,12,14,128,130,132,134,136,138,140,142},{1,3,5,7,9,11,13,1..., dimensions={0} | all-to-all | bytes 1048576 | tf_op jit(solution)/shard_map/all_to_all | solution.py:389
  125.3 0.7 fusion.1
  (5 shorter events, 0.0 us)
Async XLA Ops:
  2.7 28.3 %copy-start = (bf16[512,512]{1,0:T(8,128)(2,1)S(1)}, bf16[512,512]{1,0:T(8,128)(2,1)}, u32[]{:S(2)}) copy-start(bf16[512,512]{1,0:T(8,128)(2,1)} %constant.29.clone.mh_ref) | copy-start | bytes 1572868
  2.7 28.3 %copy-start.2 = (bf16[512,512]{1,0:T(8,128)(2,1)S(1)}, bf16[512,512]{1,0:T(8,128)(2,1)}, u32[]{:S(2)}) copy-start(bf16[512,512]{1,0:T(8,128)(2,1)} %constant.30.clone.ml_ref) | copy-start | bytes 1572868
  2.8 28.3 %copy-start.5 = (bf16[128,384]{1,0:T(8,128)(2,1)S(1)}, bf16[128,384]{1,0:T(8,128)(2,1)}, u32[]{:S(2)}) copy-start(bf16[128,384]{1,0:T(8,128)(2,1)} %constant.31.clone.z_ref) | copy-start | bytes 294916
  35.8 21.7 %copy-start.4 = (bf16[32,4,8,256]{3,2,1,0:T(8,128)(2,1)}, bf16[32,4,8,256]{3,2,1,0:T(8,128)(2,1)S(1)}, u32[]{:S(2)}) copy-start(bf16[32,4,8,256]{3,2,1,0:T(8,128)(2,1)S(1)} %get-tuple-element.31) | copy-start | bytes 1572868
  51.9 18.0 %collective-permute-start = (bf16[8,128,256]{2,1,0:T(8,128)(2,1)}, bf16[8,128,256]{2,1,0:T(8,128)(2,1)}, u32[]{:S(2)}, u32[]{:S(2)}) collective-permute-start(bf16[8,128,256]{2,1,0:T(8,128)(2,1)} %bitcast.11.own_ref), channel_id=1, source_target_pairs={{0,16},{1,17},{2,18},{3,19},{4,20},{5,21},{6,22},{7,23},{8,24},{9,... | collective-permute-start | bytes 1572872 | tf_op jit(solution)/shard_map/ppermute | solution.py:363
  53.5 16.3 %collective-permute-start.3 = (bf16[8,128,256]{2,1,0:T(8,128)(2,1)}, bf16[8,128,256]{2,1,0:T(8,128)(2,1)}, u32[]{:S(2)}, u32[]{:S(2)}) collective-permute-start(bf16[8,128,256]{2,1,0:T(8,128)(2,1)} %bitcast.11.own_ref), channel_id=1, source_target_pairs={{0,112},{1,113},{2,114},{3,115},{4,116},{5,117},{6,118},{7,119},{8... | collective-permute-start | bytes 1572872 | tf_op jit(solution)/shard_map/ppermute | solution.py:364
  57.4 15.7 %all-to-all-start.2 = ((bf16[32,4,8,256]{3,2,1,0:T(8,128)(2,1)}), bf16[32,4,8,256]{3,2,1,0:T(8,128)(2,1)S(1)}, u32[]{:S(2)}, u32[]{:S(2)}) async-start(bf16[32,4,8,256]{3,2,1,0:T(8,128)(2,1)} %copy-done.4), calls=%async_computation.2 | async-start | bytes 1048576 | tf_op jit(solution)/shard_map/all_to_all | solution.py:345
  61.6 1.0 copy-start.1
  62.6 1.0 copy-start.3
  69.8 14.2 %collective-permute-start.1 = (bf16[8,128,256]{2,1,0:T(8,128)(2,1)}, bf16[8,128,256]{2,1,0:T(8,128)(2,1)S(1)}, u32[]{:S(2)}, u32[]{:S(2)}) collective-permute-start(bf16[8,128,256]{2,1,0:T(8,128)(2,1)} %collective-permute-done.refs_0_), channel_id=1, source_target_pairs={{0,16},{1,17},{2,18},{3,19},{4,20},{5,21},{6,22},{7,23},{8,24},{9,... | collective-permute-start | bytes 1572872 | tf_op jit(solution)/shard_map/ppermute | solution.py:369
  69.8 14.2 %collective-permute-start.4 = (bf16[8,128,256]{2,1,0:T(8,128)(2,1)}, bf16[8,128,256]{2,1,0:T(8,128)(2,1)}, u32[]{:S(2)}, u32[]{:S(2)}) collective-permute-start(bf16[8,128,256]{2,1,0:T(8,128)(2,1)} %collective-permute-done.3.refs_1_), channel_id=1, source_target_pairs={{0,112},{1,113},{2,114},{3,115},{4,116},{5,117},{6,118},{7,119},{8... | collective-permute-start | bytes 1572872 | tf_op jit(solution)/shard_map/ppermute | solution.py:370
  73.1 22.2 %all-to-all-start.3 = ((bf16[32,8,8,256]{3,2,1,0:T(8,128)(2,1)}), bf16[32,8,8,256]{3,2,1,0:T(8,128)(2,1)}, u32[]{:S(2)}, u32[]{:S(2)}) async-start(bf16[32,8,8,256]{3,2,1,0:T(8,128)(2,1)} %applied.1), calls=%async_computation.3 | async-start | bytes 2097152 | tf_op jit(solution)/shard_map/all_to_all | solution.py:345
  84.0 13.0 %collective-permute-start.2 = (bf16[8,128,256]{2,1,0:T(8,128)(2,1)S(1)}, bf16[8,128,256]{2,1,0:T(8,128)(2,1)S(1)}, u32[]{:S(2)}, u32[]{:S(2)}) collective-permute-start(bf16[8,128,256]{2,1,0:T(8,128)(2,1)S(1)} %collective-permute-done.1.refs_2_), channel_id=1, source_target_pairs={{0,16},{1,17},{2,18},{3,19},{4,20},{5,21},{6,22},{7,23},{8,24},{9,... | collective-permute-start | bytes 1572872 | tf_op jit(solution)/shard_map/ppermute | solution.py:375
  84.0 13.0 %collective-permute-start.5 = (bf16[8,128,256]{2,1,0:T(8,128)(2,1)}, bf16[8,128,256]{2,1,0:T(8,128)(2,1)S(1)}, u32[]{:S(2)}, u32[]{:S(2)}) collective-permute-start(bf16[8,128,256]{2,1,0:T(8,128)(2,1)} %collective-permute-done.4.refs_3_), channel_id=1, source_target_pairs={{0,112},{1,113},{2,114},{3,115},{4,116},{5,117},{6,118},{7,119},{8... | collective-permute-start | bytes 1572872 | tf_op jit(solution)/shard_map/ppermute | solution.py:376
  87.5 17.2 %collective-permute-start.7 = (f32[16,4,8,256]{3,2,1,0:T(8,128)}, f32[16,4,8,256]{3,2,1,0:T(8,128)S(1)}, u32[]{:S(2)}, u32[]{:S(2)}) collective-permute-start(f32[16,4,8,256]{3,2,1,0:T(8,128)} %get-tuple-element.43), channel_id=1, source_target_pairs={{0,128},{1,129},{2,130},{3,131},{4,132},{5,133},{6,134},{7,135},{8... | collective-permute-start | bytes 1572872 | tf_op jit(solution)/shard_map/ppermute | solution.py:384
  97.0 8.8 %collective-permute-start.6 = (bf16[8,128,256]{2,1,0:T(8,128)(2,1)S(1)}, bf16[8,128,256]{2,1,0:T(8,128)(2,1)S(1)}, u32[]{:S(2)}, u32[]{:S(2)}) collective-permute-start(bf16[8,128,256]{2,1,0:T(8,128)(2,1)S(1)} %broadcast_select_fusion), channel_id=1, source_target_pairs={{0,16},{1,113},{2,18},{3,115},{4,20},{5,117},{6,22},{7,119},{8,24}... | collective-permute-start | bytes 1572872 | tf_op jit(solution)/shard_map/ppermute | solution.py:381
  106.5 5.9 %collective-permute-start.8 = (f32[17,64,128]{2,1,0:T(8,128)S(1)}, f32[17,64,128]{2,1,0:T(8,128)S(1)}, u32[]{:S(2)}, u32[]{:S(2)}) collective-permute-start(f32[17,64,128]{2,1,0:T(8,128)S(1)} %get-tuple-element.52), channel_id=1, source_target_pairs={{0,1},{1,0},{2,3},{3,2},{4,5},{5,4},{6,7},{7,6},{8,9},{9,8},{10,11... | collective-permute-start | bytes 1671176 | tf_op jit(solution)/shard_map/ppermute | solution.py:388

commit v6 on v5

--- a/solution.py
+++ b/solution.py
@@ -264,14 +264,15 @@
     )(weights, last, keep, send)
 
 
-def join_kernel(high_ref, rest_ref, near_ref, far_ref):
+def join_kernel(own_ref, rest_ref, near_ref, far_ref):
     side = lax.div(lax.axis_index("band"), RING)
     for ref, which in ((near_ref, side), (far_ref, 1 - side)):
-        sources = pl.ds(which * SLABS, SLABS)
-        ref[...] = high_ref[sources].astype(F32) + rest_ref[sources].astype(F32)
-
-
-def run_join(high, rest):
+        rows = pl.ds(pl.multiple_of(which * 64, 64), 64)
+        high = jnp.swapaxes(own_ref[:, rows, :].astype(F32), 0, 1).reshape(SLABS, OWN, DEPTH, HALF)
+        ref[...] = high + rest_ref[pl.ds(which * SLABS, SLABS)].astype(F32)
+
+
+def run_join(own_low, rest):
     vmem = pl.BlockSpec(memory_space=pltpu.VMEM)
     shape = jax.ShapeDtypeStruct((SLABS, OWN, DEPTH, HALF), F32)
     return pl.pallas_call(
@@ -282,7 +283,7 @@
         compiler_params=pltpu.CompilerParams(vmem_limit_bytes=KERNEL_BYTES),
         cost_estimate=pl.CostEstimate(flops=1_000_000, bytes_accessed=2_000_000, transcendentals=0),
         name="join",
-    )(high, rest)
+    )(own_low, rest)
 
 
 def place_kernel(near_ref, far_ref, out_ref, done):
@@ -358,8 +359,7 @@
     shared = jnp.broadcast_to(potential[None, None], (SLABS, 1, DEPTH, PLANE))
     block = lax.all_to_all(jnp.concatenate([block, shared], axis=1), "slab", 0, 0, tiled=True)
     filtered_low, filtered_rest, applied = run_filter(block)
-    filtered_low = over_plane(filtered_low)
-    own_low = by_depth(filtered_low)
+    own_low = by_depth(over_plane(filtered_low))
     ahead = lax.ppermute(own_low, BOTH, ring_pairs(1, 1))
     behind = lax.ppermute(own_low, BOTH, ring_pairs(-1, -1))
     blocks = [ahead, behind]
@@ -380,7 +380,7 @@
     last = jnp.where(lax.axis_index("slab") % 2 == 0, ahead, behind)
     last = lax.ppermute(last, BOTH, ring_pairs(1, -1))
     weights, keep, send = run_early(own_low, by_depth(applied[:, :OWN]), by_depth(applied[:, OWN:]), blocks)
-    near, far = run_join(filtered_low, filtered_rest)
+    near, far = run_join(own_low, filtered_rest)
     far = lax.ppermute(far, BOTH, side_pairs())
     filtered = run_place(near, after(far, keep))
     last, filtered = lax.optimization_barrier((last, filtered))

time: 127 us -> 126 us (level)
  no operation moved by 1% of the time
where the time goes in v6:
time: 126 us; the launch traced here: 125 us
  blocking collectives  56.7 us (45%)
  starting transfers between devices  26.9 us (21%)
  waiting for transfers between devices  21.4 us (17%)
  Pallas kernels  13.1 us (10%)
  local copies, waits for them, and re-layouts  5.13 us (4%)
  other arithmetic  1.53 us (1%)
    all_to_all x1, blocking collectives, on_device(): lax.all_to_all(jnp.concatenate([block, shared], axis=1), 'slab', 0, 0, ti...  28.3 us
    all_to_all x1, blocking collectives, over_plane(): lax.all_to_all(block, BOTH, 0, 0, axis_index_groups=plane_groups(), tiled...  15.2 us
    all_to_all x1, blocking collectives, on_device(): lax.all_to_all(sums, BOTH, 0, 0, axis_index_groups=core_groups(), tiled=T...  13.2 us
    all_to_all x2, starting transfers between devices, over_plane(): lax.all_to_all(block, BOTH, 0, 0, axis_index_groups=plane_groups(), tiled...  8.8 us
    all_to_all x2, waiting for transfers between devices, over_plane(): lax.all_to_all(block, BOTH, 0, 0, axis_index_groups=plane_groups(), tiled...  8.72 us
    ppermute x2, waiting for transfers between devices, on_device(): ahead = lax.ppermute(ahead, BOTH, ring_pairs(1, 1))  7.47 us
    ppermute x2, starting transfers between devices, on_device(): behind = lax.ppermute(behind, BOTH, ring_pairs(-1, -1))  5.35 us
    pallas_call x1, Pallas kernels, run_filter(): pl.pallas_call(filter_kernel, out_shape=(jax.ShapeDtypeStruct((SLABS, OWN...  4.68 us
  transfers between devices with their start and end apart: 11, of which 7 were waited for; matrix products, arithmetic and copies ran while one was open for 1% of the time, Pallas kernels for 6%

profile of v6, /device:TPU:1, one launch (start us, length us, event | category | flops | bytes accessed | tf_op | source)
XLA Modules:
  0.0 125.5 jit_solution(14520422238834454435)
XLA Ops:
  0.6 0.7 broadcast_in_dim.2
  1.4 1.4 %pad_maximum_fusion = f32[16,5,8,512]{3,2,1,0:T(8,128)S(1)} fusion(f32[16,1,8,512]{3,2,1,0:T(8,128)S(1)} %broadcast_in_dim.2, f32[16,4,8,512]{3,2,1,0:T(8,128)} %bitcast.19), kind=kLoop, calls=%fused_computation | loop fusion | flops 327680 | bytes 2621440 | tf_op jit(solution)/shard_map/concatenate | solution.py:360
  2.7 0.0 copy-start
  2.7 0.0 copy-start.2
  2.8 0.0 copy-start.5
  2.8 28.3 %all_to_all.25.x_ref = f32[16,5,8,512]{3,2,1,0:T(8,128)S(1)} all-to-all(f32[16,5,8,512]{3,2,1,0:T(8,128)S(1)} %pad_maximum_fusion), channel_id=1, replica_groups=mesh['band'=16,'slab'=16] {'slab'}, dimensions={0} | all-to-all | bytes 2621440 | tf_op jit(solution)/shard_map/all_to_all | solution.py:360
  31.1 0.0 copy-done.2
  31.1 4.7 %chebyshev.1 = (f32[16,4,8,512]{3,2,1,0:T(8,128)S(1)}, bf16[32,4,8,256]{3,2,1,0:T(8,128)(2,1)S(1)}, bf16[32,4,8,256]{3,2,1,0:T(8,128)(2,1)S(1)}) custom-call(f32[16,5,8,512]{3,2,1,0:T(8,128)S(1)} %all_to_all.25.x_ref, bf16[512,512]{1,0:T(8,128)(2,1)S(1)} %copy-done, bf16[512,512]{1,0:T(8,128)(2,1)S(1)} %copy-done.2, bf16[128,384]{1,0:T(8,128)(2,1)S(1)} %copy-done.5), custom_call_target="tpu_custom_call" | custom-call | flops 5000000000 | bytes 6000000 | tf_op jit(solution)/shard_map/chebyshev/pallas_call | solution.py:158
  35.8 0.0 copy-start.4
  35.8 15.2 %all_to_all.26 = bf16[32,4,8,256]{3,2,1,0:T(8,128)(2,1)S(1)} all-to-all(bf16[32,4,8,256]{3,2,1,0:T(8,128)(2,1)S(1)} %get-tuple-element.28), channel_id=1, replica_groups={{0,1,2,3,4,5,6,7,8,9,10,11,12,13,14,15,128,129,130,131,132,133,134,135,..., dimensions={0} | all-to-all | bytes 1048576 | tf_op jit(solution)/shard_map/all_to_all | solution.py:346
  51.0 0.1 copy.19
  51.1 1.7 %collective-permute-start = (bf16[8,128,256]{2,1,0:T(8,128)(2,1)S(1)}, bf16[8,128,256]{2,1,0:T(8,128)(2,1)}, u32[]{:S(2)}, u32[]{:S(2)}) collective-permute-start(bf16[8,128,256]{2,1,0:T(8,128)(2,1)S(1)} %bitcast.12), channel_id=1, source_target_pairs={{0,16},{1,17},{2,18},{3,19},{4,20},{5,21},{6,22},{7,23},{8,24},{9,... | collective-permute-start | bytes 1572872 | tf_op jit(solution)/shard_map/ppermute | solution.py:363
  52.8 4.0 %collective-permute-start.3 = (bf16[8,128,256]{2,1,0:T(8,128)(2,1)S(1)}, bf16[8,128,256]{2,1,0:T(8,128)(2,1)}, u32[]{:S(2)}, u32[]{:S(2)}) collective-permute-start(bf16[8,128,256]{2,1,0:T(8,128)(2,1)S(1)} %bitcast.13), channel_id=1, source_target_pairs={{0,112},{1,113},{2,114},{3,115},{4,116},{5,117},{6,118},{7,119},{8... | collective-permute-start | bytes 1572872 | tf_op jit(solution)/shard_map/ppermute | solution.py:364
  56.8 0.0 copy-done.4
  56.8 4.1 %all-to-all-start.2 = ((bf16[32,4,8,256]{3,2,1,0:T(8,128)(2,1)}), bf16[32,4,8,256]{3,2,1,0:T(8,128)(2,1)S(1)}, u32[]{:S(2)}, u32[]{:S(2)}) async-start(bf16[32,4,8,256]{3,2,1,0:T(8,128)(2,1)} %copy-done.4), calls=%async_computation.2 | async-start | bytes 1048576 | tf_op jit(solution)/shard_map/all_to_all | solution.py:346
  60.9 0.0 copy-start.1
  61.0 1.0 copy-done.1
  62.0 1.0 copy-done.3
  63.0 2.6 %applied.1 = bf16[32,8,8,256]{3,2,1,0:T(8,128)(2,1)} custom-call(f32[16,5,8,512]{3,2,1,0:T(8,128)S(1)} %all_to_all.25.x_ref, f32[16,4,8,512]{3,2,1,0:T(8,128)S(1)} %get-tuple-element.29.f_ref, bf16[512,512]{1,0:T(8,128)(2,1)S(1)} %copy-done.1, bf16[512,512]{1,0:T(8,128)(2,1)S(1)} %copy-done.3, bf16[128,384]{1,0:T(8,128)(2,1)S(1)} %copy-done.5), custom_call_target="tpu_custom_call" | custom-call | flops 1000000000 | bytes 6000000 | tf_op jit(solution)/shard_map/applied/pallas_call | solution.py:178
  65.6 3.3 %collective-permute-done.refs_0_ = bf16[8,128,256]{2,1,0:T(8,128)(2,1)} collective-permute-done((bf16[8,128,256]{2,1,0:T(8,128)(2,1)S(1)}, bf16[8,128,256]{2,1,0:T(8,128)(2,1)}, u32[]{:S(2)}, u32[]{:S(2)}) %collective-permute-start) | collective-permute-done | bytes 524320 | tf_op jit(solution)/shard_map/ppermute | solution.py:363
  68.9 0.0 collective-permute-start.1
  68.9 0.0 collective-permute-done.3.refs_1_
  68.9 2.7 %collective-permute-start.4 = (bf16[8,128,256]{2,1,0:T(8,128)(2,1)}, bf16[8,128,256]{2,1,0:T(8,128)(2,1)}, u32[]{:S(2)}, u32[]{:S(2)}) collective-permute-start(bf16[8,128,256]{2,1,0:T(8,128)(2,1)} %collective-permute-done.3.refs_1_), channel_id=1, source_target_pairs={{0,112},{1,113},{2,114},{3,115},{4,116},{5,117},{6,118},{7,119},{8... | collective-permute-start | bytes 1572872 | tf_op jit(solution)/shard_map/ppermute | solution.py:370
  71.6 0.9 all-to-all-done.2.rest_ref
  72.5 4.7 %all-to-all-start.3 = ((bf16[32,8,8,256]{3,2,1,0:T(8,128)(2,1)}), bf16[32,8,8,256]{3,2,1,0:T(8,128)(2,1)}, u32[]{:S(2)}, u32[]{:S(2)}) async-start(bf16[32,8,8,256]{3,2,1,0:T(8,128)(2,1)} %applied.1), calls=%async_computation.3 | async-start | bytes 2097152 | tf_op jit(solution)/shard_map/all_to_all | solution.py:346
  77.2 5.8 %collective-permute-done.1.refs_2_ = bf16[8,128,256]{2,1,0:T(8,128)(2,1)S(1)} collective-permute-done((bf16[8,128,256]{2,1,0:T(8,128)(2,1)}, bf16[8,128,256]{2,1,0:T(8,128)(2,1)S(1)}, u32[]{:S(2)}, u32[]{:S(2)}) %collective-permute-start.1) | collective-permute-done | bytes 524320 | tf_op jit(solution)/shard_map/ppermute | solution.py:369
  83.0 0.0 collective-permute-start.2
  83.0 0.0 collective-permute-done.4.refs_3_
  83.0 2.7 %collective-permute-start.5 = (bf16[8,128,256]{2,1,0:T(8,128)(2,1)}, bf16[8,128,256]{2,1,0:T(8,128)(2,1)S(1)}, u32[]{:S(2)}, u32[]{:S(2)}) collective-permute-start(bf16[8,128,256]{2,1,0:T(8,128)(2,1)} %collective-permute-done.4.refs_3_), channel_id=1, source_target_pairs={{0,112},{1,113},{2,114},{3,115},{4,116},{5,117},{6,118},{7,119},{8... | collective-permute-start | bytes 1572872 | tf_op jit(solution)/shard_map/ppermute | solution.py:376
  85.7 0.9 join.1
  86.6 0.0 collective-permute-start.7
  86.6 7.8 %all-to-all-done.3 = bf16[32,8,8,256]{3,2,1,0:T(8,128)(2,1)} async-done(((bf16[32,8,8,256]{3,2,1,0:T(8,128)(2,1)}), bf16[32,8,8,256]{3,2,1,0:T(8,128)(2,1)}, u32[]{:S(2)}, u32[]{:S(2)}) %all-to-all-start.3) | async-done | bytes 1048608 | tf_op jit(solution)/shard_map/all_to_all | solution.py:346
  94.4 1.6 %collective-permute-done.2.refs_4_ = bf16[8,128,256]{2,1,0:T(8,128)(2,1)S(1)} collective-permute-done((bf16[8,128,256]{2,1,0:T(8,128)(2,1)S(1)}, bf16[8,128,256]{2,1,0:T(8,128)(2,1)S(1)}, u32[]{:S(2)}, u32[]{:S(2)}) %collective-permute-start.2) | collective-permute-done | bytes 524320 | tf_op jit(solution)/shard_map/ppermute | solution.py:375
  96.1 0.0 collective-permute-done.5.refs_5_
  96.1 0.1 broadcast_select_fusion
  96.1 2.7 %collective-permute-start.6 = (bf16[8,128,256]{2,1,0:T(8,128)(2,1)S(1)}, bf16[8,128,256]{2,1,0:T(8,128)(2,1)S(1)}, u32[]{:S(2)}, u32[]{:S(2)}) collective-permute-start(bf16[8,128,256]{2,1,0:T(8,128)(2,1)S(1)} %broadcast_select_fusion), channel_id=1, source_target_pairs={{0,16},{1,113},{2,18},{3,115},{4,20},{5,117},{6,22},{7,119},{8,24}... | collective-permute-start | bytes 1572872 | tf_op jit(solution)/shard_map/ppermute | solution.py:381
  98.8 1.3 %fusion = (bf16[32,4,8,256]{3,2,1,0:T(8,128)(2,1)S(1)}, bf16[32,4,8,256]{3,2,1,0:T(8,128)(2,1)S(1)}) fusion(bf16[32,8,8,256]{3,2,1,0:T(8,128)(2,1)} %all-to-all-done.3), kind=kLoop, calls=%fused_computation.7 | loop fusion | bytes 2097152 | tf_op jit(solution)/shard_map/slice | solution.py:382
  100.1 0.2 copy_bitcast_fusion
  100.3 3.3 %pairs_early.1 = (bf16[8,384,256]{2,1,0:T(8,128)(2,1)S(1)}, f32[17,64,128]{2,1,0:T(8,128)S(1)}, f32[17,64,128]{2,1,0:T(8,128)S(1)}) custom-call(bf16[8,128,256]{2,1,0:T(8,128)(2,1)S(1)} %bitcast.15, bf16[8,128,256]{2,1,0:T(8,128)(2,1)S(1)} %get-tuple-element.58.high_ref, bf16[8,128,256]{2,1,0:T(8,128)(2,1)S(1)} %get-tuple-element.57.rest_ref, ...), custom_call_target="tpu_custom_call" | custom-call | flops 1400000000 | bytes 6000000 | tf_op jit(solution)/shard_map/pairs_early/pallas_call | solution.py:241
  103.6 0.0 collective-permute-done.7.far_ref
  103.6 1.0 place.1
  104.6 0.3 collective-permute-done.6.last_ref
  104.9 0.6 pairs_late.1
  105.6 4.3 %collective-permute-start.8 = (f32[17,64,128]{2,1,0:T(8,128)S(1)}, f32[17,64,128]{2,1,0:T(8,128)S(1)}, u32[]{:S(2)}, u32[]{:S(2)}) collective-permute-start(f32[17,64,128]{2,1,0:T(8,128)S(1)} %get-tuple-element.52), channel_id=1, source_target_pairs={{0,1},{1,0},{2,3},{3,2},{4,5},{5,4},{6,7},{7,6},{8,9},{9,8},{10,11... | collective-permute-start | bytes 1671176 | tf_op jit(solution)/shard_map/ppermute | solution.py:388
  109.8 1.6 %collective-permute-done.8 = f32[17,64,128]{2,1,0:T(8,128)S(1)} collective-permute-done((f32[17,64,128]{2,1,0:T(8,128)S(1)}, f32[17,64,128]{2,1,0:T(8,128)S(1)}, u32[]{:S(2)}, u32[]{:S(2)}) %collective-permute-start.8) | collective-permute-done | bytes 557088 | tf_op jit(solution)/shard_map/ppermute | solution.py:388
  111.4 0.1 slice_add_fusion
  111.5 13.2 %all_to_all.27 = f32[16,64,128]{2,1,0:T(8,128)S(1)} all-to-all(f32[16,64,128]{2,1,0:T(8,128)S(1)} %slice_add_fusion), channel_id=1, replica_groups={{0,2,4,6,8,10,12,14,128,130,132,134,136,138,140,142},{1,3,5,7,9,11,13,1..., dimensions={0} | all-to-all | bytes 1048576 | tf_op jit(solution)/shard_map/all_to_all | solution.py:389
  124.8 0.7 fusion.1
  (5 shorter events, 0.0 us)
Async XLA Ops:
  2.7 28.3 %copy-start = (bf16[512,512]{1,0:T(8,128)(2,1)S(1)}, bf16[512,512]{1,0:T(8,128)(2,1)}, u32[]{:S(2)}) copy-start(bf16[512,512]{1,0:T(8,128)(2,1)} %constant.29.clone.mh_ref) | copy-start | bytes 1572868
  2.7 28.3 %copy-start.2 = (bf16[512,512]{1,0:T(8,128)(2,1)S(1)}, bf16[512,512]{1,0:T(8,128)(2,1)}, u32[]{:S(2)}) copy-start(bf16[512,512]{1,0:T(8,128)(2,1)} %constant.30.clone.ml_ref) | copy-start | bytes 1572868
  2.8 28.3 %copy-start.5 = (bf16[128,384]{1,0:T(8,128)(2,1)S(1)}, bf16[128,384]{1,0:T(8,128)(2,1)}, u32[]{:S(2)}) copy-start(bf16[128,384]{1,0:T(8,128)(2,1)} %constant.31.clone.z_ref) | copy-start | bytes 294916
  35.8 21.1 %copy-start.4 = (bf16[32,4,8,256]{3,2,1,0:T(8,128)(2,1)}, bf16[32,4,8,256]{3,2,1,0:T(8,128)(2,1)S(1)}, u32[]{:S(2)}) copy-start(bf16[32,4,8,256]{3,2,1,0:T(8,128)(2,1)S(1)} %get-tuple-element.31) | copy-start | bytes 1572868
  51.1 17.8 %collective-permute-start = (bf16[8,128,256]{2,1,0:T(8,128)(2,1)S(1)}, bf16[8,128,256]{2,1,0:T(8,128)(2,1)}, u32[]{:S(2)}, u32[]{:S(2)}) collective-permute-start(bf16[8,128,256]{2,1,0:T(8,128)(2,1)S(1)} %bitcast.12), channel_id=1, source_target_pairs={{0,16},{1,17},{2,18},{3,19},{4,20},{5,21},{6,22},{7,23},{8,24},{9,... | collective-permute-start | bytes 1572872 | tf_op jit(solution)/shard_map/ppermute | solution.py:363
  52.8 16.1 %collective-permute-start.3 = (bf16[8,128,256]{2,1,0:T(8,128)(2,1)S(1)}, bf16[8,128,256]{2,1,0:T(8,128)(2,1)}, u32[]{:S(2)}, u32[]{:S(2)}) collective-permute-start(bf16[8,128,256]{2,1,0:T(8,128)(2,1)S(1)} %bitcast.13), channel_id=1, source_target_pairs={{0,112},{1,113},{2,114},{3,115},{4,116},{5,117},{6,118},{7,119},{8... | collective-permute-start | bytes 1572872 | tf_op jit(solution)/shard_map/ppermute | solution.py:364
  56.8 15.7 %all-to-all-start.2 = ((bf16[32,4,8,256]{3,2,1,0:T(8,128)(2,1)}), bf16[32,4,8,256]{3,2,1,0:T(8,128)(2,1)S(1)}, u32[]{:S(2)}, u32[]{:S(2)}) async-start(bf16[32,4,8,256]{3,2,1,0:T(8,128)(2,1)} %copy-done.4), calls=%async_computation.2 | async-start | bytes 1048576 | tf_op jit(solution)/shard_map/all_to_all | solution.py:346
  60.9 1.0 copy-start.1
  62.0 1.0 copy-start.3
  68.9 14.2 %collective-permute-start.1 = (bf16[8,128,256]{2,1,0:T(8,128)(2,1)}, bf16[8,128,256]{2,1,0:T(8,128)(2,1)S(1)}, u32[]{:S(2)}, u32[]{:S(2)}) collective-permute-start(bf16[8,128,256]{2,1,0:T(8,128)(2,1)} %collective-permute-done.refs_0_), channel_id=1, source_target_pairs={{0,16},{1,17},{2,18},{3,19},{4,20},{5,21},{6,22},{7,23},{8,24},{9,... | collective-permute-start | bytes 1572872 | tf_op jit(solution)/shard_map/ppermute | solution.py:369
  68.9 14.2 %collective-permute-start.4 = (bf16[8,128,256]{2,1,0:T(8,128)(2,1)}, bf16[8,128,256]{2,1,0:T(8,128)(2,1)}, u32[]{:S(2)}, u32[]{:S(2)}) collective-permute-start(bf16[8,128,256]{2,1,0:T(8,128)(2,1)} %collective-permute-done.3.refs_1_), channel_id=1, source_target_pairs={{0,112},{1,113},{2,114},{3,115},{4,116},{5,117},{6,118},{7,119},{8... | collective-permute-start | bytes 1572872 | tf_op jit(solution)/shard_map/ppermute | solution.py:370
  72.5 21.9 %all-to-all-start.3 = ((bf16[32,8,8,256]{3,2,1,0:T(8,128)(2,1)}), bf16[32,8,8,256]{3,2,1,0:T(8,128)(2,1)}, u32[]{:S(2)}, u32[]{:S(2)}) async-start(bf16[32,8,8,256]{3,2,1,0:T(8,128)(2,1)} %applied.1), calls=%async_computation.3 | async-start | bytes 2097152 | tf_op jit(solution)/shard_map/all_to_all | solution.py:346
  83.0 13.0 %collective-permute-start.2 = (bf16[8,128,256]{2,1,0:T(8,128)(2,1)S(1)}, bf16[8,128,256]{2,1,0:T(8,128)(2,1)S(1)}, u32[]{:S(2)}, u32[]{:S(2)}) collective-permute-start(bf16[8,128,256]{2,1,0:T(8,128)(2,1)S(1)} %collective-permute-done.1.refs_2_), channel_id=1, source_target_pairs={{0,16},{1,17},{2,18},{3,19},{4,20},{5,21},{6,22},{7,23},{8,24},{9,... | collective-permute-start | bytes 1572872 | tf_op jit(solution)/shard_map/ppermute | solution.py:375
  83.0 13.0 %collective-permute-start.5 = (bf16[8,128,256]{2,1,0:T(8,128)(2,1)}, bf16[8,128,256]{2,1,0:T(8,128)(2,1)S(1)}, u32[]{:S(2)}, u32[]{:S(2)}) collective-permute-start(bf16[8,128,256]{2,1,0:T(8,128)(2,1)} %collective-permute-done.4.refs_3_), channel_id=1, source_target_pairs={{0,112},{1,113},{2,114},{3,115},{4,116},{5,117},{6,118},{7,119},{8... | collective-permute-start | bytes 1572872 | tf_op jit(solution)/shard_map/ppermute | solution.py:376
  86.6 17.0 %collective-permute-start.7 = (f32[16,4,8,256]{3,2,1,0:T(8,128)}, f32[16,4,8,256]{3,2,1,0:T(8,128)S(1)}, u32[]{:S(2)}, u32[]{:S(2)}) collective-permute-start(f32[16,4,8,256]{3,2,1,0:T(8,128)} %get-tuple-element.43), channel_id=1, source_target_pairs={{0,128},{1,129},{2,130},{3,131},{4,132},{5,133},{6,134},{7,135},{8... | collective-permute-start | bytes 1572872 | tf_op jit(solution)/shard_map/ppermute | solution.py:384
  96.1 8.8 %collective-permute-start.6 = (bf16[8,128,256]{2,1,0:T(8,128)(2,1)S(1)}, bf16[8,128,256]{2,1,0:T(8,128)(2,1)S(1)}, u32[]{:S(2)}, u32[]{:S(2)}) collective-permute-start(bf16[8,128,256]{2,1,0:T(8,128)(2,1)S(1)} %broadcast_select_fusion), channel_id=1, source_target_pairs={{0,16},{1,113},{2,18},{3,115},{4,20},{5,117},{6,22},{7,119},{8,24}... | collective-permute-start | bytes 1572872 | tf_op jit(solution)/shard_map/ppermute | solution.py:381
  105.6 5.9 %collective-permute-start.8 = (f32[17,64,128]{2,1,0:T(8,128)S(1)}, f32[17,64,128]{2,1,0:T(8,128)S(1)}, u32[]{:S(2)}, u32[]{:S(2)}) collective-permute-start(f32[17,64,128]{2,1,0:T(8,128)S(1)} %get-tuple-element.52), channel_id=1, source_target_pairs={{0,1},{1,0},{2,3},{3,2},{4,5},{5,4},{6,7},{7,6},{8,9},{9,8},{10,11... | collective-permute-start | bytes 1671176 | tf_op jit(solution)/shard_map/ppermute | solution.py:388

commit v7 on v6

--- a/solution.py
+++ b/solution.py
@@ -81,6 +81,27 @@
     for slab in range(SLABS):
         for side in range(2):
             ref[side * SLABS + slab, orb] = value[slab_rows(slab), side * HALF : (side + 1) * HALF].astype(BF16)
+
+
+def pack_kernel(orbitals_ref, potential_ref, out_ref, done):
+    copies = [pltpu.make_async_copy(orbitals_ref, out_ref.at[:, :OWN], done.at[SLABS])]
+    copies += [pltpu.make_async_copy(potential_ref, out_ref.at[slab, OWN], done.at[slab]) for slab in range(SLABS)]
+    for copy in copies:
+        copy.start()
+    for copy in copies:
+        copy.wait()
+
+
+def run_pack(orbitals, potential):
+    return pl.pallas_call(
+        pack_kernel,
+        out_shape=jax.ShapeDtypeStruct((SLABS, OWN + 1, DEPTH, PLANE), F32),
+        in_specs=[pl.BlockSpec(memory_space=pltpu.HBM)] * 2,
+        out_specs=pl.BlockSpec(memory_space=pltpu.VMEM),
+        scratch_shapes=[pltpu.SemaphoreType.DMA((SLABS + 1,))],
+        compiler_params=pltpu.CompilerParams(vmem_limit_bytes=KERNEL_BYTES),
+        name="pack",
+    )(orbitals, potential)
 
 
 def filter_kernel(x_ref, mh_ref, ml_ref, z_ref, out_ref, low_ref, rest_ref, field_a, field_b, pot, split, total):
@@ -355,9 +376,8 @@
 
 
 def on_device(orbitals, potential):
-    block = orbitals.reshape(SLABS, OWN, DEPTH, PLANE)
-    shared = jnp.broadcast_to(potential[None, None], (SLABS, 1, DEPTH, PLANE))
-    block = lax.all_to_all(jnp.concatenate([block, shared], axis=1), "slab", 0, 0, tiled=True)
+    block = run_pack(orbitals.reshape(SLABS, OWN, DEPTH, PLANE), potential)
+    block = lax.all_to_all(block, "slab", 0, 0, tiled=True)
     filtered_low, filtered_rest, applied = run_filter(block)
     own_low = by_depth(over_plane(filtered_low))
     ahead = lax.ppermute(own_low, BOTH, ring_pairs(1, 1))

time: 126 us -> 127 us (level)
  other arithmetic: 1.53 us -> 0.18 us
    unnamed x12 -> x16, local copies, waits for them, and re-layouts: 2.1 us -> 4.04 us
    concatenate x1 -> x0, other arithmetic: 1.35 us -> none  [on_device(): jnp.concatenate([block, shared], axis=1)]
where the time goes in v7:
time: 127 us; the launch traced here: 126 us
  blocking collectives  56.7 us (45%)
  starting transfers between devices  26.9 us (21%)
  waiting for transfers between devices  21.3 us (17%)
  Pallas kernels  13.7 us (11%)
  local copies, waits for them, and re-layouts  6.33 us (5%)
    all_to_all x1, blocking collectives, on_device(): block = lax.all_to_all(block, 'slab', 0, 0, tiled=True)  28.3 us
    all_to_all x1, blocking collectives, over_plane(): lax.all_to_all(block, BOTH, 0, 0, axis_index_groups=plane_groups(), tiled...  15.2 us
    all_to_all x1, blocking collectives, on_device(): lax.all_to_all(sums, BOTH, 0, 0, axis_index_groups=core_groups(), tiled=T...  13.2 us
    all_to_all x2, starting transfers between devices, over_plane(): lax.all_to_all(block, BOTH, 0, 0, axis_index_groups=plane_groups(), tiled...  8.8 us
    all_to_all x2, waiting for transfers between devices, over_plane(): lax.all_to_all(block, BOTH, 0, 0, axis_index_groups=plane_groups(), tiled...  8.72 us
    ppermute x2, waiting for transfers between devices, on_device(): ahead = lax.ppermute(ahead, BOTH, ring_pairs(1, 1))  7.47 us
    ppermute x2, starting transfers between devices, on_device(): behind = lax.ppermute(behind, BOTH, ring_pairs(-1, -1))  5.35 us
    pallas_call x1, Pallas kernels, run_filter(): pl.pallas_call(filter_kernel, out_shape=(jax.ShapeDtypeStruct((SLABS, OWN...  4.68 us
  transfers between devices with their start and end apart: 11, of which 7 were waited for; matrix products, arithmetic and copies ran while one was open for 1% of the time, Pallas kernels for 6%

profile of v7, /device:TPU:1, one launch (start us, length us, event | category | flops | bytes accessed | tf_op | source)
XLA Modules:
  0.0 125.9 jit_solution(4878184815843166291)
XLA Ops:
  0.6 1.2 copy-done
  1.9 0.7 copy-done.7
  2.6 0.6 pack.1
  3.2 0.0 copy-start.1
  3.2 0.0 copy-start.3
  3.2 0.0 copy-start.6
  3.2 28.3 %all_to_all.25.x_ref = f32[16,5,8,512]{3,2,1,0:T(8,128)S(1)} all-to-all(f32[16,5,8,512]{3,2,1,0:T(8,128)S(1)} %pack.1), channel_id=1, replica_groups=mesh['band'=16,'slab'=16] {'slab'}, dimensions={0} | all-to-all | bytes 2621440 | tf_op jit(solution)/shard_map/all_to_all | solution.py:380
  31.5 4.7 %chebyshev.1 = (f32[16,4,8,512]{3,2,1,0:T(8,128)S(1)}, bf16[32,4,8,256]{3,2,1,0:T(8,128)(2,1)S(1)}, bf16[32,4,8,256]{3,2,1,0:T(8,128)(2,1)S(1)}) custom-call(f32[16,5,8,512]{3,2,1,0:T(8,128)S(1)} %all_to_all.25.x_ref, bf16[512,512]{1,0:T(8,128)(2,1)S(1)} %copy-done.1, bf16[512,512]{1,0:T(8,128)(2,1)S(1)} %copy-done.3, bf16[128,384]{1,0:T(8,128)(2,1)S(1)} %copy-done.6), custom_call_target="tpu_custom_call" | custom-call | flops 5000000000 | bytes 6000000 | tf_op jit(solution)/shard_map/chebyshev/pallas_call | solution.py:179
  36.2 0.0 copy-start.5
  36.2 15.2 %all_to_all.26 = bf16[32,4,8,256]{3,2,1,0:T(8,128)(2,1)S(1)} all-to-all(bf16[32,4,8,256]{3,2,1,0:T(8,128)(2,1)S(1)} %get-tuple-element.28), channel_id=1, replica_groups={{0,1,2,3,4,5,6,7,8,9,10,11,12,13,14,15,128,129,130,131,132,133,134,135,..., dimensions={0} | all-to-all | bytes 1048576 | tf_op jit(solution)/shard_map/all_to_all | solution.py:367
  51.4 0.1 copy.19
  51.5 1.7 %collective-permute-start = (bf16[8,128,256]{2,1,0:T(8,128)(2,1)S(1)}, bf16[8,128,256]{2,1,0:T(8,128)(2,1)}, u32[]{:S(2)}, u32[]{:S(2)}) collective-permute-start(bf16[8,128,256]{2,1,0:T(8,128)(2,1)S(1)} %bitcast.12), channel_id=1, source_target_pairs={{0,16},{1,17},{2,18},{3,19},{4,20},{5,21},{6,22},{7,23},{8,24},{9,... | collective-permute-start | bytes 1572872 | tf_op jit(solution)/shard_map/ppermute | solution.py:383
  53.2 4.0 %collective-permute-start.3 = (bf16[8,128,256]{2,1,0:T(8,128)(2,1)S(1)}, bf16[8,128,256]{2,1,0:T(8,128)(2,1)}, u32[]{:S(2)}, u32[]{:S(2)}) collective-permute-start(bf16[8,128,256]{2,1,0:T(8,128)(2,1)S(1)} %bitcast.13), channel_id=1, source_target_pairs={{0,112},{1,113},{2,114},{3,115},{4,116},{5,117},{6,118},{7,119},{8... | collective-permute-start | bytes 1572872 | tf_op jit(solution)/shard_map/ppermute | solution.py:384
  57.2 0.0 copy-done.5
  57.2 4.1 %all-to-all-start.2 = ((bf16[32,4,8,256]{3,2,1,0:T(8,128)(2,1)}), bf16[32,4,8,256]{3,2,1,0:T(8,128)(2,1)S(1)}, u32[]{:S(2)}, u32[]{:S(2)}) async-start(bf16[32,4,8,256]{3,2,1,0:T(8,128)(2,1)} %copy-done.5), calls=%async_computation.2 | async-start | bytes 1048576 | tf_op jit(solution)/shard_map/all_to_all | solution.py:367
  61.4 0.0 copy-start.2
  61.4 1.0 copy-done.2
  62.4 1.0 copy-done.4
  63.5 2.6 %applied.1 = bf16[32,8,8,256]{3,2,1,0:T(8,128)(2,1)} custom-call(f32[16,5,8,512]{3,2,1,0:T(8,128)S(1)} %all_to_all.25.x_ref, f32[16,4,8,512]{3,2,1,0:T(8,128)S(1)} %get-tuple-element.29.f_ref, bf16[512,512]{1,0:T(8,128)(2,1)S(1)} %copy-done.2, bf16[512,512]{1,0:T(8,128)(2,1)S(1)} %copy-done.4, bf16[128,384]{1,0:T(8,128)(2,1)S(1)} %copy-done.6), custom_call_target="tpu_custom_call" | custom-call | flops 1000000000 | bytes 6000000 | tf_op jit(solution)/shard_map/applied/pallas_call | solution.py:199
  66.1 3.3 %collective-permute-done.refs_0_ = bf16[8,128,256]{2,1,0:T(8,128)(2,1)} collective-permute-done((bf16[8,128,256]{2,1,0:T(8,128)(2,1)S(1)}, bf16[8,128,256]{2,1,0:T(8,128)(2,1)}, u32[]{:S(2)}, u32[]{:S(2)}) %collective-permute-start) | collective-permute-done | bytes 524320 | tf_op jit(solution)/shard_map/ppermute | solution.py:383
  69.3 0.0 collective-permute-start.1
  69.3 0.0 collective-permute-done.3.refs_1_
  69.3 2.7 %collective-permute-start.4 = (bf16[8,128,256]{2,1,0:T(8,128)(2,1)}, bf16[8,128,256]{2,1,0:T(8,128)(2,1)}, u32[]{:S(2)}, u32[]{:S(2)}) collective-permute-start(bf16[8,128,256]{2,1,0:T(8,128)(2,1)} %collective-permute-done.3.refs_1_), channel_id=1, source_target_pairs={{0,112},{1,113},{2,114},{3,115},{4,116},{5,117},{6,118},{7,119},{8... | collective-permute-start | bytes 1572872 | tf_op jit(solution)/shard_map/ppermute | solution.py:390
  72.0 0.9 all-to-all-done.2.rest_ref
  73.0 4.7 %all-to-all-start.3 = ((bf16[32,8,8,256]{3,2,1,0:T(8,128)(2,1)}), bf16[32,8,8,256]{3,2,1,0:T(8,128)(2,1)}, u32[]{:S(2)}, u32[]{:S(2)}) async-start(bf16[32,8,8,256]{3,2,1,0:T(8,128)(2,1)} %applied.1), calls=%async_computation.3 | async-start | bytes 2097152 | tf_op jit(solution)/shard_map/all_to_all | solution.py:367
  77.6 5.8 %collective-permute-done.1.refs_2_ = bf16[8,128,256]{2,1,0:T(8,128)(2,1)S(1)} collective-permute-done((bf16[8,128,256]{2,1,0:T(8,128)(2,1)}, bf16[8,128,256]{2,1,0:T(8,128)(2,1)S(1)}, u32[]{:S(2)}, u32[]{:S(2)}) %collective-permute-start.1) | collective-permute-done | bytes 524320 | tf_op jit(solution)/shard_map/ppermute | solution.py:389
  83.5 0.0 collective-permute-start.2
  83.5 0.0 collective-permute-done.4.refs_3_
  83.5 2.7 %collective-permute-start.5 = (bf16[8,128,256]{2,1,0:T(8,128)(2,1)}, bf16[8,128,256]{2,1,0:T(8,128)(2,1)S(1)}, u32[]{:S(2)}, u32[]{:S(2)}) collective-permute-start(bf16[8,128,256]{2,1,0:T(8,128)(2,1)} %collective-permute-done.4.refs_3_), channel_id=1, source_target_pairs={{0,112},{1,113},{2,114},{3,115},{4,116},{5,117},{6,118},{7,119},{8... | collective-permute-start | bytes 1572872 | tf_op jit(solution)/shard_map/ppermute | solution.py:396
  86.2 0.9 join.1
  87.1 0.0 collective-permute-start.7
  87.1 7.8 %all-to-all-done.3 = bf16[32,8,8,256]{3,2,1,0:T(8,128)(2,1)} async-done(((bf16[32,8,8,256]{3,2,1,0:T(8,128)(2,1)}), bf16[32,8,8,256]{3,2,1,0:T(8,128)(2,1)}, u32[]{:S(2)}, u32[]{:S(2)}) %all-to-all-start.3) | async-done | bytes 1048608 | tf_op jit(solution)/shard_map/all_to_all | solution.py:367
  94.9 1.6 %collective-permute-done.2.refs_4_ = bf16[8,128,256]{2,1,0:T(8,128)(2,1)S(1)} collective-permute-done((bf16[8,128,256]{2,1,0:T(8,128)(2,1)S(1)}, bf16[8,128,256]{2,1,0:T(8,128)(2,1)S(1)}, u32[]{:S(2)}, u32[]{:S(2)}) %collective-permute-start.2) | collective-permute-done | bytes 524320 | tf_op jit(solution)/shard_map/ppermute | solution.py:395
  96.5 0.0 collective-permute-done.5.refs_5_
  96.5 0.1 broadcast_select_fusion
  96.6 2.7 %collective-permute-start.6 = (bf16[8,128,256]{2,1,0:T(8,128)(2,1)S(1)}, bf16[8,128,256]{2,1,0:T(8,128)(2,1)S(1)}, u32[]{:S(2)}, u32[]{:S(2)}) collective-permute-start(bf16[8,128,256]{2,1,0:T(8,128)(2,1)S(1)} %broadcast_select_fusion), channel_id=1, source_target_pairs={{0,16},{1,113},{2,18},{3,115},{4,20},{5,117},{6,22},{7,119},{8,24}... | collective-permute-start | bytes 1572872 | tf_op jit(solution)/shard_map/ppermute | solution.py:401
  99.2 1.3 %fusion = (bf16[32,4,8,256]{3,2,1,0:T(8,128)(2,1)S(1)}, bf16[32,4,8,256]{3,2,1,0:T(8,128)(2,1)S(1)}) fusion(bf16[32,8,8,256]{3,2,1,0:T(8,128)(2,1)} %all-to-all-done.3), kind=kLoop, calls=%fused_computation.6 | loop fusion | bytes 2097152 | tf_op jit(solution)/shard_map/slice | solution.py:402
  100.5 0.2 copy_bitcast_fusion
  100.8 3.3 %pairs_early.1 = (bf16[8,384,256]{2,1,0:T(8,128)(2,1)S(1)}, f32[17,64,128]{2,1,0:T(8,128)S(1)}, f32[17,64,128]{2,1,0:T(8,128)S(1)}) custom-call(bf16[8,128,256]{2,1,0:T(8,128)(2,1)S(1)} %bitcast.15, bf16[8,128,256]{2,1,0:T(8,128)(2,1)S(1)} %get-tuple-element.58.high_ref, bf16[8,128,256]{2,1,0:T(8,128)(2,1)S(1)} %get-tuple-element.57.rest_ref, ...), custom_call_target="tpu_custom_call" | custom-call | flops 1400000000 | bytes 6000000 | tf_op jit(solution)/shard_map/pairs_early/pallas_call | solution.py:262
  104.1 0.0 collective-permute-done.7.far_ref
  104.1 1.0 place.1
  105.1 0.3 collective-permute-done.6.last_ref
  105.4 0.6 pairs_late.1
  106.0 4.3 %collective-permute-start.8 = (f32[17,64,128]{2,1,0:T(8,128)S(1)}, f32[17,64,128]{2,1,0:T(8,128)S(1)}, u32[]{:S(2)}, u32[]{:S(2)}) collective-permute-start(f32[17,64,128]{2,1,0:T(8,128)S(1)} %get-tuple-element.52), channel_id=1, source_target_pairs={{0,1},{1,0},{2,3},{3,2},{4,5},{5,4},{6,7},{7,6},{8,9},{9,8},{10,11... | collective-permute-start | bytes 1671176 | tf_op jit(solution)/shard_map/ppermute | solution.py:408
  110.3 1.6 %collective-permute-done.8 = f32[17,64,128]{2,1,0:T(8,128)S(1)} collective-permute-done((f32[17,64,128]{2,1,0:T(8,128)S(1)}, f32[17,64,128]{2,1,0:T(8,128)S(1)}, u32[]{:S(2)}, u32[]{:S(2)}) %collective-permute-start.8) | collective-permute-done | bytes 557088 | tf_op jit(solution)/shard_map/ppermute | solution.py:408
  111.9 0.1 slice_add_fusion
  112.0 13.2 %all_to_all.27 = f32[16,64,128]{2,1,0:T(8,128)S(1)} all-to-all(f32[16,64,128]{2,1,0:T(8,128)S(1)} %slice_add_fusion), channel_id=1, replica_groups={{0,2,4,6,8,10,12,14,128,130,132,134,136,138,140,142},{1,3,5,7,9,11,13,1..., dimensions={0} | all-to-all | bytes 1048576 | tf_op jit(solution)/shard_map/all_to_all | solution.py:409
  125.2 0.7 fusion.1
  (8 shorter events, 0.1 us)
Async XLA Ops:
  0.6 1.2 copy-start
  1.9 0.7 copy-start.7
  3.2 28.3 %copy-start.1 = (bf16[512,512]{1,0:T(8,128)(2,1)S(1)}, bf16[512,512]{1,0:T(8,128)(2,1)}, u32[]{:S(2)}) copy-start(bf16[512,512]{1,0:T(8,128)(2,1)} %constant.29.clone.mh_ref) | copy-start | bytes 1572868
  3.2 28.3 %copy-start.3 = (bf16[512,512]{1,0:T(8,128)(2,1)S(1)}, bf16[512,512]{1,0:T(8,128)(2,1)}, u32[]{:S(2)}) copy-start(bf16[512,512]{1,0:T(8,128)(2,1)} %constant.30.clone.ml_ref) | copy-start | bytes 1572868
  3.2 28.3 %copy-start.6 = (bf16[128,384]{1,0:T(8,128)(2,1)S(1)}, bf16[128,384]{1,0:T(8,128)(2,1)}, u32[]{:S(2)}) copy-start(bf16[128,384]{1,0:T(8,128)(2,1)} %constant.31.clone.z_ref) | copy-start | bytes 294916
  36.2 21.1 %copy-start.5 = (bf16[32,4,8,256]{3,2,1,0:T(8,128)(2,1)}, bf16[32,4,8,256]{3,2,1,0:T(8,128)(2,1)S(1)}, u32[]{:S(2)}) copy-start(bf16[32,4,8,256]{3,2,1,0:T(8,128)(2,1)S(1)} %get-tuple-element.31) | copy-start | bytes 1572868
  51.5 17.8 %collective-permute-start = (bf16[8,128,256]{2,1,0:T(8,128)(2,1)S(1)}, bf16[8,128,256]{2,1,0:T(8,128)(2,1)}, u32[]{:S(2)}, u32[]{:S(2)}) collective-permute-start(bf16[8,128,256]{2,1,0:T(8,128)(2,1)S(1)} %bitcast.12), channel_id=1, source_target_pairs={{0,16},{1,17},{2,18},{3,19},{4,20},{5,21},{6,22},{7,23},{8,24},{9,... | collective-permute-start | bytes 1572872 | tf_op jit(solution)/shard_map/ppermute | solution.py:383
  53.2 16.1 %collective-permute-start.3 = (bf16[8,128,256]{2,1,0:T(8,128)(2,1)S(1)}, bf16[8,128,256]{2,1,0:T(8,128)(2,1)}, u32[]{:S(2)}, u32[]{:S(2)}) collective-permute-start(bf16[8,128,256]{2,1,0:T(8,128)(2,1)S(1)} %bitcast.13), channel_id=1, source_target_pairs={{0,112},{1,113},{2,114},{3,115},{4,116},{5,117},{6,118},{7,119},{8... | collective-permute-start | bytes 1572872 | tf_op jit(solution)/shard_map/ppermute | solution.py:384
  57.2 15.7 %all-to-all-start.2 = ((bf16[32,4,8,256]{3,2,1,0:T(8,128)(2,1)}), bf16[32,4,8,256]{3,2,1,0:T(8,128)(2,1)S(1)}, u32[]{:S(2)}, u32[]{:S(2)}) async-start(bf16[32,4,8,256]{3,2,1,0:T(8,128)(2,1)} %copy-done.5), calls=%async_computation.2 | async-start | bytes 1048576 | tf_op jit(solution)/shard_map/all_to_all | solution.py:367
  61.4 1.0 copy-start.2
  62.4 1.0 copy-start.4
  69.3 14.2 %collective-permute-start.1 = (bf16[8,128,256]{2,1,0:T(8,128)(2,1)}, bf16[8,128,256]{2,1,0:T(8,128)(2,1)S(1)}, u32[]{:S(2)}, u32[]{:S(2)}) collective-permute-start(bf16[8,128,256]{2,1,0:T(8,128)(2,1)} %collective-permute-done.refs_0_), channel_id=1, source_target_pairs={{0,16},{1,17},{2,18},{3,19},{4,20},{5,21},{6,22},{7,23},{8,24},{9,... | collective-permute-start | bytes 1572872 | tf_op jit(solution)/shard_map/ppermute | solution.py:389
  69.3 14.2 %collective-permute-start.4 = (bf16[8,128,256]{2,1,0:T(8,128)(2,1)}, bf16[8,128,256]{2,1,0:T(8,128)(2,1)}, u32[]{:S(2)}, u32[]{:S(2)}) collective-permute-start(bf16[8,128,256]{2,1,0:T(8,128)(2,1)} %collective-permute-done.3.refs_1_), channel_id=1, source_target_pairs={{0,112},{1,113},{2,114},{3,115},{4,116},{5,117},{6,118},{7,119},{8... | collective-permute-start | bytes 1572872 | tf_op jit(solution)/shard_map/ppermute | solution.py:390
  73.0 21.9 %all-to-all-start.3 = ((bf16[32,8,8,256]{3,2,1,0:T(8,128)(2,1)}), bf16[32,8,8,256]{3,2,1,0:T(8,128)(2,1)}, u32[]{:S(2)}, u32[]{:S(2)}) async-start(bf16[32,8,8,256]{3,2,1,0:T(8,128)(2,1)} %applied.1), calls=%async_computation.3 | async-start | bytes 2097152 | tf_op jit(solution)/shard_map/all_to_all | solution.py:367
  83.5 13.0 %collective-permute-start.2 = (bf16[8,128,256]{2,1,0:T(8,128)(2,1)S(1)}, bf16[8,128,256]{2,1,0:T(8,128)(2,1)S(1)}, u32[]{:S(2)}, u32[]{:S(2)}) collective-permute-start(bf16[8,128,256]{2,1,0:T(8,128)(2,1)S(1)} %collective-permute-done.1.refs_2_), channel_id=1, source_target_pairs={{0,16},{1,17},{2,18},{3,19},{4,20},{5,21},{6,22},{7,23},{8,24},{9,... | collective-permute-start | bytes 1572872 | tf_op jit(solution)/shard_map/ppermute | solution.py:395
  83.5 13.0 %collective-permute-start.5 = (bf16[8,128,256]{2,1,0:T(8,128)(2,1)}, bf16[8,128,256]{2,1,0:T(8,128)(2,1)S(1)}, u32[]{:S(2)}, u32[]{:S(2)}) collective-permute-start(bf16[8,128,256]{2,1,0:T(8,128)(2,1)} %collective-permute-done.4.refs_3_), channel_id=1, source_target_pairs={{0,112},{1,113},{2,114},{3,115},{4,116},{5,117},{6,118},{7,119},{8... | collective-permute-start | bytes 1572872 | tf_op jit(solution)/shard_map/ppermute | solution.py:396
  87.1 17.0 %collective-permute-start.7 = (f32[16,4,8,256]{3,2,1,0:T(8,128)}, f32[16,4,8,256]{3,2,1,0:T(8,128)S(1)}, u32[]{:S(2)}, u32[]{:S(2)}) collective-permute-start(f32[16,4,8,256]{3,2,1,0:T(8,128)} %get-tuple-element.43), channel_id=1, source_target_pairs={{0,128},{1,129},{2,130},{3,131},{4,132},{5,133},{6,134},{7,135},{8... | collective-permute-start | bytes 1572872 | tf_op jit(solution)/shard_map/ppermute | solution.py:404
  96.6 8.8 %collective-permute-start.6 = (bf16[8,128,256]{2,1,0:T(8,128)(2,1)S(1)}, bf16[8,128,256]{2,1,0:T(8,128)(2,1)S(1)}, u32[]{:S(2)}, u32[]{:S(2)}) collective-permute-start(bf16[8,128,256]{2,1,0:T(8,128)(2,1)S(1)} %broadcast_select_fusion), channel_id=1, source_target_pairs={{0,16},{1,113},{2,18},{3,115},{4,20},{5,117},{6,22},{7,119},{8,24}... | collective-permute-start | bytes 1572872 | tf_op jit(solution)/shard_map/ppermute | solution.py:401
  106.0 5.9 %collective-permute-start.8 = (f32[17,64,128]{2,1,0:T(8,128)S(1)}, f32[17,64,128]{2,1,0:T(8,128)S(1)}, u32[]{:S(2)}, u32[]{:S(2)}) collective-permute-start(f32[17,64,128]{2,1,0:T(8,128)S(1)} %get-tuple-element.52), channel_id=1, source_target_pairs={{0,1},{1,0},{2,3},{3,2},{4,5},{5,4},{6,7},{7,6},{8,9},{9,8},{10,11... | collective-permute-start | bytes 1671176 | tf_op jit(solution)/shard_map/ppermute | solution.py:408
